TPU v7x, 32 devices: a whole 2x2x4 slice. The times are simulated.
32 devices in a mesh: groups: 2 (over x), pool: 16 (over z, y, core).
Axes of the slice: x: 2, y: 2, z: 4, core: 2. Of those that a mesh axis runs over, the one named last changes fastest.
Arguments:
- tokens: bfloat16 [64, 8192], P(('groups', 'pool')), parts along dimension 0, may hold values from -6 to 6
- base_projection_weight: bfloat16 [8192, 8192], P(None, 'pool'), may hold values from -0.0625 to 0.0625
- adapter_down_weight: bfloat16 [2048, 8192], P('pool'), may hold values from -0.0625 to 0.0625
- adapter_up_weight: bfloat16 [2048, 8192], P('pool'), may hold values from -0.5 to 0.5
- request_adapter: int32 [64, 1], P('groups'), parts along dimension 0, may hold values from 0 to 15; in each aligned block of 32 rows (0 to 31, 32 to 63, ...) at most 3 rows name the same one
- adapter_block_count: int32 [16], replicated, may hold values from 1 to 8, as said below
- adapter_store_slot: int32 [16], replicated, may hold values from 0 to 15, each once
Outputs:
- projected: bfloat16 [64, 8192], P(('groups', 'pool')), parts along dimension 0
There are 2 independent parts, one for each index of `groups`. A program takes and returns all parts, laid end to end along the dimension named above; an argument that names none is the same for every part. Nothing has to cross between parts.
Inputs may be any that keep to these rules, and one draw needn't show every extreme that they name: `adapter_block_count`: each adapter has 1 to 8 blocks; some adapter has exactly 8. `request_adapter`: among all requests of the part no adapter is named more than 3 times; some adapter is named exactly 3 times.
All inputs are finite; a program needn't handle non-finite values.
Results may differ from a plain program's by a relative error of at most 0.0046.
Values may be sent and summed in bfloat16 or wider, within the bound.
No kernel may reach another device: no remote copies, remote signals or barrier semaphores. Data moves between devices by JAX's collectives and lax.ppermute only.
A program may use at most 64 MiB of HBM per device.

v0:
```python
import jax
import jax.numpy as jnp
from jax import lax
from jax.sharding import PartitionSpec as P

RANK_BLOCK = 16
MAXIMUM_BLOCKS = 8
MOSTB = 3


def body(
    tokens,
    base_projection_weight,
    adapter_down_weight,
    adapter_up_weight,
    request_adapter,
    adapter_block_count,
    adapter_store_slot,
):
    device = lax.axis_index("pool")
    devices_pool = lax.axis_size("pool")
    rank_width = tokens.shape[1]
    nadapt = adapter_block_count.shape[0]
    per_dev = nadapt // devices_pool
    rank_extent = MAXIMUM_BLOCKS * RANK_BLOCK
    capacity = MOSTB
    gathered = lax.all_gather(tokens, "pool", axis=0, tiled=True)
    requests = gathered.shape[0]
    idents = request_adapter[:, 0]
    adapters = jnp.arange(nadapt, dtype=jnp.int32)
    pick_adapter = (idents[:, None] == adapters[None, :]).astype(jnp.int32)
    slot_of = jnp.sum(pick_adapter * adapter_store_slot[None, :], axis=1)
    owner_of = slot_of // per_dev
    local_of = slot_of % per_dev
    positions = jnp.arange(requests, dtype=jnp.int32)
    earlier = positions[:, None] > positions[None, :]
    same_ident = idents[:, None] == idents[None, :]
    occur = jnp.sum((same_ident & earlier).astype(jnp.int32), axis=1)
    slot_match = (adapter_store_slot[None, :] == adapters[:, None]).astype(jnp.int32)
    rank_by_slot = jnp.sum(slot_match * adapter_block_count[None, :], axis=1)
    local_ranks = lax.dynamic_slice_in_dim(rank_by_slot, device * per_dev, per_dev)
    local_starts = (jnp.cumsum(local_ranks) - local_ranks) * RANK_BLOCK
    padded_down_rows = jnp.concatenate(
        [adapter_down_weight, jnp.zeros((rank_extent, rank_width), adapter_down_weight.dtype)],
        axis=0,
    )
    padded_up_rows = jnp.concatenate(
        [adapter_up_weight, jnp.zeros((rank_extent, rank_width), adapter_up_weight.dtype)], axis=0
    )
    down_spans = jnp.stack(
        [lax.dynamic_slice_in_dim(padded_down_rows, local_starts[0], rank_extent, 0)]
    )
    up_spans = jnp.stack(
        [lax.dynamic_slice_in_dim(padded_up_rows, local_starts[0], rank_extent, 0)]
    )
    keep = jnp.arange(rank_extent, dtype=jnp.int32)[None, :] < (local_ranks * RANK_BLOCK)[:, None]
    owned = owner_of == device
    local_range = jnp.arange(per_dev, dtype=jnp.int32)
    occur_range = jnp.arange(capacity, dtype=jnp.int32)
    select = (
        owned[:, None, None]
        & (local_of[:, None, None] == local_range[None, :, None])
        & (occur[:, None, None] == occur_range[None, None, :])
    )
    select = select.astype(jnp.bfloat16)
    compact = jnp.einsum(
        "rkj,rd->kjd", select, gathered, preferred_element_type=jnp.float32
    ).astype(jnp.bfloat16)
    shrink = jnp.einsum("kjd,ksd->kjs", compact, down_spans, preferred_element_type=jnp.float32)
    shrink = jnp.where(keep[:, None, :], shrink, jnp.float32(0.0)).astype(jnp.bfloat16)
    delta = jnp.einsum("kjs,kse->kje", shrink, up_spans, preferred_element_type=jnp.float32).astype(
        jnp.bfloat16
    )
    base_cols = jnp.dot(gathered, base_projection_weight, preferred_element_type=jnp.float32)
    base_rows = lax.all_to_all(base_cols, "pool", split_axis=0, concat_axis=1, tiled=True)
    table = delta.reshape(-1, rank_width)
    local_index = local_of * capacity + occur
    picked = jnp.take(table, local_index, axis=0).astype(jnp.float32)
    own_delta = lax.psum_scatter(
        jnp.where(owned[:, None], picked, jnp.float32(0.0)), "pool", scatter_dimension=0, tiled=True
    )
    return (base_rows + own_delta).astype(jnp.bfloat16)


def solution(mesh):
    return jax.shard_map(
        body,
        mesh=mesh,
        in_specs=(
            P(("groups", "pool"), None),
            P(None, "pool"),
            P("pool", None),
            P("pool", None),
            P("groups", None),
            P(),
            P(),
        ),
        out_specs=P(("groups", "pool"), None),
        check_vma=False,
    )
```

profile of v0, /device:TPU:0, one launch (start us, length us, event | category | flops | bytes accessed | tf_op | source)
XLA Modules:
  0.0 140.3 jit_solution(2448379967909728435)
XLA Ops:
  6.5 0.0 copy-start
  6.5 0.0 all-reduce.3.cloned.1.call-start
  6.5 24.9 %all-gather = bf16[16,2,8192]{2,1,0:T(2,128)(2,1)S(1)} all-gather(bf16[1,2,8192]{2,1,0:T(2,128)(2,1)} %bitcast.18), channel_id=1, replica_groups=mesh['groups'=2,'pool'=16] {'pool'}, dimensions={0}, use_global_device_ids=true | all-gather | bytes 557056 | tf_op jit(solution)/shard_map/all_gather | solution.py:27
  31.4 0.2 reshape.106
  31.6 0.9 convert_reduce_fusion
  32.6 0.8 select_reduce_fusion.1
  33.3 0.8 select_reduce_fusion
  34.1 0.6 dynamic_slice.2
  35.4 2.5 %fusion.2 = bf16[3,128]{1,0:T(4,128)(2,1)S(1)} fusion(bf16[128,8192]{1,0:T(8,128)(2,1)} %param.9, bf16[32,8192]{1,0:T(8,128)(2,1)S(1)} %reshape.106, s32[32]{0:T(128)S(1)} %convert_reduce_fusion, pred[32]{0:T(512)(128)(4,1)S(1)} %get-tuple-element.6, pred[128]{0:T(512)(128)(4,1)S(1)} %iota_compare_fusion.4), kind=kOutput, calls=%fused_computation.5 | convolution fusion | flops 7889856 | bytes 2622496 | tf_op jit(solution)/shard_map/kjd,ksd->kjs/dot_general | solution.py:69
  37.9 0.0 copy-done
  37.9 0.4 convolution_convert_fusion
  38.3 0.9 gather_fusion
  39.2 1.2 convert_select_fusion
  40.4 0.0 all-reduce.3.cloned.1.call-update
  40.4 0.0 copy-start.1
  40.4 5.0 %fusion.13 = f32[32,512]{1,0:T(8,128)S(1)} fusion(bf16[32,8192]{1,0:T(8,128)(2,1)S(1)} %reshape.106, bf16[8192,512]{1,0:T(8,128)(2,1)} %param.8), kind=kOutput, calls=%fused_computation.27 | convolution fusion | flops 268435456 | bytes 8978432 | tf_op jit(solution)/shard_map/dot_general | solution.py:74
  45.4 0.7 all_to_all.14
  46.1 3.5 %all-to-all-start = ((f32[16,2,512]{2,1,0:T(2,128)}), f32[16,2,512]{2,1,0:T(2,128)S(1)}, u32[]{:S(2)}, u32[]{:S(2)}) async-start(f32[16,2,512]{2,1,0:T(2,128)} %all_to_all.14), calls=%async_computation | async-start | bytes 131072 | tf_op jit(solution)/shard_map/all_to_all | solution.py:75
  49.6 0.0 copy-done.1
  49.6 0.6 dynamic-slice
  50.9 6.1 %all-to-all-done = f32[16,2,512]{2,1,0:T(2,128)S(1)} async-done(((f32[16,2,512]{2,1,0:T(2,128)}), f32[16,2,512]{2,1,0:T(2,128)S(1)}, u32[]{:S(2)}, u32[]{:S(2)}) %all-to-all-start) | async-done | bytes 65568 | tf_op jit(solution)/shard_map/all_to_all | solution.py:75
  57.0 74.9 %all-reduce.3.cloned.1.call-done = f32[32,8192]{1,0:T(8,128)} async-done(((f32[32,8192]{1,0:T(8,128)}), f32[32,8192]{1,0:T(8,128)}) %all-reduce.3.cloned.1.call-update) | async-done | bytes 1048592
  131.9 1.6 %fusion.3 = bf16[2,8192]{1,0:T(2,128)(2,1)} fusion(f32[2,8192]{1,0:T(2,128)S(1)} %bitcast.17, f32[32,8192]{1,0:T(8,128)} %all-reduce.3.cloned.1.call-done, u32[]{:T(128)S(6)} %multiply.1), kind=kLoop, calls=%fused_computation.8 | loop fusion | flops 32768 | bytes 163844 | tf_op jit(solution)/shard_map/convert_element_type | solution.py:82
  (4 shorter events, 0.0 us)
Async XLA Ops:
  6.5 31.4 %copy-start = (bf16[128,8192]{1,0:T(8,128)(2,1)S(1)}, bf16[128,8192]{1,0:T(8,128)(2,1)}, u32[]{:S(2)}) copy-start(bf16[128,8192]{1,0:T(8,128)(2,1)} %param.10) | copy-start | bytes 6291460
  6.5 125.3 %all-reduce.3.cloned.1.call-start = ((), (), s32[]{:S(2)}) async-start(), calls=%async_computation.1 | async-start | bytes 2097152
  40.4 9.2 %copy-start.1 = (u32[32]{0:T(128)S(1)}, u32[32]{0:T(128)}, u32[]{:S(2)}) copy-start(u32[32]{0:T(128)} %constant.72) | copy-start | bytes 388
  46.1 10.9 %all-to-all-start = ((f32[16,2,512]{2,1,0:T(2,128)}), f32[16,2,512]{2,1,0:T(2,128)S(1)}, u32[]{:S(2)}, u32[]{:S(2)}) async-start(f32[16,2,512]{2,1,0:T(2,128)} %all_to_all.14), calls=%async_computation | async-start | bytes 131072 | tf_op jit(solution)/shard_map/all_to_all | solution.py:75
Sparse Core Ops, SparseCore 0:
  40.5 91.2 all-reduce.2
where the time goes:
time: 141 us; the launch traced here: 140 us
  waiting for transfers between devices  81 us (57%)
  blocking collectives  24.9 us (18%)
  between operations  14.8 us (10%)
  matrix products  7.91 us (6%)
  other arithmetic  5.29 us (4%)
  starting transfers between devices  3.5 us (2%)
  local copies, waits for them, and re-layouts  2.93 us (2%)
    unnamed x2, waiting for transfers between devices  74.9 us
    all_gather x1, blocking collectives, body(): gathered = lax.all_gather(tokens, 'pool', axis=0, tiled=True)  24.9 us
    all_to_all x1, waiting for transfers between devices, body(): lax.all_to_all(base_cols, 'pool', split_axis=0, concat_axis=1, tiled=True)  6.09 us
    dot_general x1, matrix products, body(): jnp.dot(gathered, base_projection_weight, preferred_element_type=jnp.floa...  5.01 us
    all_to_all x1, starting transfers between devices, body(): lax.all_to_all(base_cols, 'pool', split_axis=0, concat_axis=1, tiled=True)  3.5 us
  transfers between devices with their start and end apart: 2, of which 2 were waited for; matrix products, arithmetic and copies ran while one was open for 4% of the time, Pallas kernels for 0%

commit v1 on v0

v1 whole, which is shorter than its diff:
```python
import jax
import jax.numpy as jnp
from jax import lax
from jax.experimental import pallas as pl
from jax.experimental.pallas import tpu as pltpu
from jax.sharding import PartitionSpec as P

RANK_BLOCK = 16


def stages_of(devices):
    bits = [1 << k for k in range(1, devices.bit_length() - 1)]
    stages = [[b] for b in bits[:1]]
    rest = bits[1:]
    for k in range(0, len(rest), 2):
        low = rest[k]
        stages.append([low, rest[k + 1], low + rest[k + 1]] if k + 1 < len(rest) else [low])
    return stages


def exchange(array, mask, devices):
    return lax.ppermute(array, "pool", [(d, d ^ mask) for d in range(devices)])


def project_kernel(rows, where_ref, own_ref, keep_ref, near_ref, far_ref, base_ref, down_ref, up_ref, near_out, far_out):
    half = near_ref.shape[0]
    width = base_ref.shape[1]
    device = where_ref[0]
    x = jnp.concatenate([near_ref[...], far_ref[...]], axis=0)
    shrink = lax.dot_general(x, down_ref[...], (((1,), (1,)), ((), ())), preferred_element_type=jnp.float32)
    shrink = jnp.where(keep_ref[...] > 0, shrink, 0.0).astype(jnp.bfloat16)
    base = jnp.dot(x, base_ref[...], preferred_element_type=jnp.float32)
    to = lax.broadcasted_iota(jnp.int32, (half, half), 0)
    of = lax.broadcasted_iota(jnp.int32, (half, half), 1)
    order = to == (of ^ (rows * (device // 2)))
    narrow, wide = order.astype(jnp.bfloat16), order.astype(jnp.float32)
    lanes = max(width, 128)
    columns = pl.ds(pl.multiple_of(device * width // lanes * lanes, lanes), lanes)
    lane = lax.broadcasted_iota(jnp.int32, (half, lanes), 1)
    inside = lane // width == device % (lanes // width)
    for part, out in ((0, near_out), (1, far_out)):
        span = slice(part * half, (part + 1) * half)
        ranked = jnp.dot(narrow, shrink[span], preferred_element_type=jnp.float32)
        ranked = jnp.where(own_ref[span] > 0, ranked, 0.0).astype(jnp.bfloat16)
        placed = jnp.dot(wide, base[span], preferred_element_type=jnp.float32, precision=lax.Precision.HIGHEST)
        out[...] = jnp.dot(ranked, up_ref[...], preferred_element_type=jnp.float32).astype(jnp.bfloat16)
        placed = jnp.where(inside, jnp.concatenate([placed] * (lanes // width), axis=1), 0.0)
        out[:, columns] = (placed + out[:, columns].astype(jnp.float32)).astype(jnp.bfloat16)


def body(
    tokens,
    base_projection_weight,
    adapter_down_weight,
    adapter_up_weight,
    request_adapter,
    adapter_block_count,
    adapter_store_slot,
):
    device = lax.axis_index("pool")
    devices = lax.axis_size("pool")
    rows, model = tokens.shape
    half = devices // 2 * rows

    place = jnp.arange(2 * half, dtype=jnp.int32)
    core = (device % 2) ^ (place // half)
    request = ((place % half) // rows * 2 + core) * rows + place % rows
    mine = adapter_store_slot == device
    adapters = jnp.arange(mine.shape[0], dtype=jnp.int32)
    my_adapter = jnp.sum(jnp.where(mine, adapters, 0))
    my_rank = jnp.sum(jnp.where(mine, adapter_block_count, 0)) * RANK_BLOCK
    idents = request_adapter[:, 0]
    named = jnp.sum(jnp.where(request[:, None] == place[None, :], idents[None, :], 0), axis=1)
    own = (named == my_adapter).astype(jnp.int32)[:, None]
    keep = (jnp.arange(adapter_down_weight.shape[0], dtype=jnp.int32) < my_rank).astype(jnp.int32)[None, :]

    near = tokens
    for stage in stages_of(devices):
        near = jnp.concatenate([near] + [exchange(near, m, devices) for m in stage], axis=0)
    far = exchange(near, 1, devices)

    vmem = pl.BlockSpec(memory_space=pltpu.VMEM)
    near_out, far_out = pl.pallas_call(
        lambda *refs: project_kernel(rows, *refs),
        out_shape=[jax.ShapeDtypeStruct((half, model), jnp.bfloat16)] * 2,
        in_specs=[pl.BlockSpec(memory_space=pltpu.SMEM)] + [vmem] * 7,
        out_specs=[vmem] * 2,
        compiler_params=pltpu.CompilerParams(vmem_limit_bytes=40 * 1024 * 1024),
    )(
        device.astype(jnp.int32)[None],
        own,
        keep,
        near,
        far,
        pltpu.with_memory_space_constraint(base_projection_weight, pltpu.VMEM),
        pltpu.with_memory_space_constraint(adapter_down_weight, pltpu.VMEM),
        pltpu.with_memory_space_constraint(adapter_up_weight, pltpu.VMEM),
    )
    other = exchange(far_out, 1, devices)
    summed = (near_out.astype(jnp.float32) + other.astype(jnp.float32)).astype(jnp.bfloat16)
    summed = summed.reshape(devices // 2, rows, model)
    groups = [[d for d in range(devices) if d % 2 == c] for c in (0, 1)]
    pieces = lax.all_to_all(summed, "pool", 0, 0, tiled=True, axis_index_groups=groups)
    return jnp.sum(pieces.astype(jnp.float32), axis=0).astype(jnp.bfloat16)


def solution(mesh):
    return jax.shard_map(
        body,
        mesh=mesh,
        in_specs=(
            P(("groups", "pool"), None),
            P(None, "pool"),
            P("pool", None),
            P("pool", None),
            P("groups", None),
            P(),
            P(),
        ),
        out_specs=P(("groups", "pool"), None),
        check_vma=False,
    )
```

time: 141 us -> 45 us (0.32)
  waiting for transfers between devices: 81 us -> 5.75 us
  between operations: 14.8 us -> 0.76 us
  blocking collectives: 24.9 us -> 13.6 us
  matrix products: 7.91 us -> 0 us
  local copies, waits for them, and re-layouts: 2.93 us -> 7.8 us
  starting transfers between devices: 3.5 us -> 8.27 us
  Pallas kernels: 0 us -> 3.93 us
    unnamed x2 -> x0, waiting for transfers between devices: 74.9 us -> none
    all_gather x1 -> x0, blocking collectives: 24.9 us -> none  [body(): gathered = lax.all_gather(tokens, 'pool', axis=0, tiled=True)]
    all_to_all x0 -> x1, blocking collectives: none -> 13.6 us  [body(): lax.all_to_all(summed, 'pool', 0, 0, tiled=True, axis_index_groups=groups)]
    ppermute x0 -> x6, starting transfers between devices: none -> 8.27 us  [exchange(): return lax.ppermute(array, 'pool', [(d, d ^ mask) for d in range(devices)])]
    dot_general x3 -> x0, matrix products: 7.91 us -> none  [the longest x1 5.01 us: body(): jnp.dot(gathered, base_projection_weight, preferred_element_type=jnp.floa...]
    all_to_all x1 -> x0, waiting for transfers between devices: 6.09 us -> none  [body(): lax.all_to_all(base_cols, 'pool', split_axis=0, concat_axis=1, tiled=True)]
    unnamed x6, local copies, waits for them, and re-layouts: 0.79 us -> 6.56 us
    ppermute x0 -> x6, waiting for transfers between devices: none -> 5.75 us  [exchange(): return lax.ppermute(array, 'pool', [(d, d ^ mask) for d in range(devices)])]
  transfers between devices with their start and end apart: 2 -> 6, of which waited for: 2 -> 5; matrix products, arithmetic and copies ran while one was open for 4% -> 6% of each run, Pallas kernels for 0% -> 0%
where the time goes in v1:
time: 45 us; the launch traced here: 44.6 us
  blocking collectives  13.6 us (30%)
  starting transfers between devices  8.27 us (18%)
  local copies, waits for them, and re-layouts  7.8 us (17%)
  waiting for transfers between devices  5.75 us (13%)
  other arithmetic  4.55 us (10%)
  Pallas kernels  3.93 us (9%)
  between operations  0.76 us (2%)
    all_to_all x1, blocking collectives, body(): lax.all_to_all(summed, 'pool', 0, 0, tiled=True, axis_index_groups=groups)  13.6 us
    ppermute x6, starting transfers between devices, exchange(): return lax.ppermute(array, 'pool', [(d, d ^ mask) for d in range(devices)])  8.27 us
    unnamed x6, local copies, waits for them, and re-layouts  6.56 us
    ppermute x6, waiting for transfers between devices, exchange(): return lax.ppermute(array, 'pool', [(d, d ^ mask) for d in range(devices)])  5.75 us
    pallas_call x1, Pallas kernels, body(): pl.pallas_call(lambda *refs: project_kernel(rows, *refs), out_shape=[jax....  3.93 us
    reduce_sum x1, other arithmetic, body(): my_rank = jnp.sum(jnp.where(mine, adapter_block_count, 0)) * RANK_BLOCK  1.39 us
    concatenate x1, local copies, waits for them, and re-layouts, body(): jnp.concatenate([near] + [exchange(near, m, devices) for m in stage], axi...  0.97 us
  transfers between devices with their start and end apart: 6, of which 5 were waited for; matrix products, arithmetic and copies ran while one was open for 6% of the time, Pallas kernels for 0%

profile of v1, /device:TPU:0, one launch (start us, length us, event | category | flops | bytes accessed | tf_op | source)
XLA Modules:
  0.0 44.6 jit_solution(5305580308808547780)
XLA Ops:
  0.0 3.0 %collective-permute-start = (bf16[2,8192]{1,0:T(2,128)(2,1)}, bf16[2,8192]{1,0:T(2,128)(2,1)S(1)}, u32[]{:S(2)}, u32[]{:S(2)}) collective-permute-start(bf16[2,8192]{1,0:T(2,128)(2,1)} %param.7), channel_id=1, source_target_pairs={{0,2},{1,3},{2,0},{3,1},{4,6},{5,7},{6,4},{7,5},{8,10},{9,11},{10,... | collective-permute-start | bytes 98312 | tf_op jit(solution)/shard_map/ppermute | solution.py:22
  3.0 0.8 %select_reduce_fusion = s32[32]{0:T(128)S(1)} fusion(s32[32]{0:T(128)} %bitcast.4, s32[32]{0:T(128)S(1)} %fusion), kind=kLoop, calls=%fused_computation.2 | loop fusion | flops 3040 | bytes 384 | tf_op jit(solution)/shard_map/reduce_sum | solution.py:73
  3.8 1.3 %collective-permute-done = bf16[2,8192]{1,0:T(2,128)(2,1)S(1)} collective-permute-done((bf16[2,8192]{1,0:T(2,128)(2,1)}, bf16[2,8192]{1,0:T(2,128)(2,1)S(1)}, u32[]{:S(2)}, u32[]{:S(2)}) %collective-permute-start) | collective-permute-done | bytes 32800 | tf_op jit(solution)/shard_map/ppermute | solution.py:22
  5.1 0.8 %pad_maximum_fusion = bf16[4,8192]{1,0:T(4,128)(2,1)S(1)} fusion(bf16[2,8192]{1,0:T(2,128)(2,1)S(1)} %collective-permute-done, bf16[2,8192]{1,0:T(2,128)(2,1)} %param.7), kind=kLoop, calls=%fused_computation.1 | loop fusion | flops 131072 | bytes 131072 | tf_op jit(solution)/shard_map/concatenate | solution.py:79
  5.9 4.2 %collective-permute-start.3 = (bf16[4,8192]{1,0:T(4,128)(2,1)S(1)}, bf16[4,8192]{1,0:T(4,128)(2,1)S(1)}, u32[]{:S(2)}, u32[]{:S(2)}) collective-permute-start(bf16[4,8192]{1,0:T(4,128)(2,1)S(1)} %pad_maximum_fusion), channel_id=1, source_target_pairs={{0,12},{1,13},{2,14},{3,15},{4,8},{5,9},{6,10},{7,11},{8,4},{9,5},... | collective-permute-start | bytes 196616 | tf_op jit(solution)/shard_map/ppermute | solution.py:22
  10.1 0.0 collective-permute-start.2
  10.1 0.6 %collective-permute-start.1 = (bf16[4,8192]{1,0:T(4,128)(2,1)S(1)}, bf16[4,8192]{1,0:T(4,128)(2,1)S(1)}, u32[]{:S(2)}, u32[]{:S(2)}) collective-permute-start(bf16[4,8192]{1,0:T(4,128)(2,1)S(1)} %pad_maximum_fusion), channel_id=1, source_target_pairs={{0,4},{1,5},{2,6},{3,7},{4,0},{5,1},{6,2},{7,3},{8,12},{9,13},{10,... | collective-permute-start | bytes 196616 | tf_op jit(solution)/shard_map/ppermute | solution.py:22
  10.7 1.4 %fusion.2 = (s32[]{:T(128)}, s32[]{:T(128)}) fusion(s32[16]{0:T(128)} %param.12, s32[16]{0:T(128)} %param.13, s32[]{:T(128)} %axis_index.12), kind=kLoop, calls=%fused_computation.19 | loop fusion | flops 78 | bytes 140 | tf_op jit(solution)/shard_map/reduce_sum | solution.py:71
  12.1 0.4 collective-permute-done.3
  12.5 2.8 %collective-permute-done.2 = bf16[4,8192]{1,0:T(4,128)(2,1)S(1)} collective-permute-done((bf16[4,8192]{1,0:T(4,128)(2,1)S(1)}, bf16[4,8192]{1,0:T(4,128)(2,1)S(1)}, u32[]{:S(2)}, u32[]{:S(2)}) %collective-permute-start.2) | collective-permute-done | bytes 65568 | tf_op jit(solution)/shard_map/ppermute | solution.py:22
  15.3 0.0 collective-permute-done.1
  15.3 1.0 %concatenate.8.refs_3_ = bf16[16,8192]{1,0:T(8,128)(2,1)S(1)} concatenate(bf16[2,8192]{1,0:T(2,128)(2,1)} %param.7, bf16[2,8192]{1,0:T(2,128)(2,1)S(1)} %collective-permute-done, bf16[4,8192]{1,0:T(4,128)(2,1)S(1)} %collective-permute-done.1, bf16[4,8192]{1,0:T(4,128)(2,1)S(1)} %collective-permute-done.2, bf16[4,8192]{1,0:T(4,128)(2,1)S(1)} %collective-permute-done.3), dimensions={0} | concatenate | bytes 524288 | tf_op jit(solution)/shard_map/concatenate | solution.py:79
  16.2 0.1 collective-permute-start.4
  16.3 0.6 %fusion.5 = s32[32,1]{0,1:T(1,128)S(1)} fusion(s32[32]{0:T(128)S(1)} %select_reduce_fusion, s32[]{:T(128)} %get-tuple-element.10), kind=kLoop, calls=%fused_computation.22 | loop fusion | flops 64 | bytes 260 | tf_op jit(solution)/shard_map/convert_element_type | solution.py:74
  16.9 0.1 copy.9.refs_1_
  17.7 0.2 collective-permute-done.4.refs_4_
  17.8 0.0 copy-start
  17.8 3.4 %copy-done = bf16[8192,512]{1,0:T(8,128)(2,1)S(1)} copy-done((bf16[8192,512]{1,0:T(8,128)(2,1)S(1)}, bf16[8192,512]{1,0:T(8,128)(2,1)}, u32[]{:S(2)}) %copy-start) | copy-done | bytes 8388632
  21.2 0.0 copy-start.1
  21.2 1.6 %copy-done.1 = bf16[128,8192]{1,0:T(8,128)(2,1)S(1)} copy-done((bf16[128,8192]{1,0:T(8,128)(2,1)S(1)}, bf16[128,8192]{1,0:T(8,128)(2,1)}, u32[]{:S(2)}) %copy-start.1) | copy-done | bytes 2097176
  22.8 0.0 copy-start.2
  22.8 1.6 %copy-done.2 = bf16[128,8192]{1,0:T(8,128)(2,1)S(1)} copy-done((bf16[128,8192]{1,0:T(8,128)(2,1)S(1)}, bf16[128,8192]{1,0:T(8,128)(2,1)}, u32[]{:S(2)}) %copy-start.2) | copy-done | bytes 2097176
  24.4 3.9 %shard_map.73 = (bf16[16,8192]{1,0:T(8,128)(2,1)S(1)}, bf16[16,8192]{1,0:T(8,128)(2,1)S(1)}) custom-call(s32[1]{0:T(128)} %bitcast.refs_0_, s32[32,1]{1,0:T(8,128)S(1)} %copy.9.refs_1_, s32[1,128]{1,0:T(1,128)S(1)} %compare_convert_fusion.refs_2_, bf16[16,8192]{1,0:T(8,128)(2,1)S(1)} %concatenate.8.refs_3_, ...), custom_call_target="tpu_custom_call" | custom-call | tf_op jit(solution)/shard_map/pallas_call | solution.py:83
  28.3 0.4 collective-permute-start.5
  28.8 1.2 %collective-permute-done.5 = bf16[16,8192]{1,0:T(8,128)(2,1)S(1)} collective-permute-done((bf16[16,8192]{1,0:T(8,128)(2,1)S(1)}, bf16[16,8192]{1,0:T(8,128)(2,1)S(1)}, u32[]{:S(2)}, u32[]{:S(2)}) %collective-permute-start.5) | collective-permute-done | bytes 262176 | tf_op jit(solution)/shard_map/ppermute | solution.py:22
  29.9 0.1 add_convert_fusion
  30.0 0.2 reshape.75
  30.2 13.6 %all_to_all.5 = bf16[8,2,8192]{2,1,0:T(2,128)(2,1)S(1)} all-to-all(bf16[8,2,8192]{2,1,0:T(2,128)(2,1)S(1)} %reshape.75), channel_id=1, replica_groups={{0,2,4,6,8,10,12,14},{1,3,5,7,9,11,13,15},{16,18,20,22,24,26,28,30},{17..., dimensions={0} | all-to-all | bytes 524288 | tf_op jit(solution)/shard_map/all_to_all | solution.py:103
  43.8 0.9 %reduce_sum.42 = bf16[2,8192]{1,0:T(2,128)(2,1)} reduce(bf16[8,2,8192]{2,1,0:T(2,128)(2,1)S(1)} %all_to_all.5, bf16[]{:T(256)} %constant.64.clone.1), dimensions={0}, to_apply=%region_3.4 | reduce | flops 114688 | bytes 294914 | tf_op jit(solution)/shard_map/reduce_sum | solution.py:104
  (2 shorter events, 0.0 us)
Async XLA Ops:
  0.0 5.1 %collective-permute-start = (bf16[2,8192]{1,0:T(2,128)(2,1)}, bf16[2,8192]{1,0:T(2,128)(2,1)S(1)}, u32[]{:S(2)}, u32[]{:S(2)}) collective-permute-start(bf16[2,8192]{1,0:T(2,128)(2,1)} %param.7), channel_id=1, source_target_pairs={{0,2},{1,3},{2,0},{3,1},{4,6},{5,7},{6,4},{7,5},{8,10},{9,11},{10,... | collective-permute-start | bytes 98312 | tf_op jit(solution)/shard_map/ppermute | solution.py:22
  5.9 6.6 %collective-permute-start.3 = (bf16[4,8192]{1,0:T(4,128)(2,1)S(1)}, bf16[4,8192]{1,0:T(4,128)(2,1)S(1)}, u32[]{:S(2)}, u32[]{:S(2)}) collective-permute-start(bf16[4,8192]{1,0:T(4,128)(2,1)S(1)} %pad_maximum_fusion), channel_id=1, source_target_pairs={{0,12},{1,13},{2,14},{3,15},{4,8},{5,9},{6,10},{7,11},{8,4},{9,5},... | collective-permute-start | bytes 196616 | tf_op jit(solution)/shard_map/ppermute | solution.py:22
  10.1 5.2 %collective-permute-start.2 = (bf16[4,8192]{1,0:T(4,128)(2,1)S(1)}, bf16[4,8192]{1,0:T(4,128)(2,1)S(1)}, u32[]{:S(2)}, u32[]{:S(2)}) collective-permute-start(bf16[4,8192]{1,0:T(4,128)(2,1)S(1)} %pad_maximum_fusion), channel_id=1, source_target_pairs={{0,8},{1,9},{2,10},{3,11},{4,12},{5,13},{6,14},{7,15},{8,0},{9,1},... | collective-permute-start | bytes 196616 | tf_op jit(solution)/shard_map/ppermute | solution.py:22
  10.1 5.2 %collective-permute-start.1 = (bf16[4,8192]{1,0:T(4,128)(2,1)S(1)}, bf16[4,8192]{1,0:T(4,128)(2,1)S(1)}, u32[]{:S(2)}, u32[]{:S(2)}) collective-permute-start(bf16[4,8192]{1,0:T(4,128)(2,1)S(1)} %pad_maximum_fusion), channel_id=1, source_target_pairs={{0,4},{1,5},{2,6},{3,7},{4,0},{5,1},{6,2},{7,3},{8,12},{9,13},{10,... | collective-permute-start | bytes 196616 | tf_op jit(solution)/shard_map/ppermute | solution.py:22
  16.2 1.6 %collective-permute-start.4 = (bf16[16,8192]{1,0:T(8,128)(2,1)S(1)}, bf16[16,8192]{1,0:T(8,128)(2,1)S(1)}, u32[]{:S(2)}, u32[]{:S(2)}) collective-permute-start(bf16[16,8192]{1,0:T(8,128)(2,1)S(1)} %concatenate.8.refs_3_), channel_id=1, source_target_pairs={{0,1},{1,0},{2,3},{3,2},{4,5},{5,4},{6,7},{7,6},{8,9},{9,8},{10,11... | collective-permute-start | bytes 786440 | tf_op jit(solution)/shard_map/ppermute | solution.py:22
  17.8 3.4 %copy-start = (bf16[8192,512]{1,0:T(8,128)(2,1)S(1)}, bf16[8192,512]{1,0:T(8,128)(2,1)}, u32[]{:S(2)}) copy-start(bf16[8192,512]{1,0:T(8,128)(2,1)} %refs_5_.1) | copy-start | bytes 25165828
  21.2 1.6 %copy-start.1 = (bf16[128,8192]{1,0:T(8,128)(2,1)S(1)}, bf16[128,8192]{1,0:T(8,128)(2,1)}, u32[]{:S(2)}) copy-start(bf16[128,8192]{1,0:T(8,128)(2,1)} %refs_6_.1) | copy-start | bytes 6291460
  22.8 1.6 %copy-start.2 = (bf16[128,8192]{1,0:T(8,128)(2,1)S(1)}, bf16[128,8192]{1,0:T(8,128)(2,1)}, u32[]{:S(2)}) copy-start(bf16[128,8192]{1,0:T(8,128)(2,1)} %refs_7_.1) | copy-start | bytes 6291460
  28.3 1.6 %collective-permute-start.5 = (bf16[16,8192]{1,0:T(8,128)(2,1)S(1)}, bf16[16,8192]{1,0:T(8,128)(2,1)S(1)}, u32[]{:S(2)}, u32[]{:S(2)}) collective-permute-start(bf16[16,8192]{1,0:T(8,128)(2,1)S(1)} %get-tuple-element.8), channel_id=1, source_target_pairs={{0,1},{1,0},{2,3},{3,2},{4,5},{5,4},{6,7},{7,6},{8,9},{9,8},{10,11... | collective-permute-start | bytes 786440 | tf_op jit(solution)/shard_map/ppermute | solution.py:22

commit v2 on v1

v2 whole, which is shorter than its diff:
```python
import functools

import jax
import jax.numpy as jnp
from jax import lax
from jax.experimental import pallas as pl
from jax.experimental.pallas import tpu as pltpu
from jax.sharding import PartitionSpec as P

RANK_BLOCK = 16
LANES = 128
SPACE = pltpu.HBM


def stages_of(devices):
    bits = [1 << k for k in range(1, devices.bit_length() - 1)]
    stages = [[b] for b in bits[:1]]
    rest = bits[1:]
    for k in range(0, len(rest), 2):
        low = rest[k]
        stages.append([low, rest[k + 1], low + rest[k + 1]] if k + 1 < len(rest) else [low])
    return stages


def exchange(array, mask, devices):
    return lax.ppermute(array, "pool", [(d, d ^ mask) for d in range(devices)])


def canonical(rows, half, device):
    to = lax.broadcasted_iota(jnp.int32, (half, half), 0)
    of = lax.broadcasted_iota(jnp.int32, (half, half), 1)
    return to == (of ^ (rows * (device // 2)))


def mask_kernel(rows, extent, ident_ref, count_ref, slot_ref, out_ref):
    half = out_ref.shape[0]
    device = lax.axis_index("pool")

    def ranks(a, held):
        slot, count = slot_ref[a], count_ref[a] * RANK_BLOCK
        return jnp.where(slot == device, count, held[0]), jnp.where(slot == device ^ 1, count, held[1])

    rank, rank2 = lax.fori_loop(0, slot_ref.shape[0], ranks, (jnp.int32(0), jnp.int32(0)))
    row = lax.broadcasted_iota(jnp.int32, out_ref.shape, 0)
    col = lax.broadcasted_iota(jnp.int32, out_ref.shape, 1)

    def limits(q, held):
        request = (q // rows * 2 + device % 2) * rows + q % rows
        slot = slot_ref[ident_ref[request]]
        low = jnp.where(slot == device ^ 1, extent, 0)
        high = jnp.where(slot == device, rank, jnp.where(slot == device ^ 1, extent + rank2, 0))
        return jnp.where((row == q) & (col >= low) & (col < high), 1.0, held)

    out_ref[...] = lax.fori_loop(0, half, limits, jnp.zeros(out_ref.shape, jnp.float32), unroll=min(half, 16))


def delta_kernel(rows, mask_ref, near_ref, down_ref, down2_ref, up_ref, up2_ref, out_ref):
    half = near_ref.shape[0]
    extent = down_ref.shape[0]
    device = lax.axis_index("pool")
    mask = mask_ref[...]
    nt = (((1,), (1,)), ((), ()))
    order = canonical(rows, half, device).astype(jnp.bfloat16)
    ranked = []
    for ref, used in ((down_ref, mask[:, :extent]), (down2_ref, mask[:, extent:])):
        shrink = lax.dot_general(near_ref[...], ref[...], nt, preferred_element_type=jnp.float32)
        shrink = jnp.dot(order, shrink.astype(jnp.bfloat16), preferred_element_type=jnp.float32)
        ranked.append(jnp.where(used > 0, shrink, 0.0).astype(jnp.bfloat16))
    step = min(1024, out_ref.shape[1])
    for c in range(0, out_ref.shape[1], step):
        span = slice(c, c + step)
        out_ref[:, span] = (
            jnp.dot(ranked[0], up_ref[:, span], preferred_element_type=jnp.float32)
            + jnp.dot(ranked[1], up2_ref[:, span], preferred_element_type=jnp.float32)
        ).astype(jnp.bfloat16)


def base_kernel(near_ref, far_ref, weight_ref, near_out, far_out):
    half = near_ref.shape[0]
    x = jnp.concatenate([near_ref[...], far_ref[...]], axis=0)
    base = jnp.dot(x, weight_ref[...], preferred_element_type=jnp.float32)
    near_out[...] = base[:half]
    far_out[...] = base[half:]


def load_kernel(count, *refs):
    copies = [
        pltpu.make_async_copy(refs[i], refs[count + i], refs[2 * count].at[i]) for i in range(count)
    ]
    for copy in copies:
        copy.start()
    for copy in copies:
        copy.wait()


def load(*arrays):
    count = len(arrays)
    return pl.pallas_call(
        functools.partial(load_kernel, count),
        out_shape=[pltpu.VMEM(a.shape, a.dtype) for a in arrays],
        in_specs=[pl.BlockSpec(memory_space=SPACE)] * count,
        out_specs=[pl.BlockSpec(memory_space=pltpu.VMEM)] * count,
        scratch_shapes=[pltpu.SemaphoreType.DMA((count,))],
        cost_estimate=pl.CostEstimate(
            flops=0, bytes_accessed=sum(2 * a.size * a.dtype.itemsize for a in arrays), transcendentals=0
        ),
        compiler_params=pltpu.CompilerParams(vmem_limit_bytes=1024 * 1024),
        name="load",
    )(*[pltpu.with_memory_space_constraint(a, pltpu.HBM) for a in arrays])


def add_kernel(rows, delta_ref, base_ref, base2_ref, out_ref):
    half, width = base_ref.shape
    device = lax.axis_index("pool")
    order = canonical(rows, half, device).astype(jnp.float32)
    placed = [
        jnp.dot(order, ref[...], preferred_element_type=jnp.float32, precision=lax.Precision.HIGHEST)
        for ref in (base_ref, base2_ref)
    ]
    odd = device % 2 == 1
    both = jnp.concatenate(
        [jnp.where(odd, placed[1], placed[0]), jnp.where(odd, placed[0], placed[1])], axis=1
    )
    wide = 2 * width
    lanes = max(wide, LANES)
    columns = pl.ds(pl.multiple_of(device // 2 * wide // lanes * lanes, lanes), lanes)
    lane = lax.broadcasted_iota(jnp.int32, (half, lanes), 1)
    inside = lane // wide == device // 2 % (lanes // wide)
    both = jnp.where(inside, jnp.concatenate([both] * (lanes // wide), axis=1), 0.0)
    out_ref[...] = delta_ref[...]
    out_ref[:, columns] = (both + delta_ref[:, columns].astype(jnp.float32)).astype(jnp.bfloat16)


def body(
    tokens,
    base_projection_weight,
    adapter_down_weight,
    adapter_up_weight,
    request_adapter,
    adapter_block_count,
    adapter_store_slot,
):
    devices = lax.axis_size("pool")
    rows, model = tokens.shape
    half = devices // 2 * rows
    vmem, smem = pl.BlockSpec(memory_space=pltpu.VMEM), pl.BlockSpec(memory_space=pltpu.SMEM)
    params = pltpu.CompilerParams(vmem_limit_bytes=8 * 1024 * 1024)

    down2 = exchange(adapter_down_weight, 1, devices)
    up2 = exchange(adapter_up_weight, 1, devices)
    extent = adapter_down_weight.shape[0]
    mask = pl.pallas_call(
        functools.partial(mask_kernel, rows, extent),
        out_shape=jax.ShapeDtypeStruct((half, 2 * extent), jnp.float32),
        in_specs=[smem] * 3,
        out_specs=vmem,
        compiler_params=params,
        name="mask",
    )(request_adapter[:, 0], adapter_block_count, adapter_store_slot)
    near, weight = load(tokens, base_projection_weight)
    first = tokens
    down, up = adapter_down_weight, adapter_up_weight
    for k, stage in enumerate(stages_of(devices)):
        got = [exchange(first if k == 0 else near, m, devices) for m in stage]
        if k == 1:
            down, up, near = lax.optimization_barrier((down, up, near))
            down, up = load(down, up)
            down, up, near, got, mask = lax.optimization_barrier((down, up, near, got, mask))
        if k == 0:
            near, weight, got = lax.optimization_barrier((near, weight, got))
        near = jnp.concatenate([near] + got, axis=0)
    far = exchange(near, 1, devices)

    delta = pl.pallas_call(
        functools.partial(delta_kernel, rows),
        out_shape=jax.ShapeDtypeStruct((half, model), jnp.bfloat16),
        in_specs=[vmem] * 6,
        out_specs=vmem,
        compiler_params=params,
        name="delta",
    )(
        mask,
        near,
        down,
        down2,
        up,
        up2,
    )
    base, far_base = pl.pallas_call(
        base_kernel,
        out_shape=[jax.ShapeDtypeStruct((half, weight.shape[1]), jnp.float32)] * 2,
        in_specs=[vmem] * 3,
        out_specs=[vmem] * 2,
        compiler_params=params,
        name="base",
    )(near, far, weight)
    base2 = exchange(far_base, 1, devices)
    summed = pl.pallas_call(
        functools.partial(add_kernel, rows),
        out_shape=jax.ShapeDtypeStruct((half, model), jnp.bfloat16),
        in_specs=[vmem] * 3,
        out_specs=vmem,
        compiler_params=params,
        name="add",
    )(delta, base, base2)
    summed = summed.reshape(devices // 2, rows, model)
    groups = [[d for d in range(devices) if d % 2 == c] for c in (0, 1)]
    pieces = lax.all_to_all(summed, "pool", 0, 0, tiled=True, axis_index_groups=groups)
    return jnp.sum(pieces.astype(jnp.float32), axis=0).astype(jnp.bfloat16)


def solution(mesh):
    return jax.shard_map(
        body,
        mesh=mesh,
        in_specs=(
            P(("groups", "pool"), None),
            P(None, "pool"),
            P("pool", None),
            P("pool", None),
            P("groups", None),
            P(),
            P(),
        ),
        out_specs=P(("groups", "pool"), None),
        check_vma=False,
    )
```

time: 45 us -> 37.9 us (0.84)
  local copies, waits for them, and re-layouts: 7.8 us -> 0.22 us
  Pallas kernels: 3.93 us -> 11.2 us
  other arithmetic: 4.55 us -> 1.09 us
  waiting for transfers between devices: 5.75 us -> 4.49 us
  blocking collectives: 13.6 us -> 12.4 us
  between operations: 0.76 us -> 0.08 us
    pallas_call x1 -> x6, Pallas kernels: 3.93 us -> 11.2 us  [the longest x2 5.66 us: load(): pl.pallas_call(functools.partial(load_kernel, count), out_shape=[pltpu.VM...]
    unnamed x6, local copies, waits for them, and re-layouts: 6.56 us -> 0.01 us
    reduce_sum x2 -> x0, other arithmetic: 2.22 us -> none  [the longest x1 1.39 us: body(): my_rank = jnp.sum(jnp.where(mine, adapter_block_count, 0)) * RANK_BLOCK]
    ppermute x6 -> x8, waiting for transfers between devices: 5.75 us -> 4.49 us  [exchange(): return lax.ppermute(array, 'pool', [(d, d ^ mask) for d in range(devices)])]
    all_to_all x1, blocking collectives: 13.6 us -> 12.4 us  [body(): lax.all_to_all(summed, 'pool', 0, 0, tiled=True, axis_index_groups=groups)]
    concatenate x1 -> x0, local copies, waits for them, and re-layouts: 0.97 us -> none  [body(): jnp.concatenate([near] + [exchange(near, m, devices) for m in stage], axi...]
    convert_element_type x3 -> x0, other arithmetic: 0.63 us -> none  [the longest x1 0.56 us: body(): own = (named == my_adapter).astype(jnp.int32)[:, None]]
    concatenate x1 -> x2, other arithmetic: 0.83 us -> 0.23 us  [body(): near = jnp.concatenate([near] + got, axis=0)]
  transfers between devices with their start and end apart: 6 -> 8, of which waited for: 5 -> 3; matrix products, arithmetic and copies ran while one was open for 6% -> 1% of each run, Pallas kernels for 0% -> 29%
where the time goes in v2:
time: 37.9 us; the launch traced here: 37.7 us
  blocking collectives  12.4 us (33%)
  Pallas kernels  11.2 us (30%)
  starting transfers between devices  8.22 us (22%)
  waiting for transfers between devices  4.49 us (12%)
  other arithmetic  1.09 us (3%)
    all_to_all x1, blocking collectives, body(): lax.all_to_all(summed, 'pool', 0, 0, tiled=True, axis_index_groups=groups)  12.4 us
    ppermute x8, starting transfers between devices, exchange(): return lax.ppermute(array, 'pool', [(d, d ^ mask) for d in range(devices)])  8.22 us
    pallas_call x2, Pallas kernels, load(): pl.pallas_call(functools.partial(load_kernel, count), out_shape=[pltpu.VM...  5.66 us
    ppermute x8, waiting for transfers between devices, exchange(): return lax.ppermute(array, 'pool', [(d, d ^ mask) for d in range(devices)])  4.49 us
    pallas_call x1, Pallas kernels, body(): pl.pallas_call(functools.partial(delta_kernel, rows), out_shape=jax.Shape...  3.14 us
    pallas_call x1, Pallas kernels, body(): pl.pallas_call(base_kernel, out_shape=[jax.ShapeDtypeStruct((half, weight...  1.52 us
    reduce_sum x1, other arithmetic, body(): return jnp.sum(pieces.astype(jnp.float32), axis=0).astype(jnp.bfloat16)  0.85 us
  transfers between devices with their start and end apart: 8, of which 3 were waited for; matrix products, arithmetic and copies ran while one was open for 1% of the time, Pallas kernels for 29%

profile of v2, /device:TPU:0, one launch (start us, length us, event | category | flops | bytes accessed | tf_op | source)
XLA Modules:
  0.0 37.7 jit_solution(1649395322911498570)
XLA Ops:
  0.0 0.0 copy-start
  0.0 0.0 copy-start.2
  0.0 3.0 %collective-permute-start = (bf16[2,8192]{1,0:T(2,128)(2,1)}, bf16[2,8192]{1,0:T(2,128)(2,1)S(1)}, u32[]{:S(2)}, u32[]{:S(2)}) collective-permute-start(bf16[2,8192]{1,0:T(2,128)(2,1)} %refs_0_.1), channel_id=1, source_target_pairs={{0,2},{1,3},{2,0},{3,1},{4,6},{5,7},{6,4},{7,5},{8,10},{9,11},{10,... | collective-permute-start | bytes 98312 | tf_op jit(solution)/shard_map/ppermute | solution.py:26
  3.0 0.0 collective-permute-start.4
  3.0 0.5 %collective-permute-start.5 = (bf16[128,8192]{1,0:T(8,128)(2,1)}, bf16[128,8192]{1,0:T(8,128)(2,1)S(1)}, u32[]{:S(2)}, u32[]{:S(2)}) collective-permute-start(bf16[128,8192]{1,0:T(8,128)(2,1)} %refs_1_.2), channel_id=1, source_target_pairs={{0,1},{1,0},{2,3},{3,2},{4,5},{5,4},{6,7},{7,6},{8,9},{9,8},{10,11... | collective-permute-start | bytes 6291464 | tf_op jit(solution)/shard_map/ppermute | solution.py:26
  3.6 3.4 %load.2 = (bf16[2,8192]{1,0:T(2,128)(2,1)S(1)}, bf16[8192,512]{1,0:T(8,128)(2,1)S(1)}) custom-call(bf16[2,8192]{1,0:T(2,128)(2,1)} %refs_0_.1, bf16[8192,512]{1,0:T(8,128)(2,1)} %refs_1_.1), custom_call_target="tpu_custom_call" | custom-call | bytes 16842752 | tf_op jit(solution)/shard_map/load/pallas_call | solution.py:98
  7.0 0.0 collective-permute-done
  7.0 0.1 pad_maximum_fusion.1
  7.1 1.6 %collective-permute-start.1 = (bf16[4,8192]{1,0:T(4,128)(2,1)S(1)}, bf16[4,8192]{1,0:T(4,128)(2,1)S(1)}, u32[]{:S(2)}, u32[]{:S(2)}) collective-permute-start(bf16[4,8192]{1,0:T(4,128)(2,1)S(1)} %pad_maximum_fusion.1), channel_id=1, source_target_pairs={{0,4},{1,5},{2,6},{3,7},{4,0},{5,1},{6,2},{7,3},{8,12},{9,13},{10,... | collective-permute-start | bytes 196616 | tf_op jit(solution)/shard_map/ppermute | solution.py:26
  8.7 2.6 %collective-permute-start.2 = (bf16[4,8192]{1,0:T(4,128)(2,1)S(1)}, bf16[4,8192]{1,0:T(4,128)(2,1)S(1)}, u32[]{:S(2)}, u32[]{:S(2)}) collective-permute-start(bf16[4,8192]{1,0:T(4,128)(2,1)S(1)} %pad_maximum_fusion.1), channel_id=1, source_target_pairs={{0,8},{1,9},{2,10},{3,11},{4,12},{5,13},{6,14},{7,15},{8,0},{9,1},... | collective-permute-start | bytes 196616 | tf_op jit(solution)/shard_map/ppermute | solution.py:26
  11.3 0.2 collective-permute-start.3
  11.5 0.0 copy-done
  11.5 0.0 copy-done.1
  11.5 0.0 copy-done.2
  11.5 0.7 %mask.1.mask_ref = f32[16,256]{1,0:T(8,128)S(1)} custom-call(s32[32]{0:T(128)S(1)} %bitcast.1, s32[16]{0:T(128)S(1)} %copy-done.1, s32[16]{0:T(128)S(1)} %copy-done.2), custom_call_target="tpu_custom_call" | custom-call | tf_op jit(solution)/shard_map/mask/pallas_call | solution.py:152
  12.3 2.2 %load.3 = (bf16[128,8192]{1,0:T(8,128)(2,1)S(1)}, bf16[128,8192]{1,0:T(8,128)(2,1)S(1)}) custom-call(bf16[128,8192]{1,0:T(8,128)(2,1)} %refs_0_.2, bf16[128,8192]{1,0:T(8,128)(2,1)} %refs_1_.2), custom_call_target="tpu_custom_call" | custom-call | bytes 8388608 | tf_op jit(solution)/shard_map/load/pallas_call | solution.py:98
  14.5 0.0 collective-permute-done.1
  14.5 1.7 %collective-permute-done.2 = bf16[4,8192]{1,0:T(4,128)(2,1)S(1)} collective-permute-done((bf16[4,8192]{1,0:T(4,128)(2,1)S(1)}, bf16[4,8192]{1,0:T(4,128)(2,1)S(1)}, u32[]{:S(2)}, u32[]{:S(2)}) %collective-permute-start.2) | collective-permute-done | bytes 65568 | tf_op jit(solution)/shard_map/ppermute | solution.py:26
  16.2 1.3 %collective-permute-done.3 = bf16[4,8192]{1,0:T(4,128)(2,1)S(1)} collective-permute-done((bf16[4,8192]{1,0:T(4,128)(2,1)S(1)}, bf16[4,8192]{1,0:T(4,128)(2,1)S(1)}, u32[]{:S(2)}, u32[]{:S(2)}) %collective-permute-start.3) | collective-permute-done | bytes 65568 | tf_op jit(solution)/shard_map/ppermute | solution.py:26
  17.5 0.2 pad_maximum_fusion.near_ref
  17.6 0.1 collective-permute-start.6
  17.7 1.5 %collective-permute-done.6.far_ref = bf16[16,8192]{1,0:T(8,128)(2,1)S(1)} collective-permute-done((bf16[16,8192]{1,0:T(8,128)(2,1)S(1)}, bf16[16,8192]{1,0:T(8,128)(2,1)S(1)}, u32[]{:S(2)}, u32[]{:S(2)}) %collective-permute-start.6) | collective-permute-done | bytes 262176 | tf_op jit(solution)/shard_map/ppermute | solution.py:26
  19.2 1.5 %base.1 = (f32[16,512]{1,0:T(8,128)S(1)}, f32[16,512]{1,0:T(8,128)S(1)}) custom-call(bf16[16,8192]{1,0:T(8,128)(2,1)S(1)} %pad_maximum_fusion.near_ref, bf16[16,8192]{1,0:T(8,128)(2,1)S(1)} %collective-permute-done.6.far_ref, bf16[8192,512]{1,0:T(8,128)(2,1)S(1)} %get-tuple-element.40.weight_ref), custom_call_target="tpu_custom_call" | custom-call | tf_op jit(solution)/shard_map/base/pallas_call | solution.py:189
  20.7 0.2 collective-permute-start.7
  20.9 0.0 collective-permute-done.4.down2_ref
  20.9 0.0 collective-permute-done.5.up2_ref
  20.9 3.1 %delta.1.delta_ref = bf16[16,8192]{1,0:T(8,128)(2,1)S(1)} custom-call(f32[16,256]{1,0:T(8,128)S(1)} %mask.1.mask_ref, bf16[16,8192]{1,0:T(8,128)(2,1)S(1)} %pad_maximum_fusion.near_ref, bf16[128,8192]{1,0:T(8,128)(2,1)S(1)} %get-tuple-element.38.down_ref, bf16[128,8192]{1,0:T(8,128)(2,1)S(1)} %collective-permute-done.4.down2_ref, ...), custom_call_target="tpu_custom_call" | custom-call | tf_op jit(solution)/shard_map/delta/pallas_call | solution.py:174
  24.0 0.0 collective-permute-done.7.base2_ref
  24.1 0.2 add.1
  24.3 0.2 reshape.3
  24.5 12.4 %all_to_all.5 = bf16[8,2,8192]{2,1,0:T(2,128)(2,1)S(1)} all-to-all(bf16[8,2,8192]{2,1,0:T(2,128)(2,1)S(1)} %reshape.3), channel_id=1, replica_groups={{0,2,4,6,8,10,12,14},{1,3,5,7,9,11,13,15},{16,18,20,22,24,26,28,30},{17..., dimensions={0} | all-to-all | bytes 524288 | tf_op jit(solution)/shard_map/all_to_all | solution.py:208
  36.9 0.9 %reduce_sum.12 = bf16[2,8192]{1,0:T(2,128)(2,1)} reduce(bf16[8,2,8192]{2,1,0:T(2,128)(2,1)S(1)} %all_to_all.5, bf16[]{:T(256)} %constant.2.clone.1), dimensions={0}, to_apply=%region_0.0 | reduce | flops 114688 | bytes 294914 | tf_op jit(solution)/shard_map/reduce_sum | solution.py:209
  (1 shorter events, 0.0 us)
Async XLA Ops:
  0.0 11.5 %copy-start = (s32[32,1]{0,1:T(1,128)S(1)}, s32[32,1]{0,1:T(1,128)}, u32[]{:S(2)}) copy-start(s32[32,1]{0,1:T(1,128)} %param.11) | copy-start | bytes 388
  0.0 11.5 %copy-start.1 = (s32[16]{0:T(128)S(1)}, s32[16]{0:T(128)}, u32[]{:S(2)}) copy-start(s32[16]{0:T(128)} %count_ref.1) | copy-start | bytes 196
  0.0 11.5 %copy-start.2 = (s32[16]{0:T(128)S(1)}, s32[16]{0:T(128)}, u32[]{:S(2)}) copy-start(s32[16]{0:T(128)} %slot_ref.1) | copy-start | bytes 196
  0.0 7.0 %collective-permute-start = (bf16[2,8192]{1,0:T(2,128)(2,1)}, bf16[2,8192]{1,0:T(2,128)(2,1)S(1)}, u32[]{:S(2)}, u32[]{:S(2)}) collective-permute-start(bf16[2,8192]{1,0:T(2,128)(2,1)} %refs_0_.1), channel_id=1, source_target_pairs={{0,2},{1,3},{2,0},{3,1},{4,6},{5,7},{6,4},{7,5},{8,10},{9,11},{10,... | collective-permute-start | bytes 98312 | tf_op jit(solution)/shard_map/ppermute | solution.py:26
  3.0 17.9 %collective-permute-start.4 = (bf16[128,8192]{1,0:T(8,128)(2,1)}, bf16[128,8192]{1,0:T(8,128)(2,1)S(1)}, u32[]{:S(2)}, u32[]{:S(2)}) collective-permute-start(bf16[128,8192]{1,0:T(8,128)(2,1)} %refs_0_.2), channel_id=1, source_target_pairs={{0,1},{1,0},{2,3},{3,2},{4,5},{5,4},{6,7},{7,6},{8,9},{9,8},{10,11... | collective-permute-start | bytes 6291464 | tf_op jit(solution)/shard_map/ppermute | solution.py:26
  3.0 17.9 %collective-permute-start.5 = (bf16[128,8192]{1,0:T(8,128)(2,1)}, bf16[128,8192]{1,0:T(8,128)(2,1)S(1)}, u32[]{:S(2)}, u32[]{:S(2)}) collective-permute-start(bf16[128,8192]{1,0:T(8,128)(2,1)} %refs_1_.2), channel_id=1, source_target_pairs={{0,1},{1,0},{2,3},{3,2},{4,5},{5,4},{6,7},{7,6},{8,9},{9,8},{10,11... | collective-permute-start | bytes 6291464 | tf_op jit(solution)/shard_map/ppermute | solution.py:26
  7.1 7.4 %collective-permute-start.1 = (bf16[4,8192]{1,0:T(4,128)(2,1)S(1)}, bf16[4,8192]{1,0:T(4,128)(2,1)S(1)}, u32[]{:S(2)}, u32[]{:S(2)}) collective-permute-start(bf16[4,8192]{1,0:T(4,128)(2,1)S(1)} %pad_maximum_fusion.1), channel_id=1, source_target_pairs={{0,4},{1,5},{2,6},{3,7},{4,0},{5,1},{6,2},{7,3},{8,12},{9,13},{10,... | collective-permute-start | bytes 196616 | tf_op jit(solution)/shard_map/ppermute | solution.py:26
  8.7 7.5 %collective-permute-start.2 = (bf16[4,8192]{1,0:T(4,128)(2,1)S(1)}, bf16[4,8192]{1,0:T(4,128)(2,1)S(1)}, u32[]{:S(2)}, u32[]{:S(2)}) collective-permute-start(bf16[4,8192]{1,0:T(4,128)(2,1)S(1)} %pad_maximum_fusion.1), channel_id=1, source_target_pairs={{0,8},{1,9},{2,10},{3,11},{4,12},{5,13},{6,14},{7,15},{8,0},{9,1},... | collective-permute-start | bytes 196616 | tf_op jit(solution)/shard_map/ppermute | solution.py:26
  11.3 6.2 %collective-permute-start.3 = (bf16[4,8192]{1,0:T(4,128)(2,1)S(1)}, bf16[4,8192]{1,0:T(4,128)(2,1)S(1)}, u32[]{:S(2)}, u32[]{:S(2)}) collective-permute-start(bf16[4,8192]{1,0:T(4,128)(2,1)S(1)} %pad_maximum_fusion.1), channel_id=1, source_target_pairs={{0,12},{1,13},{2,14},{3,15},{4,8},{5,9},{6,10},{7,11},{8,4},{9,5},... | collective-permute-start | bytes 196616 | tf_op jit(solution)/shard_map/ppermute | solution.py:26
  17.6 1.6 %collective-permute-start.6 = (bf16[16,8192]{1,0:T(8,128)(2,1)S(1)}, bf16[16,8192]{1,0:T(8,128)(2,1)S(1)}, u32[]{:S(2)}, u32[]{:S(2)}) collective-permute-start(bf16[16,8192]{1,0:T(8,128)(2,1)S(1)} %pad_maximum_fusion.near_ref), channel_id=1, source_target_pairs={{0,1},{1,0},{2,3},{3,2},{4,5},{5,4},{6,7},{7,6},{8,9},{9,8},{10,11... | collective-permute-start | bytes 786440 | tf_op jit(solution)/shard_map/ppermute | solution.py:26
  20.7 3.3 %collective-permute-start.7 = (f32[16,512]{1,0:T(8,128)S(1)}, f32[16,512]{1,0:T(8,128)S(1)}, u32[]{:S(2)}, u32[]{:S(2)}) collective-permute-start(f32[16,512]{1,0:T(8,128)S(1)} %get-tuple-element.42), channel_id=1, source_target_pairs={{0,1},{1,0},{2,3},{3,2},{4,5},{5,4},{6,7},{7,6},{8,9},{9,8},{10,11... | collective-permute-start | bytes 98312 | tf_op jit(solution)/shard_map/ppermute | solution.py:26

commit v3 on v2

--- a/solution.py
+++ b/solution.py
@@ -54,24 +54,29 @@
     out_ref[...] = lax.fori_loop(0, half, limits, jnp.zeros(out_ref.shape, jnp.float32), unroll=min(half, 16))
 
 
-def delta_kernel(rows, mask_ref, near_ref, down_ref, down2_ref, up_ref, up2_ref, out_ref):
-    half = near_ref.shape[0]
-    extent = down_ref.shape[0]
-    device = lax.axis_index("pool")
-    mask = mask_ref[...]
-    nt = (((1,), (1,)), ((), ()))
-    order = canonical(rows, half, device).astype(jnp.bfloat16)
-    ranked = []
-    for ref, used in ((down_ref, mask[:, :extent]), (down2_ref, mask[:, extent:])):
-        shrink = lax.dot_general(near_ref[...], ref[...], nt, preferred_element_type=jnp.float32)
-        shrink = jnp.dot(order, shrink.astype(jnp.bfloat16), preferred_element_type=jnp.float32)
-        ranked.append(jnp.where(used > 0, shrink, 0.0).astype(jnp.bfloat16))
-    step = min(1024, out_ref.shape[1])
-    for c in range(0, out_ref.shape[1], step):
+def shrink_kernel(rows, mask_ref, near_ref, down_ref, down2_ref, out_ref):
+    half, extent = near_ref.shape[0], down_ref.shape[0]
+    order = canonical(rows, half, lax.axis_index("pool")).astype(jnp.bfloat16)
+    near = near_ref[...]
+    shrink = jnp.concatenate(
+        [
+            lax.dot_general(near, ref[...], (((1,), (1,)), ((), ())), preferred_element_type=jnp.float32)
+            for ref in (down_ref, down2_ref)
+        ],
+        axis=1,
+    )
+    shrink = jnp.dot(order, shrink.astype(jnp.bfloat16), preferred_element_type=jnp.float32)
+    out_ref[...] = jnp.where(mask_ref[...] > 0, shrink, 0.0).astype(jnp.bfloat16)
+
+
+def delta_kernel(shrink_ref, up_ref, up2_ref, out_ref):
+    extent, model = up_ref.shape
+    step = min(1024, model)
+    for c in range(0, model, step):
         span = slice(c, c + step)
         out_ref[:, span] = (
-            jnp.dot(ranked[0], up_ref[:, span], preferred_element_type=jnp.float32)
-            + jnp.dot(ranked[1], up2_ref[:, span], preferred_element_type=jnp.float32)
+            jnp.dot(shrink_ref[:, :extent], up_ref[:, span], preferred_element_type=jnp.float32)
+            + jnp.dot(shrink_ref[:, extent:], up2_ref[:, span], preferred_element_type=jnp.float32)
         ).astype(jnp.bfloat16)
 
 
@@ -161,7 +166,7 @@
     first = tokens
     down, up = adapter_down_weight, adapter_up_weight
     for k, stage in enumerate(stages_of(devices)):
-        got = [exchange(first if k == 0 else near, m, devices) for m in stage]
+        got = [exchange(first if k == 0 else near, m, devices) for m in stage[::-1]][::-1]
         if k == 1:
             down, up, near = lax.optimization_barrier((down, up, near))
             down, up = load(down, up)
@@ -171,21 +176,15 @@
         near = jnp.concatenate([near] + got, axis=0)
     far = exchange(near, 1, devices)
 
-    delta = pl.pallas_call(
-        functools.partial(delta_kernel, rows),
-        out_shape=jax.ShapeDtypeStruct((half, model), jnp.bfloat16),
-        in_specs=[vmem] * 6,
-        out_specs=vmem,
-        compiler_params=params,
-        name="delta",
-    )(
-        mask,
-        near,
-        down,
-        down2,
-        up,
-        up2,
-    )
+    shrink = pl.pallas_call(
+        functools.partial(shrink_kernel, rows),
+        out_shape=jax.ShapeDtypeStruct((half, 2 * extent), jnp.bfloat16),
+        in_specs=[vmem] * 4,
+        out_specs=vmem,
+        compiler_params=params,
+        name="shrink",
+    )(mask, near, down, down2)
+    far, shrink = lax.optimization_barrier((far, shrink))
     base, far_base = pl.pallas_call(
         base_kernel,
         out_shape=[jax.ShapeDtypeStruct((half, weight.shape[1]), jnp.float32)] * 2,
@@ -194,7 +193,16 @@
         compiler_params=params,
         name="base",
     )(near, far, weight)
+    shrink, base, far_base = lax.optimization_barrier((shrink, base, far_base))
     base2 = exchange(far_base, 1, devices)
+    delta = pl.pallas_call(
+        delta_kernel,
+        out_shape=jax.ShapeDtypeStruct((half, model), jnp.bfloat16),
+        in_specs=[vmem] * 3,
+        out_specs=vmem,
+        compiler_params=params,
+        name="delta",
+    )(shrink, up, up2)
     summed = pl.pallas_call(
         functools.partial(add_kernel, rows),
         out_shape=jax.ShapeDtypeStruct((half, model), jnp.bfloat16),

time: 37.9 us -> 35.7 us (0.942)
  Pallas kernels: 11.2 us -> 10 us
  waiting for transfers between devices: 4.49 us -> 3.42 us
    pallas_call x1 -> x2, Pallas kernels: 3.14 us -> 1.96 us  [the longest x1 1.3 us: body(): pl.pallas_call(functools.partial(shrink_kernel, rows), out_shape=jax.Shap...]
    ppermute x8, waiting for transfers between devices: 4.49 us -> 3.42 us  [exchange(): return lax.ppermute(array, 'pool', [(d, d ^ mask) for d in range(devices)])]
  transfers between devices with their start and end apart: 8 -> 8, of which waited for: 3 -> 4; matrix products, arithmetic and copies ran while one was open for 1% -> 1% of each run, Pallas kernels for 29% -> 28%
where the time goes in v3:
time: 35.7 us; the launch traced here: 35.5 us
  blocking collectives  12.3 us (34%)
  Pallas kernels  10 us (28%)
  starting transfers between devices  8.38 us (23%)
  waiting for transfers between devices  3.42 us (10%)
  other arithmetic  1.09 us (3%)
    all_to_all x1, blocking collectives, body(): lax.all_to_all(summed, 'pool', 0, 0, tiled=True, axis_index_groups=groups)  12.3 us
    ppermute x8, starting transfers between devices, exchange(): return lax.ppermute(array, 'pool', [(d, d ^ mask) for d in range(devices)])  8.38 us
    pallas_call x2, Pallas kernels, load(): pl.pallas_call(functools.partial(load_kernel, count), out_shape=[pltpu.VM...  5.66 us
    ppermute x8, waiting for transfers between devices, exchange(): return lax.ppermute(array, 'pool', [(d, d ^ mask) for d in range(devices)])  3.42 us
    pallas_call x1, Pallas kernels, body(): pl.pallas_call(base_kernel, out_shape=[jax.ShapeDtypeStruct((half, weight...  1.52 us
    pallas_call x1, Pallas kernels, body(): pl.pallas_call(functools.partial(shrink_kernel, rows), out_shape=jax.Shap...  1.3 us
    reduce_sum x1, other arithmetic, body(): return jnp.sum(pieces.astype(jnp.float32), axis=0).astype(jnp.bfloat16)  0.85 us
    pallas_call x1, Pallas kernels, body(): pl.pallas_call(functools.partial(mask_kernel, rows, extent), out_shape=ja...  0.71 us
  transfers between devices with their start and end apart: 8, of which 4 were waited for; matrix products, arithmetic and copies ran while one was open for 1% of the time, Pallas kernels for 28%

profile of v3, /device:TPU:0, one launch (start us, length us, event | category | flops | bytes accessed | tf_op | source)
XLA Modules:
  0.0 35.5 jit_solution(15820197249706783297)
XLA Ops:
  0.0 0.0 copy-start
  0.0 3.0 %collective-permute-start = (bf16[2,8192]{1,0:T(2,128)(2,1)}, bf16[2,8192]{1,0:T(2,128)(2,1)S(1)}, u32[]{:S(2)}, u32[]{:S(2)}) collective-permute-start(bf16[2,8192]{1,0:T(2,128)(2,1)} %refs_0_.1), channel_id=1, source_target_pairs={{0,2},{1,3},{2,0},{3,1},{4,6},{5,7},{6,4},{7,5},{8,10},{9,11},{10,... | collective-permute-start | bytes 98312 | tf_op jit(solution)/shard_map/ppermute | solution.py:26
  3.0 0.0 collective-permute-start.5
  3.0 0.5 %collective-permute-start.6 = (bf16[128,8192]{1,0:T(8,128)(2,1)}, bf16[128,8192]{1,0:T(8,128)(2,1)S(1)}, u32[]{:S(2)}, u32[]{:S(2)}) collective-permute-start(bf16[128,8192]{1,0:T(8,128)(2,1)} %refs_1_.2), channel_id=1, source_target_pairs={{0,1},{1,0},{2,3},{3,2},{4,5},{5,4},{6,7},{7,6},{8,9},{9,8},{10,11... | collective-permute-start | bytes 6291464 | tf_op jit(solution)/shard_map/ppermute | solution.py:26
  3.6 3.4 %load.2 = (bf16[2,8192]{1,0:T(2,128)(2,1)S(1)}, bf16[8192,512]{1,0:T(8,128)(2,1)S(1)}) custom-call(bf16[2,8192]{1,0:T(2,128)(2,1)} %refs_0_.1, bf16[8192,512]{1,0:T(8,128)(2,1)} %refs_1_.1), custom_call_target="tpu_custom_call" | custom-call | bytes 16842752 | tf_op jit(solution)/shard_map/load/pallas_call | solution.py:103
  7.0 0.0 collective-permute-done
  7.0 0.1 pad_maximum_fusion.1
  7.1 1.6 %collective-permute-start.1 = (bf16[4,8192]{1,0:T(4,128)(2,1)S(1)}, bf16[4,8192]{1,0:T(4,128)(2,1)S(1)}, u32[]{:S(2)}, u32[]{:S(2)}) collective-permute-start(bf16[4,8192]{1,0:T(4,128)(2,1)S(1)} %pad_maximum_fusion.1), channel_id=1, source_target_pairs={{0,4},{1,5},{2,6},{3,7},{4,0},{5,1},{6,2},{7,3},{8,12},{9,13},{10,... | collective-permute-start | bytes 196616 | tf_op jit(solution)/shard_map/ppermute | solution.py:26
  8.7 2.6 %collective-permute-start.2 = (bf16[4,8192]{1,0:T(4,128)(2,1)S(1)}, bf16[4,8192]{1,0:T(4,128)(2,1)S(1)}, u32[]{:S(2)}, u32[]{:S(2)}) collective-permute-start(bf16[4,8192]{1,0:T(4,128)(2,1)S(1)} %pad_maximum_fusion.1), channel_id=1, source_target_pairs={{0,8},{1,9},{2,10},{3,11},{4,12},{5,13},{6,14},{7,15},{8,0},{9,1},... | collective-permute-start | bytes 196616 | tf_op jit(solution)/shard_map/ppermute | solution.py:26
  11.3 0.2 collective-permute-start.3
  11.5 0.0 copy-done
  11.5 0.0 copy-done.1
  11.5 0.0 copy-done.2
  11.5 0.7 %mask.1.mask_ref = f32[16,256]{1,0:T(8,128)S(1)} custom-call(s32[32]{0:T(128)S(1)} %bitcast.1, s32[16]{0:T(128)S(1)} %copy-done.1, s32[16]{0:T(128)S(1)} %copy-done.2), custom_call_target="tpu_custom_call" | custom-call | tf_op jit(solution)/shard_map/mask/pallas_call | solution.py:157
  12.3 2.2 %load.3 = (bf16[128,8192]{1,0:T(8,128)(2,1)S(1)}, bf16[128,8192]{1,0:T(8,128)(2,1)S(1)}) custom-call(bf16[128,8192]{1,0:T(8,128)(2,1)} %refs_0_.2, bf16[128,8192]{1,0:T(8,128)(2,1)} %refs_1_.2), custom_call_target="tpu_custom_call" | custom-call | bytes 8388608 | tf_op jit(solution)/shard_map/load/pallas_call | solution.py:103
  14.5 0.0 collective-permute-done.1
  14.5 1.7 %collective-permute-done.2 = bf16[4,8192]{1,0:T(4,128)(2,1)S(1)} collective-permute-done((bf16[4,8192]{1,0:T(4,128)(2,1)S(1)}, bf16[4,8192]{1,0:T(4,128)(2,1)S(1)}, u32[]{:S(2)}, u32[]{:S(2)}) %collective-permute-start.2) | collective-permute-done | bytes 65568 | tf_op jit(solution)/shard_map/ppermute | solution.py:26
  16.2 1.3 %collective-permute-done.3 = bf16[4,8192]{1,0:T(4,128)(2,1)S(1)} collective-permute-done((bf16[4,8192]{1,0:T(4,128)(2,1)S(1)}, bf16[4,8192]{1,0:T(4,128)(2,1)S(1)}, u32[]{:S(2)}, u32[]{:S(2)}) %collective-permute-start.3) | collective-permute-done | bytes 65568 | tf_op jit(solution)/shard_map/ppermute | solution.py:26
  17.5 0.2 pad_maximum_fusion.near_ref
  17.6 0.1 collective-permute-start.4
  17.7 0.0 collective-permute-done.5.down2_ref
  17.7 1.3 %shrink.1.shrink_ref = bf16[16,256]{1,0:T(8,128)(2,1)S(1)} custom-call(f32[16,256]{1,0:T(8,128)S(1)} %mask.1.mask_ref, bf16[16,8192]{1,0:T(8,128)(2,1)S(1)} %pad_maximum_fusion.near_ref, bf16[128,8192]{1,0:T(8,128)(2,1)S(1)} %get-tuple-element.43.down_ref, bf16[128,8192]{1,0:T(8,128)(2,1)S(1)} %collective-permute-done.5.down2_ref), custom_call_target="tpu_custom_call" | custom-call | tf_op jit(solution)/shard_map/shrink/pallas_call | solution.py:179
  19.0 0.2 collective-permute-done.4.far_ref
  19.2 1.5 %base.1 = (f32[16,512]{1,0:T(8,128)S(1)}, f32[16,512]{1,0:T(8,128)S(1)}) custom-call(bf16[16,8192]{1,0:T(8,128)(2,1)S(1)} %pad_maximum_fusion.near_ref, bf16[16,8192]{1,0:T(8,128)(2,1)S(1)} %collective-permute-done.4.far_ref, bf16[8192,512]{1,0:T(8,128)(2,1)S(1)} %get-tuple-element.46.weight_ref), custom_call_target="tpu_custom_call" | custom-call | tf_op jit(solution)/shard_map/base/pallas_call | solution.py:188
  20.7 0.3 collective-permute-start.7
  21.1 0.0 collective-permute-done.6.up2_ref
  21.1 0.7 %delta.1.delta_ref = bf16[16,8192]{1,0:T(8,128)(2,1)S(1)} custom-call(bf16[16,256]{1,0:T(8,128)(2,1)S(1)} %shrink.1.shrink_ref, bf16[128,8192]{1,0:T(8,128)(2,1)S(1)} %get-tuple-element.50.up_ref, bf16[128,8192]{1,0:T(8,128)(2,1)S(1)} %collective-permute-done.6.up2_ref), custom_call_target="tpu_custom_call" | custom-call | tf_op jit(solution)/shard_map/delta/pallas_call | solution.py:198
  21.7 0.2 collective-permute-done.7.base2_ref
  22.0 0.2 add.1
  22.2 0.2 reshape.3
  22.4 12.3 %all_to_all.5 = bf16[8,2,8192]{2,1,0:T(2,128)(2,1)S(1)} all-to-all(bf16[8,2,8192]{2,1,0:T(2,128)(2,1)S(1)} %reshape.3), channel_id=1, replica_groups={{0,2,4,6,8,10,12,14},{1,3,5,7,9,11,13,15},{16,18,20,22,24,26,28,30},{17..., dimensions={0} | all-to-all | bytes 524288 | tf_op jit(solution)/shard_map/all_to_all | solution.py:216
  34.7 0.9 %reduce_sum.12 = bf16[2,8192]{1,0:T(2,128)(2,1)} reduce(bf16[8,2,8192]{2,1,0:T(2,128)(2,1)S(1)} %all_to_all.5, bf16[]{:T(256)} %constant.2.clone.1), dimensions={0}, to_apply=%region_0.0 | reduce | flops 114688 | bytes 294914 | tf_op jit(solution)/shard_map/reduce_sum | solution.py:217
  (2 shorter events, 0.0 us)
Async XLA Ops:
  0.0 11.5 %copy-start = (s32[32,1]{0,1:T(1,128)S(1)}, s32[32,1]{0,1:T(1,128)}, u32[]{:S(2)}) copy-start(s32[32,1]{0,1:T(1,128)} %param.11) | copy-start | bytes 388
  0.0 11.5 %copy-start.1 = (s32[16]{0:T(128)S(1)}, s32[16]{0:T(128)}, u32[]{:S(2)}) copy-start(s32[16]{0:T(128)} %count_ref.1) | copy-start | bytes 196
  0.0 11.5 %copy-start.2 = (s32[16]{0:T(128)S(1)}, s32[16]{0:T(128)}, u32[]{:S(2)}) copy-start(s32[16]{0:T(128)} %slot_ref.1) | copy-start | bytes 196
  0.0 7.0 %collective-permute-start = (bf16[2,8192]{1,0:T(2,128)(2,1)}, bf16[2,8192]{1,0:T(2,128)(2,1)S(1)}, u32[]{:S(2)}, u32[]{:S(2)}) collective-permute-start(bf16[2,8192]{1,0:T(2,128)(2,1)} %refs_0_.1), channel_id=1, source_target_pairs={{0,2},{1,3},{2,0},{3,1},{4,6},{5,7},{6,4},{7,5},{8,10},{9,11},{10,... | collective-permute-start | bytes 98312 | tf_op jit(solution)/shard_map/ppermute | solution.py:26
  3.0 14.7 %collective-permute-start.5 = (bf16[128,8192]{1,0:T(8,128)(2,1)}, bf16[128,8192]{1,0:T(8,128)(2,1)S(1)}, u32[]{:S(2)}, u32[]{:S(2)}) collective-permute-start(bf16[128,8192]{1,0:T(8,128)(2,1)} %refs_0_.2), channel_id=1, source_target_pairs={{0,1},{1,0},{2,3},{3,2},{4,5},{5,4},{6,7},{7,6},{8,9},{9,8},{10,11... | collective-permute-start | bytes 6291464 | tf_op jit(solution)/shard_map/ppermute | solution.py:26
  3.0 18.0 %collective-permute-start.6 = (bf16[128,8192]{1,0:T(8,128)(2,1)}, bf16[128,8192]{1,0:T(8,128)(2,1)S(1)}, u32[]{:S(2)}, u32[]{:S(2)}) collective-permute-start(bf16[128,8192]{1,0:T(8,128)(2,1)} %refs_1_.2), channel_id=1, source_target_pairs={{0,1},{1,0},{2,3},{3,2},{4,5},{5,4},{6,7},{7,6},{8,9},{9,8},{10,11... | collective-permute-start | bytes 6291464 | tf_op jit(solution)/shard_map/ppermute | solution.py:26
  7.1 7.4 %collective-permute-start.1 = (bf16[4,8192]{1,0:T(4,128)(2,1)S(1)}, bf16[4,8192]{1,0:T(4,128)(2,1)S(1)}, u32[]{:S(2)}, u32[]{:S(2)}) collective-permute-start(bf16[4,8192]{1,0:T(4,128)(2,1)S(1)} %pad_maximum_fusion.1), channel_id=1, source_target_pairs={{0,4},{1,5},{2,6},{3,7},{4,0},{5,1},{6,2},{7,3},{8,12},{9,13},{10,... | collective-permute-start | bytes 196616 | tf_op jit(solution)/shard_map/ppermute | solution.py:26
  8.7 7.5 %collective-permute-start.2 = (bf16[4,8192]{1,0:T(4,128)(2,1)S(1)}, bf16[4,8192]{1,0:T(4,128)(2,1)S(1)}, u32[]{:S(2)}, u32[]{:S(2)}) collective-permute-start(bf16[4,8192]{1,0:T(4,128)(2,1)S(1)} %pad_maximum_fusion.1), channel_id=1, source_target_pairs={{0,8},{1,9},{2,10},{3,11},{4,12},{5,13},{6,14},{7,15},{8,0},{9,1},... | collective-permute-start | bytes 196616 | tf_op jit(solution)/shard_map/ppermute | solution.py:26
  11.3 6.2 %collective-permute-start.3 = (bf16[4,8192]{1,0:T(4,128)(2,1)S(1)}, bf16[4,8192]{1,0:T(4,128)(2,1)S(1)}, u32[]{:S(2)}, u32[]{:S(2)}) collective-permute-start(bf16[4,8192]{1,0:T(4,128)(2,1)S(1)} %pad_maximum_fusion.1), channel_id=1, source_target_pairs={{0,12},{1,13},{2,14},{3,15},{4,8},{5,9},{6,10},{7,11},{8,4},{9,5},... | collective-permute-start | bytes 196616 | tf_op jit(solution)/shard_map/ppermute | solution.py:26
  17.6 1.6 %collective-permute-start.4 = (bf16[16,8192]{1,0:T(8,128)(2,1)S(1)}, bf16[16,8192]{1,0:T(8,128)(2,1)S(1)}, u32[]{:S(2)}, u32[]{:S(2)}) collective-permute-start(bf16[16,8192]{1,0:T(8,128)(2,1)S(1)} %pad_maximum_fusion.near_ref), channel_id=1, source_target_pairs={{0,1},{1,0},{2,3},{3,2},{4,5},{5,4},{6,7},{7,6},{8,9},{9,8},{10,11... | collective-permute-start | bytes 786440 | tf_op jit(solution)/shard_map/ppermute | solution.py:26
  20.7 1.2 %collective-permute-start.7 = (f32[16,512]{1,0:T(8,128)S(1)}, f32[16,512]{1,0:T(8,128)S(1)}, u32[]{:S(2)}, u32[]{:S(2)}) collective-permute-start(f32[16,512]{1,0:T(8,128)S(1)} %get-tuple-element.52), channel_id=1, source_target_pairs={{0,1},{1,0},{2,3},{3,2},{4,5},{5,4},{6,7},{7,6},{8,9},{9,8},{10,11... | collective-permute-start | bytes 98312 | tf_op jit(solution)/shard_map/ppermute | solution.py:26

commit v4 on v3

--- a/solution.py
+++ b/solution.py
@@ -9,7 +9,6 @@
 
 RANK_BLOCK = 16
 LANES = 128
-SPACE = pltpu.HBM
 
 
 def stages_of(devices):
@@ -40,7 +39,10 @@
         slot, count = slot_ref[a], count_ref[a] * RANK_BLOCK
         return jnp.where(slot == device, count, held[0]), jnp.where(slot == device ^ 1, count, held[1])
 
-    rank, rank2 = lax.fori_loop(0, slot_ref.shape[0], ranks, (jnp.int32(0), jnp.int32(0)))
+    adapters = slot_ref.shape[0]
+    rank, rank2 = lax.fori_loop(
+        0, adapters, ranks, (jnp.int32(0), jnp.int32(0)), unroll=min(adapters, 16)
+    )
     row = lax.broadcasted_iota(jnp.int32, out_ref.shape, 0)
     col = lax.broadcasted_iota(jnp.int32, out_ref.shape, 1)
 
@@ -80,38 +82,44 @@
         ).astype(jnp.bfloat16)
 
 
-def base_kernel(near_ref, far_ref, weight_ref, near_out, far_out):
+def base_kernel(near_ref, far_ref, weight_ref, weight2_ref, near_out, far_out):
     half = near_ref.shape[0]
+    cut = weight_ref.shape[0]
     x = jnp.concatenate([near_ref[...], far_ref[...]], axis=0)
-    base = jnp.dot(x, weight_ref[...], preferred_element_type=jnp.float32)
+    base = jnp.dot(x[:, :cut], weight_ref[...], preferred_element_type=jnp.float32)
+    base += jnp.dot(x[:, cut:], weight2_ref[...], preferred_element_type=jnp.float32)
     near_out[...] = base[:half]
     far_out[...] = base[half:]
 
 
-def load_kernel(count, *refs):
-    copies = [
-        pltpu.make_async_copy(refs[i], refs[count + i], refs[2 * count].at[i]) for i in range(count)
-    ]
+def load_kernel(starts, *refs):
+    count = len(starts)
+    copies = []
+    for i, start in enumerate(starts):
+        held = refs[count + i]
+        source = refs[i].at[pl.ds(start, held.shape[0])]
+        copies.append(pltpu.make_async_copy(source, held, refs[2 * count].at[i]))
     for copy in copies:
         copy.start()
     for copy in copies:
         copy.wait()
 
 
-def load(*arrays):
-    count = len(arrays)
+def load(*parts):
+    count = len(parts)
+    shapes = [((stop - start, a.shape[1]), a.dtype) for a, start, stop in parts]
     return pl.pallas_call(
-        functools.partial(load_kernel, count),
-        out_shape=[pltpu.VMEM(a.shape, a.dtype) for a in arrays],
-        in_specs=[pl.BlockSpec(memory_space=SPACE)] * count,
+        functools.partial(load_kernel, [start for _, start, _ in parts]),
+        out_shape=[pltpu.VMEM(*shape) for shape in shapes],
+        in_specs=[pl.BlockSpec(memory_space=pltpu.HBM)] * count,
         out_specs=[pl.BlockSpec(memory_space=pltpu.VMEM)] * count,
         scratch_shapes=[pltpu.SemaphoreType.DMA((count,))],
         cost_estimate=pl.CostEstimate(
-            flops=0, bytes_accessed=sum(2 * a.size * a.dtype.itemsize for a in arrays), transcendentals=0
+            flops=0, bytes_accessed=sum(4 * dims[0] * dims[1] for dims, _ in shapes), transcendentals=0
         ),
         compiler_params=pltpu.CompilerParams(vmem_limit_bytes=1024 * 1024),
         name="load",
-    )(*[pltpu.with_memory_space_constraint(a, pltpu.HBM) for a in arrays])
+    )(*[pltpu.with_memory_space_constraint(a, pltpu.HBM) for a, _, _ in parts])
 
 
 def add_kernel(rows, delta_ref, base_ref, base2_ref, out_ref):
@@ -132,8 +140,13 @@
     lane = lax.broadcasted_iota(jnp.int32, (half, lanes), 1)
     inside = lane // wide == device // 2 % (lanes // wide)
     both = jnp.where(inside, jnp.concatenate([both] * (lanes // wide), axis=1), 0.0)
-    out_ref[...] = delta_ref[...]
-    out_ref[:, columns] = (both + delta_ref[:, columns].astype(jnp.float32)).astype(jnp.bfloat16)
+    out_ref[...] = delta_ref[...].reshape(out_ref.shape)
+    both = (both + delta_ref[:, columns].astype(jnp.float32)).astype(jnp.bfloat16)
+    out_ref[:, :, columns] = both.reshape(out_ref.shape[:2] + (lanes,))
+
+
+def sum_kernel(pieces_ref, out_ref):
+    out_ref[...] = jnp.sum(pieces_ref[...].astype(jnp.float32), axis=0).astype(jnp.bfloat16)
 
 
 def body(
@@ -162,17 +175,18 @@
         compiler_params=params,
         name="mask",
     )(request_adapter[:, 0], adapter_block_count, adapter_store_slot)
-    near, weight = load(tokens, base_projection_weight)
-    first = tokens
-    down, up = adapter_down_weight, adapter_up_weight
+    weight, down, up = base_projection_weight, adapter_down_weight, adapter_up_weight
+    cut = model * 3 // 8
+    near, head = load((tokens, 0, rows), (weight, 0, cut))
     for k, stage in enumerate(stages_of(devices)):
-        got = [exchange(first if k == 0 else near, m, devices) for m in stage[::-1]][::-1]
+        got = [exchange(near if k else tokens, m, devices) for m in stage]
+        if k == 0:
+            near, head, got = lax.optimization_barrier((near, head, got))
         if k == 1:
-            down, up, near = lax.optimization_barrier((down, up, near))
-            down, up = load(down, up)
-            down, up, near, got, mask = lax.optimization_barrier((down, up, near, got, mask))
-        if k == 0:
-            near, weight, got = lax.optimization_barrier((near, weight, got))
+            weight, down, up, near = lax.optimization_barrier((weight, down, up, near))
+            (tail,) = load((weight, cut, model))
+            near, tail, mask, *got = lax.optimization_barrier((near, tail, mask, *got[::-1]))
+            got = got[::-1]
         near = jnp.concatenate([near] + got, axis=0)
     far = exchange(near, 1, devices)
 
@@ -188,11 +202,11 @@
     base, far_base = pl.pallas_call(
         base_kernel,
         out_shape=[jax.ShapeDtypeStruct((half, weight.shape[1]), jnp.float32)] * 2,
-        in_specs=[vmem] * 3,
+        in_specs=[vmem] * 4,
         out_specs=[vmem] * 2,
         compiler_params=params,
         name="base",
-    )(near, far, weight)
+    )(near, far, head, tail)
     shrink, base, far_base = lax.optimization_barrier((shrink, base, far_base))
     base2 = exchange(far_base, 1, devices)
     delta = pl.pallas_call(
@@ -205,16 +219,22 @@
     )(shrink, up, up2)
     summed = pl.pallas_call(
         functools.partial(add_kernel, rows),
-        out_shape=jax.ShapeDtypeStruct((half, model), jnp.bfloat16),
+        out_shape=pltpu.VMEM((devices // 2, rows, model), jnp.bfloat16),
         in_specs=[vmem] * 3,
         out_specs=vmem,
         compiler_params=params,
         name="add",
     )(delta, base, base2)
-    summed = summed.reshape(devices // 2, rows, model)
     groups = [[d for d in range(devices) if d % 2 == c] for c in (0, 1)]
     pieces = lax.all_to_all(summed, "pool", 0, 0, tiled=True, axis_index_groups=groups)
-    return jnp.sum(pieces.astype(jnp.float32), axis=0).astype(jnp.bfloat16)
+    return pl.pallas_call(
+        sum_kernel,
+        out_shape=jax.ShapeDtypeStruct((rows, model), jnp.bfloat16),
+        in_specs=[vmem],
+        out_specs=vmem,
+        compiler_params=params,
+        name="sum",
+    )(pieces)
 
 
 def solution(mesh):

time: 35.7 us -> 34.3 us (0.961)
  waiting for transfers between devices: 3.42 us -> 2.1 us
  blocking collectives: 12.3 us -> 13.5 us
  other arithmetic: 1.09 us -> 0.23 us
    ppermute x8, waiting for transfers between devices: 3.42 us -> 2.1 us  [exchange(): return lax.ppermute(array, 'pool', [(d, d ^ mask) for d in range(devices)])]
    all_to_all x1, blocking collectives: 12.3 us -> 13.5 us  [body(): lax.all_to_all(summed, 'pool', 0, 0, tiled=True, axis_index_groups=groups)]
    reduce_sum x1 -> x0, other arithmetic: 0.85 us -> none  [body(): return jnp.sum(pieces.astype(jnp.float32), axis=0).astype(jnp.bfloat16)]
    pallas_call x3 -> x4, Pallas kernels: 5.84 us -> 5.66 us  [the longest x2 4.57 us: load(): pl.pallas_call(functools.partial(load_kernel, [start for _, start, _ in p...]
  transfers between devices with their start and end apart: 8 -> 8, of which waited for: 4 -> 3; matrix products, arithmetic and copies ran while one was open for 1% -> 1% of each run, Pallas kernels for 28% -> 25%
where the time goes in v4:
time: 34.3 us; the launch traced here: 34.2 us
  blocking collectives  13.5 us (39%)
  Pallas kernels  9.78 us (29%)
  starting transfers between devices  8.39 us (24%)
  waiting for transfers between devices  2.1 us (6%)
    all_to_all x1, blocking collectives, body(): lax.all_to_all(summed, 'pool', 0, 0, tiled=True, axis_index_groups=groups)  13.5 us
    ppermute x8, starting transfers between devices, exchange(): return lax.ppermute(array, 'pool', [(d, d ^ mask) for d in range(devices)])  8.39 us
    pallas_call x2, Pallas kernels, load(): pl.pallas_call(functools.partial(load_kernel, [start for _, start, _ in p...  4.57 us
    ppermute x8, waiting for transfers between devices, exchange(): return lax.ppermute(array, 'pool', [(d, d ^ mask) for d in range(devices)])  2.1 us
    pallas_call x1, Pallas kernels, body(): pl.pallas_call(base_kernel, out_shape=[jax.ShapeDtypeStruct((half, weight...  1.52 us
    pallas_call x1, Pallas kernels, body(): pl.pallas_call(functools.partial(shrink_kernel, rows), out_shape=jax.Shap...  1.3 us
    pallas_call x1, Pallas kernels, body(): pl.pallas_call(sum_kernel, out_shape=jax.ShapeDtypeStruct((rows, model),...  0.87 us
  transfers between devices with their start and end apart: 8, of which 3 were waited for; matrix products, arithmetic and copies ran while one was open for 1% of the time, Pallas kernels for 25%

profile of v4, /device:TPU:0, one launch (start us, length us, event | category | flops | bytes accessed | tf_op | source)
XLA Modules:
  0.0 34.2 jit_solution(8061639843257170539)
XLA Ops:
  0.0 3.0 %collective-permute-start = (bf16[2,8192]{1,0:T(2,128)(2,1)}, bf16[2,8192]{1,0:T(2,128)(2,1)S(1)}, u32[]{:S(2)}, u32[]{:S(2)}) collective-permute-start(bf16[2,8192]{1,0:T(2,128)(2,1)} %refs_0_.1), channel_id=1, source_target_pairs={{0,2},{1,3},{2,0},{3,1},{4,6},{5,7},{6,4},{7,5},{8,10},{9,11},{10,... | collective-permute-start | bytes 98312 | tf_op jit(solution)/shard_map/ppermute | solution.py:25
  3.0 0.0 collective-permute-start.5
  3.0 0.5 %collective-permute-start.6 = (bf16[128,8192]{1,0:T(8,128)(2,1)}, bf16[128,8192]{1,0:T(8,128)(2,1)S(1)}, u32[]{:S(2)}, u32[]{:S(2)}) collective-permute-start(bf16[128,8192]{1,0:T(8,128)(2,1)} %up_ref), channel_id=1, source_target_pairs={{0,1},{1,0},{2,3},{3,2},{4,5},{5,4},{6,7},{7,6},{8,9},{9,8},{10,11... | collective-permute-start | bytes 6291464 | tf_op jit(solution)/shard_map/ppermute | solution.py:25
  3.6 1.9 %load.2 = (bf16[2,8192]{1,0:T(2,128)(2,1)S(1)}, bf16[3072,512]{1,0:T(8,128)(2,1)S(1)}) custom-call(bf16[2,8192]{1,0:T(2,128)(2,1)} %refs_0_.1, bf16[8192,512]{1,0:T(8,128)(2,1)} %refs_0_.2), custom_call_target="tpu_custom_call" | custom-call | bytes 6356992 | tf_op jit(solution)/shard_map/load/pallas_call | solution.py:111
  5.5 0.0 collective-permute-done
  5.5 0.1 pad_maximum_fusion.1
  5.6 3.8 %collective-permute-start.1 = (bf16[4,8192]{1,0:T(4,128)(2,1)S(1)}, bf16[4,8192]{1,0:T(4,128)(2,1)S(1)}, u32[]{:S(2)}, u32[]{:S(2)}) collective-permute-start(bf16[4,8192]{1,0:T(4,128)(2,1)S(1)} %pad_maximum_fusion.1), channel_id=1, source_target_pairs={{0,12},{1,13},{2,14},{3,15},{4,8},{5,9},{6,10},{7,11},{8,4},{9,5},... | collective-permute-start | bytes 196616 | tf_op jit(solution)/shard_map/ppermute | solution.py:25
  9.4 0.0 collective-permute-start.2
  9.4 0.6 %collective-permute-start.3 = (bf16[4,8192]{1,0:T(4,128)(2,1)S(1)}, bf16[4,8192]{1,0:T(4,128)(2,1)S(1)}, u32[]{:S(2)}, u32[]{:S(2)}) collective-permute-start(bf16[4,8192]{1,0:T(4,128)(2,1)S(1)} %pad_maximum_fusion.1), channel_id=1, source_target_pairs={{0,4},{1,5},{2,6},{3,7},{4,0},{5,1},{6,2},{7,3},{8,12},{9,13},{10,... | collective-permute-start | bytes 196616 | tf_op jit(solution)/shard_map/ppermute | solution.py:25
  10.0 0.0 copy-done.2
  10.0 0.0 copy-done.3
  10.0 0.0 copy-done.4
  10.0 0.6 %mask.1.mask_ref = f32[16,256]{1,0:T(8,128)S(1)} custom-call(s32[32]{0:T(128)S(1)} %bitcast.1, s32[16]{0:T(128)S(1)} %copy-done.3, s32[16]{0:T(128)S(1)} %copy-done.4), custom_call_target="tpu_custom_call" | custom-call | tf_op jit(solution)/shard_map/mask/pallas_call | solution.py:170
  10.7 0.0 copy-start
  10.7 2.6 %load.3.weight2_ref = bf16[5120,512]{1,0:T(8,128)(2,1)S(1)} custom-call(bf16[8192,512]{1,0:T(8,128)(2,1)} %refs_0_.2), custom_call_target="tpu_custom_call" | custom-call | bytes 10485760 | tf_op jit(solution)/shard_map/load/pallas_call | solution.py:111
  13.4 0.0 collective-permute-done.1
  13.4 1.6 %collective-permute-done.2 = bf16[4,8192]{1,0:T(4,128)(2,1)S(1)} collective-permute-done((bf16[4,8192]{1,0:T(4,128)(2,1)S(1)}, bf16[4,8192]{1,0:T(4,128)(2,1)S(1)}, u32[]{:S(2)}, u32[]{:S(2)}) %collective-permute-start.2) | collective-permute-done | bytes 65568 | tf_op jit(solution)/shard_map/ppermute | solution.py:25
  15.0 0.0 collective-permute-done.3
  15.0 0.2 pad_maximum_fusion.near_ref
  15.2 0.1 collective-permute-start.4
  15.3 0.0 collective-permute-done.5.down2_ref
  15.3 0.0 copy-done
  15.3 1.3 %shrink.1.shrink_ref = bf16[16,256]{1,0:T(8,128)(2,1)S(1)} custom-call(f32[16,256]{1,0:T(8,128)S(1)} %mask.1.mask_ref, bf16[16,8192]{1,0:T(8,128)(2,1)S(1)} %pad_maximum_fusion.near_ref, bf16[128,8192]{1,0:T(8,128)(2,1)S(1)} %copy-done, bf16[128,8192]{1,0:T(8,128)(2,1)S(1)} %collective-permute-done.5.down2_ref), custom_call_target="tpu_custom_call" | custom-call | tf_op jit(solution)/shard_map/shrink/pallas_call | solution.py:193
  16.6 0.2 collective-permute-done.4.far_ref
  16.8 1.5 %base.1 = (f32[16,512]{1,0:T(8,128)S(1)}, f32[16,512]{1,0:T(8,128)S(1)}) custom-call(bf16[16,8192]{1,0:T(8,128)(2,1)S(1)} %pad_maximum_fusion.near_ref, bf16[16,8192]{1,0:T(8,128)(2,1)S(1)} %collective-permute-done.4.far_ref, bf16[3072,512]{1,0:T(8,128)(2,1)S(1)} %get-tuple-element.41.weight_ref, bf16[5120,512]{1,0:T(8,128)(2,1)S(1)} %load.3.weight2_ref), custom_call_target="tpu_custom_call" | custom-call | tf_op jit(solution)/shard_map/base/pallas_call | solution.py:202
  18.3 0.3 collective-permute-start.7
  18.6 0.0 collective-permute-done.6.up2_ref
  18.6 0.7 %delta.1.delta_ref = bf16[16,8192]{1,0:T(8,128)(2,1)S(1)} custom-call(bf16[16,256]{1,0:T(8,128)(2,1)S(1)} %shrink.1.shrink_ref, bf16[128,8192]{1,0:T(8,128)(2,1)S(1)} %copy-done.1, bf16[128,8192]{1,0:T(8,128)(2,1)S(1)} %collective-permute-done.6.up2_ref), custom_call_target="tpu_custom_call" | custom-call | tf_op jit(solution)/shard_map/delta/pallas_call | solution.py:212
  19.3 0.2 collective-permute-done.7.base2_ref
  19.5 0.2 add.1
  19.8 13.5 %all_to_all.5.pieces_ref = bf16[8,2,8192]{2,1,0:T(2,128)(2,1)S(1)} all-to-all(bf16[8,2,8192]{2,1,0:T(2,128)(2,1)S(1)} %add.1), channel_id=1, replica_groups={{0,2,4,6,8,10,12,14},{1,3,5,7,9,11,13,15},{16,18,20,22,24,26,28,30},{17..., dimensions={0} | all-to-all | bytes 524288 | tf_op jit(solution)/shard_map/all_to_all | solution.py:229
  33.3 0.9 %sum.1 = bf16[2,8192]{1,0:T(2,128)(2,1)} custom-call(bf16[8,2,8192]{2,1,0:T(2,128)(2,1)S(1)} %all_to_all.5.pieces_ref), custom_call_target="tpu_custom_call" | custom-call | tf_op jit(solution)/shard_map/sum/pallas_call | solution.py:230
  (5 shorter events, 0.0 us)
Async XLA Ops:
  0.0 10.0 %copy-start.2 = (s32[32,1]{0,1:T(1,128)S(1)}, s32[32,1]{0,1:T(1,128)}, u32[]{:S(2)}) copy-start(s32[32,1]{0,1:T(1,128)} %param.11) | copy-start | bytes 388
  0.0 10.0 %copy-start.3 = (s32[16]{0:T(128)S(1)}, s32[16]{0:T(128)}, u32[]{:S(2)}) copy-start(s32[16]{0:T(128)} %count_ref.1) | copy-start | bytes 196
  0.0 10.0 %copy-start.4 = (s32[16]{0:T(128)S(1)}, s32[16]{0:T(128)}, u32[]{:S(2)}) copy-start(s32[16]{0:T(128)} %slot_ref.1) | copy-start | bytes 196
  0.0 5.5 %collective-permute-start = (bf16[2,8192]{1,0:T(2,128)(2,1)}, bf16[2,8192]{1,0:T(2,128)(2,1)S(1)}, u32[]{:S(2)}, u32[]{:S(2)}) collective-permute-start(bf16[2,8192]{1,0:T(2,128)(2,1)} %refs_0_.1), channel_id=1, source_target_pairs={{0,2},{1,3},{2,0},{3,1},{4,6},{5,7},{6,4},{7,5},{8,10},{9,11},{10,... | collective-permute-start | bytes 98312 | tf_op jit(solution)/shard_map/ppermute | solution.py:25
  3.0 12.2 %collective-permute-start.5 = (bf16[128,8192]{1,0:T(8,128)(2,1)}, bf16[128,8192]{1,0:T(8,128)(2,1)S(1)}, u32[]{:S(2)}, u32[]{:S(2)}) collective-permute-start(bf16[128,8192]{1,0:T(8,128)(2,1)} %down_ref), channel_id=1, source_target_pairs={{0,1},{1,0},{2,3},{3,2},{4,5},{5,4},{6,7},{7,6},{8,9},{9,8},{10,11... | collective-permute-start | bytes 6291464 | tf_op jit(solution)/shard_map/ppermute | solution.py:25
  3.0 15.6 %collective-permute-start.6 = (bf16[128,8192]{1,0:T(8,128)(2,1)}, bf16[128,8192]{1,0:T(8,128)(2,1)S(1)}, u32[]{:S(2)}, u32[]{:S(2)}) collective-permute-start(bf16[128,8192]{1,0:T(8,128)(2,1)} %up_ref), channel_id=1, source_target_pairs={{0,1},{1,0},{2,3},{3,2},{4,5},{5,4},{6,7},{7,6},{8,9},{9,8},{10,11... | collective-permute-start | bytes 6291464 | tf_op jit(solution)/shard_map/ppermute | solution.py:25
  5.6 7.8 %collective-permute-start.1 = (bf16[4,8192]{1,0:T(4,128)(2,1)S(1)}, bf16[4,8192]{1,0:T(4,128)(2,1)S(1)}, u32[]{:S(2)}, u32[]{:S(2)}) collective-permute-start(bf16[4,8192]{1,0:T(4,128)(2,1)S(1)} %pad_maximum_fusion.1), channel_id=1, source_target_pairs={{0,12},{1,13},{2,14},{3,15},{4,8},{5,9},{6,10},{7,11},{8,4},{9,5},... | collective-permute-start | bytes 196616 | tf_op jit(solution)/shard_map/ppermute | solution.py:25
  9.4 5.6 %collective-permute-start.2 = (bf16[4,8192]{1,0:T(4,128)(2,1)S(1)}, bf16[4,8192]{1,0:T(4,128)(2,1)S(1)}, u32[]{:S(2)}, u32[]{:S(2)}) collective-permute-start(bf16[4,8192]{1,0:T(4,128)(2,1)S(1)} %pad_maximum_fusion.1), channel_id=1, source_target_pairs={{0,8},{1,9},{2,10},{3,11},{4,12},{5,13},{6,14},{7,15},{8,0},{9,1},... | collective-permute-start | bytes 196616 | tf_op jit(solution)/shard_map/ppermute | solution.py:25
  9.4 5.6 %collective-permute-start.3 = (bf16[4,8192]{1,0:T(4,128)(2,1)S(1)}, bf16[4,8192]{1,0:T(4,128)(2,1)S(1)}, u32[]{:S(2)}, u32[]{:S(2)}) collective-permute-start(bf16[4,8192]{1,0:T(4,128)(2,1)S(1)} %pad_maximum_fusion.1), channel_id=1, source_target_pairs={{0,4},{1,5},{2,6},{3,7},{4,0},{5,1},{6,2},{7,3},{8,12},{9,13},{10,... | collective-permute-start | bytes 196616 | tf_op jit(solution)/shard_map/ppermute | solution.py:25
  10.7 4.6 %copy-start = (bf16[128,8192]{1,0:T(8,128)(2,1)S(1)}, bf16[128,8192]{1,0:T(8,128)(2,1)}, u32[]{:S(2)}) copy-start(bf16[128,8192]{1,0:T(8,128)(2,1)} %down_ref) | copy-start | bytes 6291460
  15.2 1.6 %collective-permute-start.4 = (bf16[16,8192]{1,0:T(8,128)(2,1)S(1)}, bf16[16,8192]{1,0:T(8,128)(2,1)S(1)}, u32[]{:S(2)}, u32[]{:S(2)}) collective-permute-start(bf16[16,8192]{1,0:T(8,128)(2,1)S(1)} %pad_maximum_fusion.near_ref), channel_id=1, source_target_pairs={{0,1},{1,0},{2,3},{3,2},{4,5},{5,4},{6,7},{7,6},{8,9},{9,8},{10,11... | collective-permute-start | bytes 786440 | tf_op jit(solution)/shard_map/ppermute | solution.py:25
  16.6 2.0 %copy-start.1 = (bf16[128,8192]{1,0:T(8,128)(2,1)S(1)}, bf16[128,8192]{1,0:T(8,128)(2,1)}, u32[]{:S(2)}) copy-start(bf16[128,8192]{1,0:T(8,128)(2,1)} %up_ref) | copy-start | bytes 6291460
  18.3 1.2 %collective-permute-start.7 = (f32[16,512]{1,0:T(8,128)S(1)}, f32[16,512]{1,0:T(8,128)S(1)}, u32[]{:S(2)}, u32[]{:S(2)}) collective-permute-start(f32[16,512]{1,0:T(8,128)S(1)} %get-tuple-element.48), channel_id=1, source_target_pairs={{0,1},{1,0},{2,3},{3,2},{4,5},{5,4},{6,7},{7,6},{8,9},{9,8},{10,11... | collective-permute-start | bytes 98312 | tf_op jit(solution)/shard_map/ppermute | solution.py:25

commit v5 on v4

--- a/solution.py
+++ b/solution.py
@@ -25,10 +25,10 @@
     return lax.ppermute(array, "pool", [(d, d ^ mask) for d in range(devices)])
 
 
-def canonical(rows, half, device):
+def by_y(rows, half):
     to = lax.broadcasted_iota(jnp.int32, (half, half), 0)
     of = lax.broadcasted_iota(jnp.int32, (half, half), 1)
-    return to == (of ^ (rows * (device // 2)))
+    return of == to % (half // 2) // rows * 2 * rows + to // (half // 2) * rows + to % rows
 
 
 def mask_kernel(rows, extent, ident_ref, count_ref, slot_ref, out_ref):
@@ -47,7 +47,8 @@
     col = lax.broadcasted_iota(jnp.int32, out_ref.shape, 1)
 
     def limits(q, held):
-        request = (q // rows * 2 + device % 2) * rows + q % rows
+        chip = q % (half // 2) // rows * 2 + q // (half // 2)
+        request = (device ^ (2 * chip)) * rows + q % rows
         slot = slot_ref[ident_ref[request]]
         low = jnp.where(slot == device ^ 1, extent, 0)
         high = jnp.where(slot == device, rank, jnp.where(slot == device ^ 1, extent + rank2, 0))
@@ -57,8 +58,6 @@
 
 
 def shrink_kernel(rows, mask_ref, near_ref, down_ref, down2_ref, out_ref):
-    half, extent = near_ref.shape[0], down_ref.shape[0]
-    order = canonical(rows, half, lax.axis_index("pool")).astype(jnp.bfloat16)
     near = near_ref[...]
     shrink = jnp.concatenate(
         [
@@ -67,29 +66,40 @@
         ],
         axis=1,
     )
+    order = by_y(rows, near.shape[0]).astype(jnp.bfloat16)
     shrink = jnp.dot(order, shrink.astype(jnp.bfloat16), preferred_element_type=jnp.float32)
     out_ref[...] = jnp.where(mask_ref[...] > 0, shrink, 0.0).astype(jnp.bfloat16)
 
 
-def delta_kernel(shrink_ref, up_ref, up2_ref, out_ref):
+def delta_kernel(shrink_ref, up_ref, up2_ref, own_out, other_out):
     extent, model = up_ref.shape
+    part = own_out.shape[0]
     step = min(1024, model)
     for c in range(0, model, step):
         span = slice(c, c + step)
-        out_ref[:, span] = (
-            jnp.dot(shrink_ref[:, :extent], up_ref[:, span], preferred_element_type=jnp.float32)
-            + jnp.dot(shrink_ref[:, extent:], up2_ref[:, span], preferred_element_type=jnp.float32)
-        ).astype(jnp.bfloat16)
-
-
-def base_kernel(near_ref, far_ref, weight_ref, weight2_ref, near_out, far_out):
-    half = near_ref.shape[0]
+        delta = jnp.dot(
+            shrink_ref[:, :extent], up_ref[:, span], preferred_element_type=jnp.float32
+        ) + jnp.dot(shrink_ref[:, extent:], up2_ref[:, span], preferred_element_type=jnp.float32)
+        own_out[:, span] = delta[:part].astype(jnp.bfloat16)
+        other_out[:, span] = delta[part:].astype(jnp.bfloat16)
+
+
+def base_kernel(rows, near_ref, far_ref, weight_ref, weight2_ref, *outs):
+    part = outs[0].shape[0]
     cut = weight_ref.shape[0]
     x = jnp.concatenate([near_ref[...], far_ref[...]], axis=0)
     base = jnp.dot(x[:, :cut], weight_ref[...], preferred_element_type=jnp.float32)
     base += jnp.dot(x[:, cut:], weight2_ref[...], preferred_element_type=jnp.float32)
-    near_out[...] = base[:half]
-    far_out[...] = base[half:]
+    order = by_y(rows, 2 * part).astype(jnp.float32)
+    for k in (0, 2):
+        placed = jnp.dot(
+            order,
+            base[k * part : (k + 2) * part],
+            preferred_element_type=jnp.float32,
+            precision=lax.Precision.HIGHEST,
+        )
+        outs[k][...] = placed[:part]
+        outs[k + 1][...] = placed[part:]
 
 
 def load_kernel(starts, *refs):
@@ -122,31 +132,32 @@
     )(*[pltpu.with_memory_space_constraint(a, pltpu.HBM) for a, _, _ in parts])
 
 
-def add_kernel(rows, delta_ref, base_ref, base2_ref, out_ref):
-    half, width = base_ref.shape
+def add_kernel(own_ref, other_ref, *refs):
+    pieces, outs = [refs[k][...] for k in (0, 3, 1, 2)], refs[4:]
+    rows = outs[0].shape[0]
+    width = pieces[0].shape[1]
     device = lax.axis_index("pool")
-    order = canonical(rows, half, device).astype(jnp.float32)
-    placed = [
-        jnp.dot(order, ref[...], preferred_element_type=jnp.float32, precision=lax.Precision.HIGHEST)
-        for ref in (base_ref, base2_ref)
-    ]
-    odd = device % 2 == 1
-    both = jnp.concatenate(
-        [jnp.where(odd, placed[1], placed[0]), jnp.where(odd, placed[0], placed[1])], axis=1
-    )
-    wide = 2 * width
-    lanes = max(wide, LANES)
-    columns = pl.ds(pl.multiple_of(device // 2 * wide // lanes * lanes, lanes), lanes)
-    lane = lax.broadcasted_iota(jnp.int32, (half, lanes), 1)
-    inside = lane // wide == device // 2 % (lanes // wide)
-    both = jnp.where(inside, jnp.concatenate([both] * (lanes // wide), axis=1), 0.0)
-    out_ref[...] = delta_ref[...].reshape(out_ref.shape)
-    both = (both + delta_ref[:, columns].astype(jnp.float32)).astype(jnp.bfloat16)
-    out_ref[:, :, columns] = both.reshape(out_ref.shape[:2] + (lanes,))
-
-
-def sum_kernel(pieces_ref, out_ref):
-    out_ref[...] = jnp.sum(pieces_ref[...].astype(jnp.float32), axis=0).astype(jnp.bfloat16)
+    columns = pl.ds(pl.multiple_of(device // 4 * (4 * width), 4 * width), 4 * width)
+    base = []
+    for place in range(4):
+        piece = pieces[0]
+        for mask in (1, 2, 3):
+            piece = jnp.where(device % 4 == place ^ mask, pieces[mask], piece)
+        base.append(piece)
+    base = jnp.concatenate(base, axis=1)
+    both = own_ref[...].astype(jnp.float32) + other_ref[...].astype(jnp.float32)
+    part = own_ref[:, columns].astype(jnp.float32) + other_ref[:, columns].astype(jnp.float32) + base
+    for k, out in enumerate(outs):
+        span = slice(k * rows, (k + 1) * rows)
+        out[...] = both[span].astype(jnp.bfloat16)
+        out[:, columns] = part[span].astype(jnp.bfloat16)
+
+
+def sum_kernel(*refs):
+    total = refs[0][...].astype(jnp.float32)
+    for ref in refs[1:-1]:
+        total += ref[...].astype(jnp.float32)
+    refs[-1][...] = total.astype(jnp.bfloat16)
 
 
 def body(
@@ -176,7 +187,7 @@
         name="mask",
     )(request_adapter[:, 0], adapter_block_count, adapter_store_slot)
     weight, down, up = base_projection_weight, adapter_down_weight, adapter_up_weight
-    cut = model * 3 // 8
+    cut = model // 2
     near, head = load((tokens, 0, rows), (weight, 0, cut))
     for k, stage in enumerate(stages_of(devices)):
         got = [exchange(near if k else tokens, m, devices) for m in stage]
@@ -198,43 +209,42 @@
         compiler_params=params,
         name="shrink",
     )(mask, near, down, down2)
-    far, shrink = lax.optimization_barrier((far, shrink))
-    base, far_base = pl.pallas_call(
-        base_kernel,
-        out_shape=[jax.ShapeDtypeStruct((half, weight.shape[1]), jnp.float32)] * 2,
+    own, other = pl.pallas_call(
+        delta_kernel,
+        out_shape=[jax.ShapeDtypeStruct((half // 2, model), jnp.bfloat16)] * 2,
+        in_specs=[vmem] * 3,
+        out_specs=[vmem] * 2,
+        compiler_params=params,
+        name="delta",
+    )(shrink, up, up2)
+    other = exchange(other, 2, devices)
+    far, own = lax.optimization_barrier((far, own))
+    base = pl.pallas_call(
+        functools.partial(base_kernel, rows),
+        out_shape=[jax.ShapeDtypeStruct((half // 2, weight.shape[1]), jnp.float32)] * 4,
         in_specs=[vmem] * 4,
-        out_specs=[vmem] * 2,
+        out_specs=[vmem] * 4,
         compiler_params=params,
         name="base",
     )(near, far, head, tail)
-    shrink, base, far_base = lax.optimization_barrier((shrink, base, far_base))
-    base2 = exchange(far_base, 1, devices)
-    delta = pl.pallas_call(
-        delta_kernel,
-        out_shape=jax.ShapeDtypeStruct((half, model), jnp.bfloat16),
-        in_specs=[vmem] * 3,
-        out_specs=vmem,
-        compiler_params=params,
-        name="delta",
-    )(shrink, up, up2)
-    summed = pl.pallas_call(
-        functools.partial(add_kernel, rows),
-        out_shape=pltpu.VMEM((devices // 2, rows, model), jnp.bfloat16),
-        in_specs=[vmem] * 3,
-        out_specs=vmem,
+    base = [base[0], exchange(base[2], 1, devices), exchange(base[1], 2, devices), exchange(base[3], 3, devices)]
+    sums = pl.pallas_call(
+        add_kernel,
+        out_shape=[jax.ShapeDtypeStruct((rows, model), jnp.bfloat16)] * (devices // 4),
+        in_specs=[vmem] * 6,
+        out_specs=[vmem] * (devices // 4),
         compiler_params=params,
         name="add",
-    )(delta, base, base2)
-    groups = [[d for d in range(devices) if d % 2 == c] for c in (0, 1)]
-    pieces = lax.all_to_all(summed, "pool", 0, 0, tiled=True, axis_index_groups=groups)
+    )(own, other, base[0], base[2], base[3], base[1])
+    got = [exchange(sums[k], 4 * k, devices) for k in range(1, devices // 4)]
     return pl.pallas_call(
         sum_kernel,
         out_shape=jax.ShapeDtypeStruct((rows, model), jnp.bfloat16),
-        in_specs=[vmem],
+        in_specs=[vmem] * (devices // 4),
         out_specs=vmem,
         compiler_params=params,
         name="sum",
-    )(pieces)
+    )(sums[0], *got[::-1])
 
 
 def solution(mesh):

time: 34.3 us -> 33.1 us (0.965)
  blocking collectives: 13.5 us -> 0 us
  starting transfers between devices: 8.39 us -> 16.2 us
  waiting for transfers between devices: 2.1 us -> 6.52 us
    all_to_all x1 -> x0, blocking collectives: 13.5 us -> none  [body(): lax.all_to_all(summed, 'pool', 0, 0, tiled=True, axis_index_groups=groups)]
    ppermute x8 -> x14, starting transfers between devices: 8.39 us -> 16.2 us  [exchange(): return lax.ppermute(array, 'pool', [(d, d ^ mask) for d in range(devices)])]
    ppermute x8 -> x14, waiting for transfers between devices: 2.1 us -> 6.52 us  [exchange(): return lax.ppermute(array, 'pool', [(d, d ^ mask) for d in range(devices)])]
  transfers between devices with their start and end apart: 8 -> 14, of which waited for: 3 -> 5; matrix products, arithmetic and copies ran while one was open for 1% -> 1% of each run, Pallas kernels for 25% -> 27%
where the time goes in v5:
time: 33.1 us; the launch traced here: 32.9 us
  starting transfers between devices  16.2 us (49%)
  Pallas kernels  9.63 us (29%)
  waiting for transfers between devices  6.52 us (20%)
    ppermute x14, starting transfers between devices, exchange(): return lax.ppermute(array, 'pool', [(d, d ^ mask) for d in range(devices)])  16.2 us
    ppermute x14, waiting for transfers between devices, exchange(): return lax.ppermute(array, 'pool', [(d, d ^ mask) for d in range(devices)])  6.52 us
    pallas_call x2, Pallas kernels, load(): pl.pallas_call(functools.partial(load_kernel, [start for _, start, _ in p...  4.57 us
    pallas_call x1, Pallas kernels, body(): pl.pallas_call(functools.partial(base_kernel, rows), out_shape=[jax.Shape...  1.72 us
    pallas_call x1, Pallas kernels, body(): pl.pallas_call(functools.partial(shrink_kernel, rows), out_shape=jax.Shap...  1.3 us
    pallas_call x1, Pallas kernels, body(): pl.pallas_call(sum_kernel, out_shape=jax.ShapeDtypeStruct((rows, model),...  0.66 us
  transfers between devices with their start and end apart: 14, of which 5 were waited for; matrix products, arithmetic and copies ran while one was open for 1% of the time, Pallas kernels for 27%

profile of v5, /device:TPU:0, one launch (start us, length us, event | category | flops | bytes accessed | tf_op | source)
XLA Modules:
  0.0 32.9 jit_solution(12356634425955577898)
XLA Ops:
  0.0 0.5 %collective-permute-start.5 = (bf16[128,8192]{1,0:T(8,128)(2,1)}, bf16[128,8192]{1,0:T(8,128)(2,1)S(1)}, u32[]{:S(2)}, u32[]{:S(2)}) collective-permute-start(bf16[128,8192]{1,0:T(8,128)(2,1)} %down_ref), channel_id=1, source_target_pairs={{0,1},{1,0},{2,3},{3,2},{4,5},{5,4},{6,7},{7,6},{8,9},{9,8},{10,11... | collective-permute-start | bytes 6291464 | tf_op jit(solution)/shard_map/ppermute | solution.py:25
  0.5 0.1 collective-permute-start.6
  0.6 2.9 %collective-permute-start = (bf16[2,8192]{1,0:T(2,128)(2,1)}, bf16[2,8192]{1,0:T(2,128)(2,1)S(1)}, u32[]{:S(2)}, u32[]{:S(2)}) collective-permute-start(bf16[2,8192]{1,0:T(2,128)(2,1)} %refs_0_.1), channel_id=1, source_target_pairs={{0,2},{1,3},{2,0},{3,1},{4,6},{5,7},{6,4},{7,5},{8,10},{9,11},{10,... | collective-permute-start | bytes 98312 | tf_op jit(solution)/shard_map/ppermute | solution.py:25
  3.6 2.2 %load.2 = (bf16[2,8192]{1,0:T(2,128)(2,1)S(1)}, bf16[4096,512]{1,0:T(8,128)(2,1)S(1)}) custom-call(bf16[2,8192]{1,0:T(2,128)(2,1)} %refs_0_.1, bf16[8192,512]{1,0:T(8,128)(2,1)} %refs_0_.2), custom_call_target="tpu_custom_call" | custom-call | bytes 8454144 | tf_op jit(solution)/shard_map/load/pallas_call | solution.py:121
  5.8 0.0 collective-permute-done
  5.8 0.1 pad_maximum_fusion.1
  5.9 4.0 %collective-permute-start.1 = (bf16[4,8192]{1,0:T(4,128)(2,1)S(1)}, bf16[4,8192]{1,0:T(4,128)(2,1)S(1)}, u32[]{:S(2)}, u32[]{:S(2)}) collective-permute-start(bf16[4,8192]{1,0:T(4,128)(2,1)S(1)} %pad_maximum_fusion.1), channel_id=1, source_target_pairs={{0,12},{1,13},{2,14},{3,15},{4,8},{5,9},{6,10},{7,11},{8,4},{9,5},... | collective-permute-start | bytes 196616 | tf_op jit(solution)/shard_map/ppermute | solution.py:25
  9.9 0.6 %collective-permute-start.3 = (bf16[4,8192]{1,0:T(4,128)(2,1)S(1)}, bf16[4,8192]{1,0:T(4,128)(2,1)S(1)}, u32[]{:S(2)}, u32[]{:S(2)}) collective-permute-start(bf16[4,8192]{1,0:T(4,128)(2,1)S(1)} %pad_maximum_fusion.1), channel_id=1, source_target_pairs={{0,4},{1,5},{2,6},{3,7},{4,0},{5,1},{6,2},{7,3},{8,12},{9,13},{10,... | collective-permute-start | bytes 196616 | tf_op jit(solution)/shard_map/ppermute | solution.py:25
  10.6 0.6 %mask.1.mask_ref = f32[16,256]{1,0:T(8,128)S(1)} custom-call(s32[32]{0:T(128)S(1)} %bitcast.1, s32[16]{0:T(128)S(1)} %copy-done.3, s32[16]{0:T(128)S(1)} %copy-done.4), custom_call_target="tpu_custom_call" | custom-call | tf_op jit(solution)/shard_map/mask/pallas_call | solution.py:181
  11.2 0.0 copy-start
  11.2 2.3 %load.3.weight2_ref = bf16[4096,512]{1,0:T(8,128)(2,1)S(1)} custom-call(bf16[8192,512]{1,0:T(8,128)(2,1)} %refs_0_.2), custom_call_target="tpu_custom_call" | custom-call | bytes 8388608 | tf_op jit(solution)/shard_map/load/pallas_call | solution.py:121
  13.6 1.6 %collective-permute-done.2 = bf16[4,8192]{1,0:T(4,128)(2,1)S(1)} collective-permute-done((bf16[4,8192]{1,0:T(4,128)(2,1)S(1)}, bf16[4,8192]{1,0:T(4,128)(2,1)S(1)}, u32[]{:S(2)}, u32[]{:S(2)}) %collective-permute-start.2) | collective-permute-done | bytes 65568 | tf_op jit(solution)/shard_map/ppermute | solution.py:25
  15.2 0.1 collective-permute-done.3
  15.2 0.2 pad_maximum_fusion.near_ref
  15.4 0.0 copy-start.1
  15.4 0.1 collective-permute-start.4
  15.5 0.0 collective-permute-done.5.down2_ref
  15.5 1.3 %shrink.1.shrink_ref = bf16[16,256]{1,0:T(8,128)(2,1)S(1)} custom-call(f32[16,256]{1,0:T(8,128)S(1)} %mask.1.mask_ref, bf16[16,8192]{1,0:T(8,128)(2,1)S(1)} %pad_maximum_fusion.near_ref, bf16[128,8192]{1,0:T(8,128)(2,1)S(1)} %copy-done, bf16[128,8192]{1,0:T(8,128)(2,1)S(1)} %collective-permute-done.5.down2_ref), custom_call_target="tpu_custom_call" | custom-call | tf_op jit(solution)/shard_map/shrink/pallas_call | solution.py:204
  16.8 0.2 copy-done.1
  17.0 0.7 %delta.1 = (bf16[8,8192]{1,0:T(8,128)(2,1)S(1)}, bf16[8,8192]{1,0:T(8,128)(2,1)S(1)}) custom-call(bf16[16,256]{1,0:T(8,128)(2,1)S(1)} %shrink.1.shrink_ref, bf16[128,8192]{1,0:T(8,128)(2,1)S(1)} %copy-done.1, bf16[128,8192]{1,0:T(8,128)(2,1)S(1)} %collective-permute-done.6.up2_ref), custom_call_target="tpu_custom_call" | custom-call | tf_op jit(solution)/shard_map/delta/pallas_call | solution.py:212
  17.6 1.6 %collective-permute-start.7 = (bf16[8,8192]{1,0:T(8,128)(2,1)S(1)}, bf16[8,8192]{1,0:T(8,128)(2,1)S(1)}, u32[]{:S(2)}, u32[]{:S(2)}) collective-permute-start(bf16[8,8192]{1,0:T(8,128)(2,1)S(1)} %get-tuple-element.47), channel_id=1, source_target_pairs={{0,2},{1,3},{2,0},{3,1},{4,6},{5,7},{6,4},{7,5},{8,10},{9,11},{10,... | collective-permute-start | bytes 393224 | tf_op jit(solution)/shard_map/ppermute | solution.py:25
  19.2 1.7 %base.1 = (f32[8,512]{1,0:T(8,128)S(1)}, f32[8,512]{1,0:T(8,128)S(1)}, f32[8,512]{1,0:T(8,128)S(1)}, f32[8,512]{1,0:T(8,128)S(1)}) custom-call(bf16[16,8192]{1,0:T(8,128)(2,1)S(1)} %pad_maximum_fusion.near_ref, bf16[16,8192]{1,0:T(8,128)(2,1)S(1)} %collective-permute-done.4.far_ref, bf16[4096,512]{1,0:T(8,128)(2,1)S(1)} %get-tuple-element.49.weight_ref, ...), custom_call_target="tpu_custom_call" | custom-call | tf_op jit(solution)/shard_map/base/pallas_call | solution.py:222
  20.9 0.1 collective-permute-start.10
  21.0 0.5 %collective-permute-start.8 = (f32[8,512]{1,0:T(8,128)S(1)}, f32[8,512]{1,0:T(8,128)S(1)}, u32[]{:S(2)}, u32[]{:S(2)}) collective-permute-start(f32[8,512]{1,0:T(8,128)S(1)} %get-tuple-element.52), channel_id=1, source_target_pairs={{0,2},{1,3},{2,0},{3,1},{4,6},{5,7},{6,4},{7,5},{8,10},{9,11},{10,... | collective-permute-start | bytes 49160 | tf_op jit(solution)/shard_map/ppermute | solution.py:25
  21.5 1.3 %collective-permute-start.9 = (f32[8,512]{1,0:T(8,128)S(1)}, f32[8,512]{1,0:T(8,128)S(1)}, u32[]{:S(2)}, u32[]{:S(2)}) collective-permute-start(f32[8,512]{1,0:T(8,128)S(1)} %get-tuple-element.53), channel_id=1, source_target_pairs={{0,3},{1,2},{2,1},{3,0},{4,7},{5,6},{6,5},{7,4},{8,11},{9,10},{10,... | collective-permute-start | bytes 49160 | tf_op jit(solution)/shard_map/ppermute | solution.py:25
  22.8 2.0 %collective-permute-done.8.refs_1_ = f32[8,512]{1,0:T(8,128)S(1)} collective-permute-done((f32[8,512]{1,0:T(8,128)S(1)}, f32[8,512]{1,0:T(8,128)S(1)}, u32[]{:S(2)}, u32[]{:S(2)}) %collective-permute-start.8) | collective-permute-done | bytes 16416 | tf_op jit(solution)/shard_map/ppermute | solution.py:25
  24.8 0.1 add.1
  24.9 2.5 %collective-permute-start.11 = (bf16[2,8192]{1,0:T(2,128)(2,1)S(1)}, bf16[2,8192]{1,0:T(2,128)(2,1)S(1)}, u32[]{:S(2)}, u32[]{:S(2)}) collective-permute-start(bf16[2,8192]{1,0:T(2,128)(2,1)S(1)} %get-tuple-element.56), channel_id=1, source_target_pairs={{0,12},{1,13},{2,14},{3,15},{4,8},{5,9},{6,10},{7,11},{8,4},{9,5},... | collective-permute-start | bytes 98312 | tf_op jit(solution)/shard_map/ppermute | solution.py:25
  27.4 2.0 %collective-permute-start.13 = (bf16[2,8192]{1,0:T(2,128)(2,1)S(1)}, bf16[2,8192]{1,0:T(2,128)(2,1)S(1)}, u32[]{:S(2)}, u32[]{:S(2)}) collective-permute-start(bf16[2,8192]{1,0:T(2,128)(2,1)S(1)} %get-tuple-element.58), channel_id=1, source_target_pairs={{0,4},{1,5},{2,6},{3,7},{4,0},{5,1},{6,2},{7,3},{8,12},{9,13},{10,... | collective-permute-start | bytes 98312 | tf_op jit(solution)/shard_map/ppermute | solution.py:25
  29.4 1.5 %collective-permute-done.11.refs_1_ = bf16[2,8192]{1,0:T(2,128)(2,1)S(1)} collective-permute-done((bf16[2,8192]{1,0:T(2,128)(2,1)S(1)}, bf16[2,8192]{1,0:T(2,128)(2,1)S(1)}, u32[]{:S(2)}, u32[]{:S(2)}) %collective-permute-start.11) | collective-permute-done | bytes 32800 | tf_op jit(solution)/shard_map/ppermute | solution.py:25
  30.9 1.3 %collective-permute-done.12.refs_2_ = bf16[2,8192]{1,0:T(2,128)(2,1)S(1)} collective-permute-done((bf16[2,8192]{1,0:T(2,128)(2,1)S(1)}, bf16[2,8192]{1,0:T(2,128)(2,1)S(1)}, u32[]{:S(2)}, u32[]{:S(2)}) %collective-permute-start.12) | collective-permute-done | bytes 32800 | tf_op jit(solution)/shard_map/ppermute | solution.py:25
  32.2 0.7 %sum.1 = bf16[2,8192]{1,0:T(2,128)(2,1)} custom-call(bf16[2,8192]{1,0:T(2,128)(2,1)S(1)} %get-tuple-element.55.refs_0_, bf16[2,8192]{1,0:T(2,128)(2,1)S(1)} %collective-permute-done.11.refs_1_, bf16[2,8192]{1,0:T(2,128)(2,1)S(1)} %collective-permute-done.12.refs_2_, bf16[2,8192]{1,0:T(2,128)(2,1)S(1)} %collective-permute-done.13.refs_3_), custom_call_target="tpu_custom_call" | custom-call | tf_op jit(solution)/shard_map/sum/pallas_call | solution.py:240
  (16 shorter events, 0.0 us)
Async XLA Ops:
  0.0 10.5 %copy-start.2 = (s32[32,1]{0,1:T(1,128)S(1)}, s32[32,1]{0,1:T(1,128)}, u32[]{:S(2)}) copy-start(s32[32,1]{0,1:T(1,128)} %param.11) | copy-start | bytes 388
  0.0 10.5 %copy-start.3 = (s32[16]{0:T(128)S(1)}, s32[16]{0:T(128)}, u32[]{:S(2)}) copy-start(s32[16]{0:T(128)} %count_ref.1) | copy-start | bytes 196
  0.0 10.5 %copy-start.4 = (s32[16]{0:T(128)S(1)}, s32[16]{0:T(128)}, u32[]{:S(2)}) copy-start(s32[16]{0:T(128)} %slot_ref.1) | copy-start | bytes 196
  0.0 15.5 %collective-permute-start.5 = (bf16[128,8192]{1,0:T(8,128)(2,1)}, bf16[128,8192]{1,0:T(8,128)(2,1)S(1)}, u32[]{:S(2)}, u32[]{:S(2)}) collective-permute-start(bf16[128,8192]{1,0:T(8,128)(2,1)} %down_ref), channel_id=1, source_target_pairs={{0,1},{1,0},{2,3},{3,2},{4,5},{5,4},{6,7},{7,6},{8,9},{9,8},{10,11... | collective-permute-start | bytes 6291464 | tf_op jit(solution)/shard_map/ppermute | solution.py:25
  0.5 16.3 %collective-permute-start.6 = (bf16[128,8192]{1,0:T(8,128)(2,1)}, bf16[128,8192]{1,0:T(8,128)(2,1)S(1)}, u32[]{:S(2)}, u32[]{:S(2)}) collective-permute-start(bf16[128,8192]{1,0:T(8,128)(2,1)} %up_ref), channel_id=1, source_target_pairs={{0,1},{1,0},{2,3},{3,2},{4,5},{5,4},{6,7},{7,6},{8,9},{9,8},{10,11... | collective-permute-start | bytes 6291464 | tf_op jit(solution)/shard_map/ppermute | solution.py:25
  0.6 5.2 %collective-permute-start = (bf16[2,8192]{1,0:T(2,128)(2,1)}, bf16[2,8192]{1,0:T(2,128)(2,1)S(1)}, u32[]{:S(2)}, u32[]{:S(2)}) collective-permute-start(bf16[2,8192]{1,0:T(2,128)(2,1)} %refs_0_.1), channel_id=1, source_target_pairs={{0,2},{1,3},{2,0},{3,1},{4,6},{5,7},{6,4},{7,5},{8,10},{9,11},{10,... | collective-permute-start | bytes 98312 | tf_op jit(solution)/shard_map/ppermute | solution.py:25
  5.9 7.7 %collective-permute-start.1 = (bf16[4,8192]{1,0:T(4,128)(2,1)S(1)}, bf16[4,8192]{1,0:T(4,128)(2,1)S(1)}, u32[]{:S(2)}, u32[]{:S(2)}) collective-permute-start(bf16[4,8192]{1,0:T(4,128)(2,1)S(1)} %pad_maximum_fusion.1), channel_id=1, source_target_pairs={{0,12},{1,13},{2,14},{3,15},{4,8},{5,9},{6,10},{7,11},{8,4},{9,5},... | collective-permute-start | bytes 196616 | tf_op jit(solution)/shard_map/ppermute | solution.py:25
  9.9 5.3 %collective-permute-start.2 = (bf16[4,8192]{1,0:T(4,128)(2,1)S(1)}, bf16[4,8192]{1,0:T(4,128)(2,1)S(1)}, u32[]{:S(2)}, u32[]{:S(2)}) collective-permute-start(bf16[4,8192]{1,0:T(4,128)(2,1)S(1)} %pad_maximum_fusion.1), channel_id=1, source_target_pairs={{0,8},{1,9},{2,10},{3,11},{4,12},{5,13},{6,14},{7,15},{8,0},{9,1},... | collective-permute-start | bytes 196616 | tf_op jit(solution)/shard_map/ppermute | solution.py:25
  9.9 5.3 %collective-permute-start.3 = (bf16[4,8192]{1,0:T(4,128)(2,1)S(1)}, bf16[4,8192]{1,0:T(4,128)(2,1)S(1)}, u32[]{:S(2)}, u32[]{:S(2)}) collective-permute-start(bf16[4,8192]{1,0:T(4,128)(2,1)S(1)} %pad_maximum_fusion.1), channel_id=1, source_target_pairs={{0,4},{1,5},{2,6},{3,7},{4,0},{5,1},{6,2},{7,3},{8,12},{9,13},{10,... | collective-permute-start | bytes 196616 | tf_op jit(solution)/shard_map/ppermute | solution.py:25
  11.2 4.3 %copy-start = (bf16[128,8192]{1,0:T(8,128)(2,1)S(1)}, bf16[128,8192]{1,0:T(8,128)(2,1)}, u32[]{:S(2)}) copy-start(bf16[128,8192]{1,0:T(8,128)(2,1)} %down_ref) | copy-start | bytes 6291460
  15.4 1.6 %copy-start.1 = (bf16[128,8192]{1,0:T(8,128)(2,1)S(1)}, bf16[128,8192]{1,0:T(8,128)(2,1)}, u32[]{:S(2)}) copy-start(bf16[128,8192]{1,0:T(8,128)(2,1)} %up_ref) | copy-start | bytes 6291460
  15.4 3.8 %collective-permute-start.4 = (bf16[16,8192]{1,0:T(8,128)(2,1)S(1)}, bf16[16,8192]{1,0:T(8,128)(2,1)S(1)}, u32[]{:S(2)}, u32[]{:S(2)}) collective-permute-start(bf16[16,8192]{1,0:T(8,128)(2,1)S(1)} %pad_maximum_fusion.near_ref), channel_id=1, source_target_pairs={{0,1},{1,0},{2,3},{3,2},{4,5},{5,4},{6,7},{7,6},{8,9},{9,8},{10,11... | collective-permute-start | bytes 786440 | tf_op jit(solution)/shard_map/ppermute | solution.py:25
  17.6 7.2 %collective-permute-start.7 = (bf16[8,8192]{1,0:T(8,128)(2,1)S(1)}, bf16[8,8192]{1,0:T(8,128)(2,1)S(1)}, u32[]{:S(2)}, u32[]{:S(2)}) collective-permute-start(bf16[8,8192]{1,0:T(8,128)(2,1)S(1)} %get-tuple-element.47), channel_id=1, source_target_pairs={{0,2},{1,3},{2,0},{3,1},{4,6},{5,7},{6,4},{7,5},{8,10},{9,11},{10,... | collective-permute-start | bytes 393224 | tf_op jit(solution)/shard_map/ppermute | solution.py:25
  20.9 1.9 %collective-permute-start.10 = (f32[8,512]{1,0:T(8,128)S(1)}, f32[8,512]{1,0:T(8,128)S(1)}, u32[]{:S(2)}, u32[]{:S(2)}) collective-permute-start(f32[8,512]{1,0:T(8,128)S(1)} %get-tuple-element.54), channel_id=1, source_target_pairs={{0,1},{1,0},{2,3},{3,2},{4,5},{5,4},{6,7},{7,6},{8,9},{9,8},{10,11... | collective-permute-start | bytes 49160 | tf_op jit(solution)/shard_map/ppermute | solution.py:25
  21.0 3.8 %collective-permute-start.8 = (f32[8,512]{1,0:T(8,128)S(1)}, f32[8,512]{1,0:T(8,128)S(1)}, u32[]{:S(2)}, u32[]{:S(2)}) collective-permute-start(f32[8,512]{1,0:T(8,128)S(1)} %get-tuple-element.52), channel_id=1, source_target_pairs={{0,2},{1,3},{2,0},{3,1},{4,6},{5,7},{6,4},{7,5},{8,10},{9,11},{10,... | collective-permute-start | bytes 49160 | tf_op jit(solution)/shard_map/ppermute | solution.py:25
  21.5 3.3 %collective-permute-start.9 = (f32[8,512]{1,0:T(8,128)S(1)}, f32[8,512]{1,0:T(8,128)S(1)}, u32[]{:S(2)}, u32[]{:S(2)}) collective-permute-start(f32[8,512]{1,0:T(8,128)S(1)} %get-tuple-element.53), channel_id=1, source_target_pairs={{0,3},{1,2},{2,1},{3,0},{4,7},{5,6},{6,5},{7,4},{8,11},{9,10},{10,... | collective-permute-start | bytes 49160 | tf_op jit(solution)/shard_map/ppermute | solution.py:25
  24.9 6.0 %collective-permute-start.11 = (bf16[2,8192]{1,0:T(2,128)(2,1)S(1)}, bf16[2,8192]{1,0:T(2,128)(2,1)S(1)}, u32[]{:S(2)}, u32[]{:S(2)}) collective-permute-start(bf16[2,8192]{1,0:T(2,128)(2,1)S(1)} %get-tuple-element.56), channel_id=1, source_target_pairs={{0,12},{1,13},{2,14},{3,15},{4,8},{5,9},{6,10},{7,11},{8,4},{9,5},... | collective-permute-start | bytes 98312 | tf_op jit(solution)/shard_map/ppermute | solution.py:25
  27.4 4.8 %collective-permute-start.12 = (bf16[2,8192]{1,0:T(2,128)(2,1)S(1)}, bf16[2,8192]{1,0:T(2,128)(2,1)S(1)}, u32[]{:S(2)}, u32[]{:S(2)}) collective-permute-start(bf16[2,8192]{1,0:T(2,128)(2,1)S(1)} %get-tuple-element.57), channel_id=1, source_target_pairs={{0,8},{1,9},{2,10},{3,11},{4,12},{5,13},{6,14},{7,15},{8,0},{9,1},... | collective-permute-start | bytes 98312 | tf_op jit(solution)/shard_map/ppermute | solution.py:25
  27.4 4.8 %collective-permute-start.13 = (bf16[2,8192]{1,0:T(2,128)(2,1)S(1)}, bf16[2,8192]{1,0:T(2,128)(2,1)S(1)}, u32[]{:S(2)}, u32[]{:S(2)}) collective-permute-start(bf16[2,8192]{1,0:T(2,128)(2,1)S(1)} %get-tuple-element.58), channel_id=1, source_target_pairs={{0,4},{1,5},{2,6},{3,7},{4,0},{5,1},{6,2},{7,3},{8,12},{9,13},{10,... | collective-permute-start | bytes 98312 | tf_op jit(solution)/shard_map/ppermute | solution.py:25

commit v6 on v5

--- a/solution.py
+++ b/solution.py
@@ -25,10 +25,9 @@
     return lax.ppermute(array, "pool", [(d, d ^ mask) for d in range(devices)])
 
 
-def by_y(rows, half):
-    to = lax.broadcasted_iota(jnp.int32, (half, half), 0)
-    of = lax.broadcasted_iota(jnp.int32, (half, half), 1)
-    return of == to % (half // 2) // rows * 2 * rows + to // (half // 2) * rows + to % rows
+def by_y(rows, array):
+    blocks = [array[r : r + rows] for r in range(0, array.shape[0], rows)]
+    return jnp.concatenate(blocks[::2] + blocks[1::2], axis=0)
 
 
 def mask_kernel(rows, extent, ident_ref, count_ref, slot_ref, out_ref):
@@ -66,9 +65,7 @@
         ],
         axis=1,
     )
-    order = by_y(rows, near.shape[0]).astype(jnp.bfloat16)
-    shrink = jnp.dot(order, shrink.astype(jnp.bfloat16), preferred_element_type=jnp.float32)
-    out_ref[...] = jnp.where(mask_ref[...] > 0, shrink, 0.0).astype(jnp.bfloat16)
+    out_ref[...] = jnp.where(mask_ref[...] > 0, by_y(rows, shrink), 0.0).astype(jnp.bfloat16)
 
 
 def delta_kernel(shrink_ref, up_ref, up2_ref, own_out, other_out):
@@ -90,14 +87,8 @@
     x = jnp.concatenate([near_ref[...], far_ref[...]], axis=0)
     base = jnp.dot(x[:, :cut], weight_ref[...], preferred_element_type=jnp.float32)
     base += jnp.dot(x[:, cut:], weight2_ref[...], preferred_element_type=jnp.float32)
-    order = by_y(rows, 2 * part).astype(jnp.float32)
     for k in (0, 2):
-        placed = jnp.dot(
-            order,
-            base[k * part : (k + 2) * part],
-            preferred_element_type=jnp.float32,
-            precision=lax.Precision.HIGHEST,
-        )
+        placed = by_y(rows, base[k * part : (k + 2) * part])
         outs[k][...] = placed[:part]
         outs[k + 1][...] = placed[part:]
 

time: 33.1 us -> 32.9 us (level)
  transfers between devices with their start and end apart: 14 -> 14, of which waited for: 5 -> 5; matrix products, arithmetic and copies ran while one was open for 1% -> 1% of each run, Pallas kernels for 27% -> 26%
where the time goes in v6:
time: 32.9 us; the launch traced here: 32.8 us
  starting transfers between devices  16.2 us (49%)
  Pallas kernels  9.33 us (28%)
  waiting for transfers between devices  6.52 us (20%)
    ppermute x14, starting transfers between devices, exchange(): return lax.ppermute(array, 'pool', [(d, d ^ mask) for d in range(devices)])  16.2 us
    ppermute x14, waiting for transfers between devices, exchange(): return lax.ppermute(array, 'pool', [(d, d ^ mask) for d in range(devices)])  6.52 us
    pallas_call x2, Pallas kernels, load(): pl.pallas_call(functools.partial(load_kernel, [start for _, start, _ in p...  4.57 us
    pallas_call x1, Pallas kernels, body(): pl.pallas_call(functools.partial(base_kernel, rows), out_shape=[jax.Shape...  1.54 us
    pallas_call x1, Pallas kernels, body(): pl.pallas_call(functools.partial(shrink_kernel, rows), out_shape=jax.Shap...  1.19 us
    pallas_call x1, Pallas kernels, body(): pl.pallas_call(sum_kernel, out_shape=jax.ShapeDtypeStruct((rows, model),...  0.66 us
    pallas_call x1, Pallas kernels, body(): pl.pallas_call(delta_kernel, out_shape=[jax.ShapeDtypeStruct((half // 2,...  0.66 us
  transfers between devices with their start and end apart: 14, of which 5 were waited for; matrix products, arithmetic and copies ran while one was open for 1% of the time, Pallas kernels for 26%

profile of v6, /device:TPU:0, one launch (start us, length us, event | category | flops | bytes accessed | tf_op | source)
XLA Modules:
  0.0 32.8 jit_solution(10542129693166653926)
XLA Ops:
  0.0 0.5 %collective-permute-start.5 = (bf16[128,8192]{1,0:T(8,128)(2,1)}, bf16[128,8192]{1,0:T(8,128)(2,1)S(1)}, u32[]{:S(2)}, u32[]{:S(2)}) collective-permute-start(bf16[128,8192]{1,0:T(8,128)(2,1)} %down_ref), channel_id=1, source_target_pairs={{0,1},{1,0},{2,3},{3,2},{4,5},{5,4},{6,7},{7,6},{8,9},{9,8},{10,11... | collective-permute-start | bytes 6291464 | tf_op jit(solution)/shard_map/ppermute | solution.py:25
  0.5 0.1 collective-permute-start.6
  0.6 2.9 %collective-permute-start = (bf16[2,8192]{1,0:T(2,128)(2,1)}, bf16[2,8192]{1,0:T(2,128)(2,1)S(1)}, u32[]{:S(2)}, u32[]{:S(2)}) collective-permute-start(bf16[2,8192]{1,0:T(2,128)(2,1)} %refs_0_.1), channel_id=1, source_target_pairs={{0,2},{1,3},{2,0},{3,1},{4,6},{5,7},{6,4},{7,5},{8,10},{9,11},{10,... | collective-permute-start | bytes 98312 | tf_op jit(solution)/shard_map/ppermute | solution.py:25
  3.6 2.2 %load.2 = (bf16[2,8192]{1,0:T(2,128)(2,1)S(1)}, bf16[4096,512]{1,0:T(8,128)(2,1)S(1)}) custom-call(bf16[2,8192]{1,0:T(2,128)(2,1)} %refs_0_.1, bf16[8192,512]{1,0:T(8,128)(2,1)} %refs_0_.2), custom_call_target="tpu_custom_call" | custom-call | bytes 8454144 | tf_op jit(solution)/shard_map/load/pallas_call | solution.py:112
  5.8 0.1 pad_maximum_fusion.1
  5.9 4.0 %collective-permute-start.1 = (bf16[4,8192]{1,0:T(4,128)(2,1)S(1)}, bf16[4,8192]{1,0:T(4,128)(2,1)S(1)}, u32[]{:S(2)}, u32[]{:S(2)}) collective-permute-start(bf16[4,8192]{1,0:T(4,128)(2,1)S(1)} %pad_maximum_fusion.1), channel_id=1, source_target_pairs={{0,12},{1,13},{2,14},{3,15},{4,8},{5,9},{6,10},{7,11},{8,4},{9,5},... | collective-permute-start | bytes 196616 | tf_op jit(solution)/shard_map/ppermute | solution.py:25
  9.9 0.0 collective-permute-start.2
  9.9 0.6 %collective-permute-start.3 = (bf16[4,8192]{1,0:T(4,128)(2,1)S(1)}, bf16[4,8192]{1,0:T(4,128)(2,1)S(1)}, u32[]{:S(2)}, u32[]{:S(2)}) collective-permute-start(bf16[4,8192]{1,0:T(4,128)(2,1)S(1)} %pad_maximum_fusion.1), channel_id=1, source_target_pairs={{0,4},{1,5},{2,6},{3,7},{4,0},{5,1},{6,2},{7,3},{8,12},{9,13},{10,... | collective-permute-start | bytes 196616 | tf_op jit(solution)/shard_map/ppermute | solution.py:25
  10.6 0.6 %mask.1.mask_ref = f32[16,256]{1,0:T(8,128)S(1)} custom-call(s32[32]{0:T(128)S(1)} %bitcast.1, s32[16]{0:T(128)S(1)} %copy-done.3, s32[16]{0:T(128)S(1)} %copy-done.4), custom_call_target="tpu_custom_call" | custom-call | tf_op jit(solution)/shard_map/mask/pallas_call | solution.py:172
  11.2 0.0 copy-start
  11.2 2.3 %load.3.weight2_ref = bf16[4096,512]{1,0:T(8,128)(2,1)S(1)} custom-call(bf16[8192,512]{1,0:T(8,128)(2,1)} %refs_0_.2), custom_call_target="tpu_custom_call" | custom-call | bytes 8388608 | tf_op jit(solution)/shard_map/load/pallas_call | solution.py:112
  13.6 0.0 collective-permute-done.1
  13.6 1.6 %collective-permute-done.2 = bf16[4,8192]{1,0:T(4,128)(2,1)S(1)} collective-permute-done((bf16[4,8192]{1,0:T(4,128)(2,1)S(1)}, bf16[4,8192]{1,0:T(4,128)(2,1)S(1)}, u32[]{:S(2)}, u32[]{:S(2)}) %collective-permute-start.2) | collective-permute-done | bytes 65568 | tf_op jit(solution)/shard_map/ppermute | solution.py:25
  15.2 0.1 collective-permute-done.3
  15.2 0.2 pad_maximum_fusion.near_ref
  15.4 0.0 copy-start.1
  15.4 0.1 collective-permute-start.4
  15.5 1.2 %shrink.1.shrink_ref = bf16[16,256]{1,0:T(8,128)(2,1)S(1)} custom-call(f32[16,256]{1,0:T(8,128)S(1)} %mask.1.mask_ref, bf16[16,8192]{1,0:T(8,128)(2,1)S(1)} %pad_maximum_fusion.near_ref, bf16[128,8192]{1,0:T(8,128)(2,1)S(1)} %copy-done, bf16[128,8192]{1,0:T(8,128)(2,1)S(1)} %collective-permute-done.5.down2_ref), custom_call_target="tpu_custom_call" | custom-call | tf_op jit(solution)/shard_map/shrink/pallas_call | solution.py:195
  16.7 0.3 copy-done.1
  17.0 0.7 %delta.1 = (bf16[8,8192]{1,0:T(8,128)(2,1)S(1)}, bf16[8,8192]{1,0:T(8,128)(2,1)S(1)}) custom-call(bf16[16,256]{1,0:T(8,128)(2,1)S(1)} %shrink.1.shrink_ref, bf16[128,8192]{1,0:T(8,128)(2,1)S(1)} %copy-done.1, bf16[128,8192]{1,0:T(8,128)(2,1)S(1)} %collective-permute-done.6.up2_ref), custom_call_target="tpu_custom_call" | custom-call | tf_op jit(solution)/shard_map/delta/pallas_call | solution.py:203
  17.6 1.6 %collective-permute-start.7 = (bf16[8,8192]{1,0:T(8,128)(2,1)S(1)}, bf16[8,8192]{1,0:T(8,128)(2,1)S(1)}, u32[]{:S(2)}, u32[]{:S(2)}) collective-permute-start(bf16[8,8192]{1,0:T(8,128)(2,1)S(1)} %get-tuple-element.47), channel_id=1, source_target_pairs={{0,2},{1,3},{2,0},{3,1},{4,6},{5,7},{6,4},{7,5},{8,10},{9,11},{10,... | collective-permute-start | bytes 393224 | tf_op jit(solution)/shard_map/ppermute | solution.py:25
  19.2 1.5 %base.1 = (f32[8,512]{1,0:T(8,128)S(1)}, f32[8,512]{1,0:T(8,128)S(1)}, f32[8,512]{1,0:T(8,128)S(1)}, f32[8,512]{1,0:T(8,128)S(1)}) custom-call(bf16[16,8192]{1,0:T(8,128)(2,1)S(1)} %pad_maximum_fusion.near_ref, bf16[16,8192]{1,0:T(8,128)(2,1)S(1)} %collective-permute-done.4.far_ref, bf16[4096,512]{1,0:T(8,128)(2,1)S(1)} %get-tuple-element.49.weight_ref, ...), custom_call_target="tpu_custom_call" | custom-call | tf_op jit(solution)/shard_map/base/pallas_call | solution.py:213
  20.8 0.1 collective-permute-start.10
  20.8 0.5 %collective-permute-start.8 = (f32[8,512]{1,0:T(8,128)S(1)}, f32[8,512]{1,0:T(8,128)S(1)}, u32[]{:S(2)}, u32[]{:S(2)}) collective-permute-start(f32[8,512]{1,0:T(8,128)S(1)} %get-tuple-element.52), channel_id=1, source_target_pairs={{0,2},{1,3},{2,0},{3,1},{4,6},{5,7},{6,4},{7,5},{8,10},{9,11},{10,... | collective-permute-start | bytes 49160 | tf_op jit(solution)/shard_map/ppermute | solution.py:25
  21.4 1.3 %collective-permute-start.9 = (f32[8,512]{1,0:T(8,128)S(1)}, f32[8,512]{1,0:T(8,128)S(1)}, u32[]{:S(2)}, u32[]{:S(2)}) collective-permute-start(f32[8,512]{1,0:T(8,128)S(1)} %get-tuple-element.53), channel_id=1, source_target_pairs={{0,3},{1,2},{2,1},{3,0},{4,7},{5,6},{6,5},{7,4},{8,11},{9,10},{10,... | collective-permute-start | bytes 49160 | tf_op jit(solution)/shard_map/ppermute | solution.py:25
  22.7 2.0 %collective-permute-done.8.refs_1_ = f32[8,512]{1,0:T(8,128)S(1)} collective-permute-done((f32[8,512]{1,0:T(8,128)S(1)}, f32[8,512]{1,0:T(8,128)S(1)}, u32[]{:S(2)}, u32[]{:S(2)}) %collective-permute-start.8) | collective-permute-done | bytes 16416 | tf_op jit(solution)/shard_map/ppermute | solution.py:25
  24.7 0.1 add.1
  24.8 2.5 %collective-permute-start.11 = (bf16[2,8192]{1,0:T(2,128)(2,1)S(1)}, bf16[2,8192]{1,0:T(2,128)(2,1)S(1)}, u32[]{:S(2)}, u32[]{:S(2)}) collective-permute-start(bf16[2,8192]{1,0:T(2,128)(2,1)S(1)} %get-tuple-element.56), channel_id=1, source_target_pairs={{0,12},{1,13},{2,14},{3,15},{4,8},{5,9},{6,10},{7,11},{8,4},{9,5},... | collective-permute-start | bytes 98312 | tf_op jit(solution)/shard_map/ppermute | solution.py:25
  27.3 2.0 %collective-permute-start.13 = (bf16[2,8192]{1,0:T(2,128)(2,1)S(1)}, bf16[2,8192]{1,0:T(2,128)(2,1)S(1)}, u32[]{:S(2)}, u32[]{:S(2)}) collective-permute-start(bf16[2,8192]{1,0:T(2,128)(2,1)S(1)} %get-tuple-element.58), channel_id=1, source_target_pairs={{0,4},{1,5},{2,6},{3,7},{4,0},{5,1},{6,2},{7,3},{8,12},{9,13},{10,... | collective-permute-start | bytes 98312 | tf_op jit(solution)/shard_map/ppermute | solution.py:25
  29.3 1.5 %collective-permute-done.11.refs_1_ = bf16[2,8192]{1,0:T(2,128)(2,1)S(1)} collective-permute-done((bf16[2,8192]{1,0:T(2,128)(2,1)S(1)}, bf16[2,8192]{1,0:T(2,128)(2,1)S(1)}, u32[]{:S(2)}, u32[]{:S(2)}) %collective-permute-start.11) | collective-permute-done | bytes 32800 | tf_op jit(solution)/shard_map/ppermute | solution.py:25
  30.8 1.3 %collective-permute-done.12.refs_2_ = bf16[2,8192]{1,0:T(2,128)(2,1)S(1)} collective-permute-done((bf16[2,8192]{1,0:T(2,128)(2,1)S(1)}, bf16[2,8192]{1,0:T(2,128)(2,1)S(1)}, u32[]{:S(2)}, u32[]{:S(2)}) %collective-permute-start.12) | collective-permute-done | bytes 32800 | tf_op jit(solution)/shard_map/ppermute | solution.py:25
  32.1 0.7 %sum.1 = bf16[2,8192]{1,0:T(2,128)(2,1)} custom-call(bf16[2,8192]{1,0:T(2,128)(2,1)S(1)} %get-tuple-element.55.refs_0_, bf16[2,8192]{1,0:T(2,128)(2,1)S(1)} %collective-permute-done.11.refs_1_, bf16[2,8192]{1,0:T(2,128)(2,1)S(1)} %collective-permute-done.12.refs_2_, bf16[2,8192]{1,0:T(2,128)(2,1)S(1)} %collective-permute-done.13.refs_3_), custom_call_target="tpu_custom_call" | custom-call | tf_op jit(solution)/shard_map/sum/pallas_call | solution.py:231
  (16 shorter events, 0.0 us)
Async XLA Ops:
  0.0 10.5 %copy-start.2 = (s32[32,1]{0,1:T(1,128)S(1)}, s32[32,1]{0,1:T(1,128)}, u32[]{:S(2)}) copy-start(s32[32,1]{0,1:T(1,128)} %param.11) | copy-start | bytes 388
  0.0 10.5 %copy-start.3 = (s32[16]{0:T(128)S(1)}, s32[16]{0:T(128)}, u32[]{:S(2)}) copy-start(s32[16]{0:T(128)} %count_ref.1) | copy-start | bytes 196
  0.0 10.5 %copy-start.4 = (s32[16]{0:T(128)S(1)}, s32[16]{0:T(128)}, u32[]{:S(2)}) copy-start(s32[16]{0:T(128)} %slot_ref.1) | copy-start | bytes 196
  0.0 15.5 %collective-permute-start.5 = (bf16[128,8192]{1,0:T(8,128)(2,1)}, bf16[128,8192]{1,0:T(8,128)(2,1)S(1)}, u32[]{:S(2)}, u32[]{:S(2)}) collective-permute-start(bf16[128,8192]{1,0:T(8,128)(2,1)} %down_ref), channel_id=1, source_target_pairs={{0,1},{1,0},{2,3},{3,2},{4,5},{5,4},{6,7},{7,6},{8,9},{9,8},{10,11... | collective-permute-start | bytes 6291464 | tf_op jit(solution)/shard_map/ppermute | solution.py:25
  0.5 16.2 %collective-permute-start.6 = (bf16[128,8192]{1,0:T(8,128)(2,1)}, bf16[128,8192]{1,0:T(8,128)(2,1)S(1)}, u32[]{:S(2)}, u32[]{:S(2)}) collective-permute-start(bf16[128,8192]{1,0:T(8,128)(2,1)} %up_ref), channel_id=1, source_target_pairs={{0,1},{1,0},{2,3},{3,2},{4,5},{5,4},{6,7},{7,6},{8,9},{9,8},{10,11... | collective-permute-start | bytes 6291464 | tf_op jit(solution)/shard_map/ppermute | solution.py:25
  0.6 5.2 %collective-permute-start = (bf16[2,8192]{1,0:T(2,128)(2,1)}, bf16[2,8192]{1,0:T(2,128)(2,1)S(1)}, u32[]{:S(2)}, u32[]{:S(2)}) collective-permute-start(bf16[2,8192]{1,0:T(2,128)(2,1)} %refs_0_.1), channel_id=1, source_target_pairs={{0,2},{1,3},{2,0},{3,1},{4,6},{5,7},{6,4},{7,5},{8,10},{9,11},{10,... | collective-permute-start | bytes 98312 | tf_op jit(solution)/shard_map/ppermute | solution.py:25
  5.9 7.7 %collective-permute-start.1 = (bf16[4,8192]{1,0:T(4,128)(2,1)S(1)}, bf16[4,8192]{1,0:T(4,128)(2,1)S(1)}, u32[]{:S(2)}, u32[]{:S(2)}) collective-permute-start(bf16[4,8192]{1,0:T(4,128)(2,1)S(1)} %pad_maximum_fusion.1), channel_id=1, source_target_pairs={{0,12},{1,13},{2,14},{3,15},{4,8},{5,9},{6,10},{7,11},{8,4},{9,5},... | collective-permute-start | bytes 196616 | tf_op jit(solution)/shard_map/ppermute | solution.py:25
  9.9 5.3 %collective-permute-start.2 = (bf16[4,8192]{1,0:T(4,128)(2,1)S(1)}, bf16[4,8192]{1,0:T(4,128)(2,1)S(1)}, u32[]{:S(2)}, u32[]{:S(2)}) collective-permute-start(bf16[4,8192]{1,0:T(4,128)(2,1)S(1)} %pad_maximum_fusion.1), channel_id=1, source_target_pairs={{0,8},{1,9},{2,10},{3,11},{4,12},{5,13},{6,14},{7,15},{8,0},{9,1},... | collective-permute-start | bytes 196616 | tf_op jit(solution)/shard_map/ppermute | solution.py:25
  9.9 5.3 %collective-permute-start.3 = (bf16[4,8192]{1,0:T(4,128)(2,1)S(1)}, bf16[4,8192]{1,0:T(4,128)(2,1)S(1)}, u32[]{:S(2)}, u32[]{:S(2)}) collective-permute-start(bf16[4,8192]{1,0:T(4,128)(2,1)S(1)} %pad_maximum_fusion.1), channel_id=1, source_target_pairs={{0,4},{1,5},{2,6},{3,7},{4,0},{5,1},{6,2},{7,3},{8,12},{9,13},{10,... | collective-permute-start | bytes 196616 | tf_op jit(solution)/shard_map/ppermute | solution.py:25
  11.2 4.3 %copy-start = (bf16[128,8192]{1,0:T(8,128)(2,1)S(1)}, bf16[128,8192]{1,0:T(8,128)(2,1)}, u32[]{:S(2)}) copy-start(bf16[128,8192]{1,0:T(8,128)(2,1)} %down_ref) | copy-start | bytes 6291460
  15.4 1.6 %copy-start.1 = (bf16[128,8192]{1,0:T(8,128)(2,1)S(1)}, bf16[128,8192]{1,0:T(8,128)(2,1)}, u32[]{:S(2)}) copy-start(bf16[128,8192]{1,0:T(8,128)(2,1)} %up_ref) | copy-start | bytes 6291460
  15.4 3.8 %collective-permute-start.4 = (bf16[16,8192]{1,0:T(8,128)(2,1)S(1)}, bf16[16,8192]{1,0:T(8,128)(2,1)S(1)}, u32[]{:S(2)}, u32[]{:S(2)}) collective-permute-start(bf16[16,8192]{1,0:T(8,128)(2,1)S(1)} %pad_maximum_fusion.near_ref), channel_id=1, source_target_pairs={{0,1},{1,0},{2,3},{3,2},{4,5},{5,4},{6,7},{7,6},{8,9},{9,8},{10,11... | collective-permute-start | bytes 786440 | tf_op jit(solution)/shard_map/ppermute | solution.py:25
  17.6 7.1 %collective-permute-start.7 = (bf16[8,8192]{1,0:T(8,128)(2,1)S(1)}, bf16[8,8192]{1,0:T(8,128)(2,1)S(1)}, u32[]{:S(2)}, u32[]{:S(2)}) collective-permute-start(bf16[8,8192]{1,0:T(8,128)(2,1)S(1)} %get-tuple-element.47), channel_id=1, source_target_pairs={{0,2},{1,3},{2,0},{3,1},{4,6},{5,7},{6,4},{7,5},{8,10},{9,11},{10,... | collective-permute-start | bytes 393224 | tf_op jit(solution)/shard_map/ppermute | solution.py:25
  20.8 1.9 %collective-permute-start.10 = (f32[8,512]{1,0:T(8,128)S(1)}, f32[8,512]{1,0:T(8,128)S(1)}, u32[]{:S(2)}, u32[]{:S(2)}) collective-permute-start(f32[8,512]{1,0:T(8,128)S(1)} %get-tuple-element.54), channel_id=1, source_target_pairs={{0,1},{1,0},{2,3},{3,2},{4,5},{5,4},{6,7},{7,6},{8,9},{9,8},{10,11... | collective-permute-start | bytes 49160 | tf_op jit(solution)/shard_map/ppermute | solution.py:25
  20.8 3.9 %collective-permute-start.8 = (f32[8,512]{1,0:T(8,128)S(1)}, f32[8,512]{1,0:T(8,128)S(1)}, u32[]{:S(2)}, u32[]{:S(2)}) collective-permute-start(f32[8,512]{1,0:T(8,128)S(1)} %get-tuple-element.52), channel_id=1, source_target_pairs={{0,2},{1,3},{2,0},{3,1},{4,6},{5,7},{6,4},{7,5},{8,10},{9,11},{10,... | collective-permute-start | bytes 49160 | tf_op jit(solution)/shard_map/ppermute | solution.py:25
  21.4 3.3 %collective-permute-start.9 = (f32[8,512]{1,0:T(8,128)S(1)}, f32[8,512]{1,0:T(8,128)S(1)}, u32[]{:S(2)}, u32[]{:S(2)}) collective-permute-start(f32[8,512]{1,0:T(8,128)S(1)} %get-tuple-element.53), channel_id=1, source_target_pairs={{0,3},{1,2},{2,1},{3,0},{4,7},{5,6},{6,5},{7,4},{8,11},{9,10},{10,... | collective-permute-start | bytes 49160 | tf_op jit(solution)/shard_map/ppermute | solution.py:25
  24.8 6.0 %collective-permute-start.11 = (bf16[2,8192]{1,0:T(2,128)(2,1)S(1)}, bf16[2,8192]{1,0:T(2,128)(2,1)S(1)}, u32[]{:S(2)}, u32[]{:S(2)}) collective-permute-start(bf16[2,8192]{1,0:T(2,128)(2,1)S(1)} %get-tuple-element.56), channel_id=1, source_target_pairs={{0,12},{1,13},{2,14},{3,15},{4,8},{5,9},{6,10},{7,11},{8,4},{9,5},... | collective-permute-start | bytes 98312 | tf_op jit(solution)/shard_map/ppermute | solution.py:25
  27.3 4.8 %collective-permute-start.12 = (bf16[2,8192]{1,0:T(2,128)(2,1)S(1)}, bf16[2,8192]{1,0:T(2,128)(2,1)S(1)}, u32[]{:S(2)}, u32[]{:S(2)}) collective-permute-start(bf16[2,8192]{1,0:T(2,128)(2,1)S(1)} %get-tuple-element.57), channel_id=1, source_target_pairs={{0,8},{1,9},{2,10},{3,11},{4,12},{5,13},{6,14},{7,15},{8,0},{9,1},... | collective-permute-start | bytes 98312 | tf_op jit(solution)/shard_map/ppermute | solution.py:25
  27.3 4.8 %collective-permute-start.13 = (bf16[2,8192]{1,0:T(2,128)(2,1)S(1)}, bf16[2,8192]{1,0:T(2,128)(2,1)S(1)}, u32[]{:S(2)}, u32[]{:S(2)}) collective-permute-start(bf16[2,8192]{1,0:T(2,128)(2,1)S(1)} %get-tuple-element.58), channel_id=1, source_target_pairs={{0,4},{1,5},{2,6},{3,7},{4,0},{5,1},{6,2},{7,3},{8,12},{9,13},{10,... | collective-permute-start | bytes 98312 | tf_op jit(solution)/shard_map/ppermute | solution.py:25

commit v7 on v6

--- a/solution.py
+++ b/solution.py
@@ -32,28 +32,21 @@
 
 def mask_kernel(rows, extent, ident_ref, count_ref, slot_ref, out_ref):
     half = out_ref.shape[0]
+    requests, adapters = ident_ref.shape[1], slot_ref.shape[1]
     device = lax.axis_index("pool")
-
-    def ranks(a, held):
-        slot, count = slot_ref[a], count_ref[a] * RANK_BLOCK
-        return jnp.where(slot == device, count, held[0]), jnp.where(slot == device ^ 1, count, held[1])
-
-    adapters = slot_ref.shape[0]
-    rank, rank2 = lax.fori_loop(
-        0, adapters, ranks, (jnp.int32(0), jnp.int32(0)), unroll=min(adapters, 16)
-    )
-    row = lax.broadcasted_iota(jnp.int32, out_ref.shape, 0)
-    col = lax.broadcasted_iota(jnp.int32, out_ref.shape, 1)
-
-    def limits(q, held):
-        chip = q % (half // 2) // rows * 2 + q // (half // 2)
-        request = (device ^ (2 * chip)) * rows + q % rows
-        slot = slot_ref[ident_ref[request]]
-        low = jnp.where(slot == device ^ 1, extent, 0)
-        high = jnp.where(slot == device, rank, jnp.where(slot == device ^ 1, extent + rank2, 0))
-        return jnp.where((row == q) & (col >= low) & (col < high), 1.0, held)
-
-    out_ref[...] = lax.fori_loop(0, half, limits, jnp.zeros(out_ref.shape, jnp.float32), unroll=min(half, 16))
+    slots, counts = slot_ref[...], count_ref[...]
+    rank = jnp.sum(jnp.where(slots == device, counts, 0), axis=1, keepdims=True) * RANK_BLOCK
+    rank2 = jnp.sum(jnp.where(slots == device ^ 1, counts, 0), axis=1, keepdims=True) * RANK_BLOCK
+    row = lax.broadcasted_iota(jnp.int32, (half, requests), 0)
+    chip = row % (half // 2) // rows * 2 + row // (half // 2)
+    request = (device ^ (2 * chip)) * rows + row % rows
+    picked = request == lax.broadcasted_iota(jnp.int32, (half, requests), 1)
+    ident = jnp.sum(jnp.where(picked, ident_ref[...], 0), axis=1, keepdims=True)
+    named = ident == lax.broadcasted_iota(jnp.int32, (half, adapters), 1)
+    slot = jnp.sum(jnp.where(named, slots, 0), axis=1, keepdims=True)
+    col = lax.broadcasted_iota(jnp.int32, (half, extent), 1)
+    out_ref[:, :extent] = jnp.where((slot == device) & (col < rank), 1.0, 0.0)
+    out_ref[:, extent:] = jnp.where((slot == device ^ 1) & (col < rank2), 1.0, 0.0)
 
 
 def shrink_kernel(rows, mask_ref, near_ref, down_ref, down2_ref, out_ref):
@@ -163,7 +156,7 @@
     devices = lax.axis_size("pool")
     rows, model = tokens.shape
     half = devices // 2 * rows
-    vmem, smem = pl.BlockSpec(memory_space=pltpu.VMEM), pl.BlockSpec(memory_space=pltpu.SMEM)
+    vmem = pl.BlockSpec(memory_space=pltpu.VMEM)
     params = pltpu.CompilerParams(vmem_limit_bytes=8 * 1024 * 1024)
 
     down2 = exchange(adapter_down_weight, 1, devices)
@@ -172,18 +165,18 @@
     mask = pl.pallas_call(
         functools.partial(mask_kernel, rows, extent),
         out_shape=jax.ShapeDtypeStruct((half, 2 * extent), jnp.float32),
-        in_specs=[smem] * 3,
+        in_specs=[vmem] * 3,
         out_specs=vmem,
         compiler_params=params,
         name="mask",
-    )(request_adapter[:, 0], adapter_block_count, adapter_store_slot)
+    )(request_adapter.reshape(1, -1), adapter_block_count[None], adapter_store_slot[None])
     weight, down, up = base_projection_weight, adapter_down_weight, adapter_up_weight
-    cut = model // 2
-    near, head = load((tokens, 0, rows), (weight, 0, cut))
+    cut = model // 4
+    near, head, up = load((tokens, 0, rows), (weight, 0, cut), (up, 0, extent))
     for k, stage in enumerate(stages_of(devices)):
         got = [exchange(near if k else tokens, m, devices) for m in stage]
         if k == 0:
-            near, head, got = lax.optimization_barrier((near, head, got))
+            near, head, up, got = lax.optimization_barrier((near, head, up, got))
         if k == 1:
             weight, down, up, near = lax.optimization_barrier((weight, down, up, near))
             (tail,) = load((weight, cut, model))

time: 32.9 us -> 32.8 us (level)
    pallas_call x2, Pallas kernels: 4.57 us -> 5.21 us  [load(): pl.pallas_call(functools.partial(load_kernel, [start for _, start, _ in p...]
    pallas_call x1, Pallas kernels: 0.64 us -> 0.18 us  [body(): pl.pallas_call(functools.partial(mask_kernel, rows, extent), out_shape=ja...]
  transfers between devices with their start and end apart: 14 -> 14, of which waited for: 5 -> 5; matrix products, arithmetic and copies ran while one was open for 1% -> 1% of each run, Pallas kernels for 26% -> 27%
where the time goes in v7:
time: 32.8 us; the launch traced here: 32.6 us
  starting transfers between devices  16.2 us (49%)
  Pallas kernels  9.5 us (29%)
  waiting for transfers between devices  6.63 us (20%)
    ppermute x14, starting transfers between devices, exchange(): return lax.ppermute(array, 'pool', [(d, d ^ mask) for d in range(devices)])  16.2 us
    ppermute x14, waiting for transfers between devices, exchange(): return lax.ppermute(array, 'pool', [(d, d ^ mask) for d in range(devices)])  6.63 us
    pallas_call x2, Pallas kernels, load(): pl.pallas_call(functools.partial(load_kernel, [start for _, start, _ in p...  5.21 us
    pallas_call x1, Pallas kernels, body(): pl.pallas_call(functools.partial(base_kernel, rows), out_shape=[jax.Shape...  1.54 us
    pallas_call x1, Pallas kernels, body(): pl.pallas_call(functools.partial(shrink_kernel, rows), out_shape=jax.Shap...  1.19 us
    pallas_call x1, Pallas kernels, body(): pl.pallas_call(sum_kernel, out_shape=jax.ShapeDtypeStruct((rows, model),...  0.66 us
  transfers between devices with their start and end apart: 14, of which 5 were waited for; matrix products, arithmetic and copies ran while one was open for 1% of the time, Pallas kernels for 27%

profile of v7, /device:TPU:0, one launch (start us, length us, event | category | flops | bytes accessed | tf_op | source)
XLA Modules:
  0.0 32.6 jit_solution(5104149903669849792)
XLA Ops:
  0.0 0.5 %collective-permute-start.5 = (bf16[128,8192]{1,0:T(8,128)(2,1)}, bf16[128,8192]{1,0:T(8,128)(2,1)S(1)}, u32[]{:S(2)}, u32[]{:S(2)}) collective-permute-start(bf16[128,8192]{1,0:T(8,128)(2,1)} %down_ref), channel_id=1, source_target_pairs={{0,1},{1,0},{2,3},{3,2},{4,5},{5,4},{6,7},{7,6},{8,9},{9,8},{10,11... | collective-permute-start | bytes 6291464 | tf_op jit(solution)/shard_map/ppermute | solution.py:25
  0.5 0.1 collective-permute-start.6
  0.6 2.9 %collective-permute-start = (bf16[2,8192]{1,0:T(2,128)(2,1)}, bf16[2,8192]{1,0:T(2,128)(2,1)S(1)}, u32[]{:S(2)}, u32[]{:S(2)}) collective-permute-start(bf16[2,8192]{1,0:T(2,128)(2,1)} %refs_0_.1), channel_id=1, source_target_pairs={{0,2},{1,3},{2,0},{3,1},{4,6},{5,7},{6,4},{7,5},{8,10},{9,11},{10,... | collective-permute-start | bytes 98312 | tf_op jit(solution)/shard_map/ppermute | solution.py:25
  3.6 2.3 %load.2 = (bf16[2,8192]{1,0:T(2,128)(2,1)S(1)}, bf16[2048,512]{1,0:T(8,128)(2,1)S(1)}, bf16[128,8192]{1,0:T(8,128)(2,1)S(1)}) custom-call(bf16[2,8192]{1,0:T(2,128)(2,1)} %refs_0_.1, bf16[8192,512]{1,0:T(8,128)(2,1)} %refs_0_.2, bf16[128,8192]{1,0:T(8,128)(2,1)} %refs_2_.1), custom_call_target="tpu_custom_call" | custom-call | bytes 8454144 | tf_op jit(solution)/shard_map/load/pallas_call | solution.py:105
  5.8 0.0 collective-permute-done
  5.8 0.1 pad_maximum_fusion.1
  5.9 4.0 %collective-permute-start.1 = (bf16[4,8192]{1,0:T(4,128)(2,1)S(1)}, bf16[4,8192]{1,0:T(4,128)(2,1)S(1)}, u32[]{:S(2)}, u32[]{:S(2)}) collective-permute-start(bf16[4,8192]{1,0:T(4,128)(2,1)S(1)} %pad_maximum_fusion.1), channel_id=1, source_target_pairs={{0,12},{1,13},{2,14},{3,15},{4,8},{5,9},{6,10},{7,11},{8,4},{9,5},... | collective-permute-start | bytes 196616 | tf_op jit(solution)/shard_map/ppermute | solution.py:25
  9.9 0.6 %collective-permute-start.3 = (bf16[4,8192]{1,0:T(4,128)(2,1)S(1)}, bf16[4,8192]{1,0:T(4,128)(2,1)S(1)}, u32[]{:S(2)}, u32[]{:S(2)}) collective-permute-start(bf16[4,8192]{1,0:T(4,128)(2,1)S(1)} %pad_maximum_fusion.1), channel_id=1, source_target_pairs={{0,4},{1,5},{2,6},{3,7},{4,0},{5,1},{6,2},{7,3},{8,12},{9,13},{10,... | collective-permute-start | bytes 196616 | tf_op jit(solution)/shard_map/ppermute | solution.py:25
  10.6 0.2 mask.1.mask_ref
  10.7 2.9 %load.3.weight2_ref = bf16[6144,512]{1,0:T(8,128)(2,1)S(1)} custom-call(bf16[8192,512]{1,0:T(8,128)(2,1)} %refs_0_.2), custom_call_target="tpu_custom_call" | custom-call | bytes 12582912 | tf_op jit(solution)/shard_map/load/pallas_call | solution.py:105
  13.7 0.0 collective-permute-done.1
  13.7 1.5 %collective-permute-done.2 = bf16[4,8192]{1,0:T(4,128)(2,1)S(1)} collective-permute-done((bf16[4,8192]{1,0:T(4,128)(2,1)S(1)}, bf16[4,8192]{1,0:T(4,128)(2,1)S(1)}, u32[]{:S(2)}, u32[]{:S(2)}) %collective-permute-start.2) | collective-permute-done | bytes 65568 | tf_op jit(solution)/shard_map/ppermute | solution.py:25
  15.2 0.1 collective-permute-done.3
  15.3 0.2 pad_maximum_fusion.near_ref
  15.4 0.1 collective-permute-start.4
  15.5 0.0 collective-permute-done.5.down2_ref
  15.5 1.2 %shrink.1.shrink_ref = bf16[16,256]{1,0:T(8,128)(2,1)S(1)} custom-call(f32[16,256]{1,0:T(8,128)S(1)} %mask.1.mask_ref, bf16[16,8192]{1,0:T(8,128)(2,1)S(1)} %pad_maximum_fusion.near_ref, bf16[128,8192]{1,0:T(8,128)(2,1)S(1)} %copy-done, bf16[128,8192]{1,0:T(8,128)(2,1)S(1)} %collective-permute-done.5.down2_ref), custom_call_target="tpu_custom_call" | custom-call | tf_op jit(solution)/shard_map/shrink/pallas_call | solution.py:188
  16.7 0.7 %delta.1 = (bf16[8,8192]{1,0:T(8,128)(2,1)S(1)}, bf16[8,8192]{1,0:T(8,128)(2,1)S(1)}) custom-call(bf16[16,256]{1,0:T(8,128)(2,1)S(1)} %shrink.1.shrink_ref, bf16[128,8192]{1,0:T(8,128)(2,1)S(1)} %get-tuple-element.48.up_ref, bf16[128,8192]{1,0:T(8,128)(2,1)S(1)} %collective-permute-done.6.up2_ref), custom_call_target="tpu_custom_call" | custom-call | tf_op jit(solution)/shard_map/delta/pallas_call | solution.py:196
  17.4 1.5 %collective-permute-start.7 = (bf16[8,8192]{1,0:T(8,128)(2,1)S(1)}, bf16[8,8192]{1,0:T(8,128)(2,1)S(1)}, u32[]{:S(2)}, u32[]{:S(2)}) collective-permute-start(bf16[8,8192]{1,0:T(8,128)(2,1)S(1)} %get-tuple-element.51), channel_id=1, source_target_pairs={{0,2},{1,3},{2,0},{3,1},{4,6},{5,7},{6,4},{7,5},{8,10},{9,11},{10,... | collective-permute-start | bytes 393224 | tf_op jit(solution)/shard_map/ppermute | solution.py:25
  18.9 0.0 collective-permute-done.4.far_ref
  18.9 1.5 %base.1 = (f32[8,512]{1,0:T(8,128)S(1)}, f32[8,512]{1,0:T(8,128)S(1)}, f32[8,512]{1,0:T(8,128)S(1)}, f32[8,512]{1,0:T(8,128)S(1)}) custom-call(bf16[16,8192]{1,0:T(8,128)(2,1)S(1)} %pad_maximum_fusion.near_ref, bf16[16,8192]{1,0:T(8,128)(2,1)S(1)} %collective-permute-done.4.far_ref, bf16[2048,512]{1,0:T(8,128)(2,1)S(1)} %get-tuple-element.53.weight_ref, ...), custom_call_target="tpu_custom_call" | custom-call | tf_op jit(solution)/shard_map/base/pallas_call | solution.py:206
  20.5 0.3 collective-permute-start.10
  20.7 0.5 %collective-permute-start.8 = (f32[8,512]{1,0:T(8,128)S(1)}, f32[8,512]{1,0:T(8,128)S(1)}, u32[]{:S(2)}, u32[]{:S(2)}) collective-permute-start(f32[8,512]{1,0:T(8,128)S(1)} %get-tuple-element.56), channel_id=1, source_target_pairs={{0,2},{1,3},{2,0},{3,1},{4,6},{5,7},{6,4},{7,5},{8,10},{9,11},{10,... | collective-permute-start | bytes 49160 | tf_op jit(solution)/shard_map/ppermute | solution.py:25
  21.2 1.2 %collective-permute-start.9 = (f32[8,512]{1,0:T(8,128)S(1)}, f32[8,512]{1,0:T(8,128)S(1)}, u32[]{:S(2)}, u32[]{:S(2)}) collective-permute-start(f32[8,512]{1,0:T(8,128)S(1)} %get-tuple-element.57), channel_id=1, source_target_pairs={{0,3},{1,2},{2,1},{3,0},{4,7},{5,6},{6,5},{7,4},{8,11},{9,10},{10,... | collective-permute-start | bytes 49160 | tf_op jit(solution)/shard_map/ppermute | solution.py:25
  22.4 2.2 %collective-permute-done.8.refs_1_ = f32[8,512]{1,0:T(8,128)S(1)} collective-permute-done((f32[8,512]{1,0:T(8,128)S(1)}, f32[8,512]{1,0:T(8,128)S(1)}, u32[]{:S(2)}, u32[]{:S(2)}) %collective-permute-start.8) | collective-permute-done | bytes 16416 | tf_op jit(solution)/shard_map/ppermute | solution.py:25
  24.6 0.0 collective-permute-done.9.refs_2_
  24.6 0.1 add.1
  24.7 2.5 %collective-permute-start.11 = (bf16[2,8192]{1,0:T(2,128)(2,1)S(1)}, bf16[2,8192]{1,0:T(2,128)(2,1)S(1)}, u32[]{:S(2)}, u32[]{:S(2)}) collective-permute-start(bf16[2,8192]{1,0:T(2,128)(2,1)S(1)} %get-tuple-element.60), channel_id=1, source_target_pairs={{0,12},{1,13},{2,14},{3,15},{4,8},{5,9},{6,10},{7,11},{8,4},{9,5},... | collective-permute-start | bytes 98312 | tf_op jit(solution)/shard_map/ppermute | solution.py:25
  27.2 2.0 %collective-permute-start.13 = (bf16[2,8192]{1,0:T(2,128)(2,1)S(1)}, bf16[2,8192]{1,0:T(2,128)(2,1)S(1)}, u32[]{:S(2)}, u32[]{:S(2)}) collective-permute-start(bf16[2,8192]{1,0:T(2,128)(2,1)S(1)} %get-tuple-element.62), channel_id=1, source_target_pairs={{0,4},{1,5},{2,6},{3,7},{4,0},{5,1},{6,2},{7,3},{8,12},{9,13},{10,... | collective-permute-start | bytes 98312 | tf_op jit(solution)/shard_map/ppermute | solution.py:25
  29.1 1.5 %collective-permute-done.11.refs_1_ = bf16[2,8192]{1,0:T(2,128)(2,1)S(1)} collective-permute-done((bf16[2,8192]{1,0:T(2,128)(2,1)S(1)}, bf16[2,8192]{1,0:T(2,128)(2,1)S(1)}, u32[]{:S(2)}, u32[]{:S(2)}) %collective-permute-start.11) | collective-permute-done | bytes 32800 | tf_op jit(solution)/shard_map/ppermute | solution.py:25
  30.6 1.4 %collective-permute-done.12.refs_2_ = bf16[2,8192]{1,0:T(2,128)(2,1)S(1)} collective-permute-done((bf16[2,8192]{1,0:T(2,128)(2,1)S(1)}, bf16[2,8192]{1,0:T(2,128)(2,1)S(1)}, u32[]{:S(2)}, u32[]{:S(2)}) %collective-permute-start.12) | collective-permute-done | bytes 32800 | tf_op jit(solution)/shard_map/ppermute | solution.py:25
  32.0 0.7 %sum.1 = bf16[2,8192]{1,0:T(2,128)(2,1)} custom-call(bf16[2,8192]{1,0:T(2,128)(2,1)S(1)} %get-tuple-element.59.refs_0_, bf16[2,8192]{1,0:T(2,128)(2,1)S(1)} %collective-permute-done.11.refs_1_, bf16[2,8192]{1,0:T(2,128)(2,1)S(1)} %collective-permute-done.12.refs_2_, bf16[2,8192]{1,0:T(2,128)(2,1)S(1)} %collective-permute-done.13.refs_3_), custom_call_target="tpu_custom_call" | custom-call | tf_op jit(solution)/shard_map/sum/pallas_call | solution.py:224
  (14 shorter events, 0.0 us)
Async XLA Ops:
  0.0 10.5 %copy-start.1 = (s32[32,1]{0,1:T(1,128)S(1)}, s32[32,1]{0,1:T(1,128)}, u32[]{:S(2)}) copy-start(s32[32,1]{0,1:T(1,128)} %param.11) | copy-start | bytes 388
  0.0 10.5 %copy-start.2 = (s32[16]{0:T(128)S(1)}, s32[16]{0:T(128)}, u32[]{:S(2)}) copy-start(s32[16]{0:T(128)} %param.12) | copy-start | bytes 196
  0.0 10.5 %copy-start.3 = (s32[16]{0:T(128)S(1)}, s32[16]{0:T(128)}, u32[]{:S(2)}) copy-start(s32[16]{0:T(128)} %param.13) | copy-start | bytes 196
  0.0 15.5 %collective-permute-start.5 = (bf16[128,8192]{1,0:T(8,128)(2,1)}, bf16[128,8192]{1,0:T(8,128)(2,1)S(1)}, u32[]{:S(2)}, u32[]{:S(2)}) collective-permute-start(bf16[128,8192]{1,0:T(8,128)(2,1)} %down_ref), channel_id=1, source_target_pairs={{0,1},{1,0},{2,3},{3,2},{4,5},{5,4},{6,7},{7,6},{8,9},{9,8},{10,11... | collective-permute-start | bytes 6291464 | tf_op jit(solution)/shard_map/ppermute | solution.py:25
  0.5 16.2 %collective-permute-start.6 = (bf16[128,8192]{1,0:T(8,128)(2,1)}, bf16[128,8192]{1,0:T(8,128)(2,1)S(1)}, u32[]{:S(2)}, u32[]{:S(2)}) collective-permute-start(bf16[128,8192]{1,0:T(8,128)(2,1)} %refs_2_.1), channel_id=1, source_target_pairs={{0,1},{1,0},{2,3},{3,2},{4,5},{5,4},{6,7},{7,6},{8,9},{9,8},{10,11... | collective-permute-start | bytes 6291464 | tf_op jit(solution)/shard_map/ppermute | solution.py:25
  0.6 5.2 %collective-permute-start = (bf16[2,8192]{1,0:T(2,128)(2,1)}, bf16[2,8192]{1,0:T(2,128)(2,1)S(1)}, u32[]{:S(2)}, u32[]{:S(2)}) collective-permute-start(bf16[2,8192]{1,0:T(2,128)(2,1)} %refs_0_.1), channel_id=1, source_target_pairs={{0,2},{1,3},{2,0},{3,1},{4,6},{5,7},{6,4},{7,5},{8,10},{9,11},{10,... | collective-permute-start | bytes 98312 | tf_op jit(solution)/shard_map/ppermute | solution.py:25
  5.9 7.8 %collective-permute-start.1 = (bf16[4,8192]{1,0:T(4,128)(2,1)S(1)}, bf16[4,8192]{1,0:T(4,128)(2,1)S(1)}, u32[]{:S(2)}, u32[]{:S(2)}) collective-permute-start(bf16[4,8192]{1,0:T(4,128)(2,1)S(1)} %pad_maximum_fusion.1), channel_id=1, source_target_pairs={{0,12},{1,13},{2,14},{3,15},{4,8},{5,9},{6,10},{7,11},{8,4},{9,5},... | collective-permute-start | bytes 196616 | tf_op jit(solution)/shard_map/ppermute | solution.py:25
  9.9 5.3 %collective-permute-start.2 = (bf16[4,8192]{1,0:T(4,128)(2,1)S(1)}, bf16[4,8192]{1,0:T(4,128)(2,1)S(1)}, u32[]{:S(2)}, u32[]{:S(2)}) collective-permute-start(bf16[4,8192]{1,0:T(4,128)(2,1)S(1)} %pad_maximum_fusion.1), channel_id=1, source_target_pairs={{0,8},{1,9},{2,10},{3,11},{4,12},{5,13},{6,14},{7,15},{8,0},{9,1},... | collective-permute-start | bytes 196616 | tf_op jit(solution)/shard_map/ppermute | solution.py:25
  9.9 5.4 %collective-permute-start.3 = (bf16[4,8192]{1,0:T(4,128)(2,1)S(1)}, bf16[4,8192]{1,0:T(4,128)(2,1)S(1)}, u32[]{:S(2)}, u32[]{:S(2)}) collective-permute-start(bf16[4,8192]{1,0:T(4,128)(2,1)S(1)} %pad_maximum_fusion.1), channel_id=1, source_target_pairs={{0,4},{1,5},{2,6},{3,7},{4,0},{5,1},{6,2},{7,3},{8,12},{9,13},{10,... | collective-permute-start | bytes 196616 | tf_op jit(solution)/shard_map/ppermute | solution.py:25
  10.7 4.8 %copy-start = (bf16[128,8192]{1,0:T(8,128)(2,1)S(1)}, bf16[128,8192]{1,0:T(8,128)(2,1)}, u32[]{:S(2)}) copy-start(bf16[128,8192]{1,0:T(8,128)(2,1)} %down_ref) | copy-start | bytes 6291460
  15.4 3.5 %collective-permute-start.4 = (bf16[16,8192]{1,0:T(8,128)(2,1)S(1)}, bf16[16,8192]{1,0:T(8,128)(2,1)S(1)}, u32[]{:S(2)}, u32[]{:S(2)}) collective-permute-start(bf16[16,8192]{1,0:T(8,128)(2,1)S(1)} %pad_maximum_fusion.near_ref), channel_id=1, source_target_pairs={{0,1},{1,0},{2,3},{3,2},{4,5},{5,4},{6,7},{7,6},{8,9},{9,8},{10,11... | collective-permute-start | bytes 786440 | tf_op jit(solution)/shard_map/ppermute | solution.py:25
  17.4 7.2 %collective-permute-start.7 = (bf16[8,8192]{1,0:T(8,128)(2,1)S(1)}, bf16[8,8192]{1,0:T(8,128)(2,1)S(1)}, u32[]{:S(2)}, u32[]{:S(2)}) collective-permute-start(bf16[8,8192]{1,0:T(8,128)(2,1)S(1)} %get-tuple-element.51), channel_id=1, source_target_pairs={{0,2},{1,3},{2,0},{3,1},{4,6},{5,7},{6,4},{7,5},{8,10},{9,11},{10,... | collective-permute-start | bytes 393224 | tf_op jit(solution)/shard_map/ppermute | solution.py:25
  20.5 1.9 %collective-permute-start.10 = (f32[8,512]{1,0:T(8,128)S(1)}, f32[8,512]{1,0:T(8,128)S(1)}, u32[]{:S(2)}, u32[]{:S(2)}) collective-permute-start(f32[8,512]{1,0:T(8,128)S(1)} %get-tuple-element.58), channel_id=1, source_target_pairs={{0,1},{1,0},{2,3},{3,2},{4,5},{5,4},{6,7},{7,6},{8,9},{9,8},{10,11... | collective-permute-start | bytes 49160 | tf_op jit(solution)/shard_map/ppermute | solution.py:25
  20.7 3.8 %collective-permute-start.8 = (f32[8,512]{1,0:T(8,128)S(1)}, f32[8,512]{1,0:T(8,128)S(1)}, u32[]{:S(2)}, u32[]{:S(2)}) collective-permute-start(f32[8,512]{1,0:T(8,128)S(1)} %get-tuple-element.56), channel_id=1, source_target_pairs={{0,2},{1,3},{2,0},{3,1},{4,6},{5,7},{6,4},{7,5},{8,10},{9,11},{10,... | collective-permute-start | bytes 49160 | tf_op jit(solution)/shard_map/ppermute | solution.py:25
  21.2 3.3 %collective-permute-start.9 = (f32[8,512]{1,0:T(8,128)S(1)}, f32[8,512]{1,0:T(8,128)S(1)}, u32[]{:S(2)}, u32[]{:S(2)}) collective-permute-start(f32[8,512]{1,0:T(8,128)S(1)} %get-tuple-element.57), channel_id=1, source_target_pairs={{0,3},{1,2},{2,1},{3,0},{4,7},{5,6},{6,5},{7,4},{8,11},{9,10},{10,... | collective-permute-start | bytes 49160 | tf_op jit(solution)/shard_map/ppermute | solution.py:25
  24.7 5.9 %collective-permute-start.11 = (bf16[2,8192]{1,0:T(2,128)(2,1)S(1)}, bf16[2,8192]{1,0:T(2,128)(2,1)S(1)}, u32[]{:S(2)}, u32[]{:S(2)}) collective-permute-start(bf16[2,8192]{1,0:T(2,128)(2,1)S(1)} %get-tuple-element.60), channel_id=1, source_target_pairs={{0,12},{1,13},{2,14},{3,15},{4,8},{5,9},{6,10},{7,11},{8,4},{9,5},... | collective-permute-start | bytes 98312 | tf_op jit(solution)/shard_map/ppermute | solution.py:25
  27.2 4.8 %collective-permute-start.12 = (bf16[2,8192]{1,0:T(2,128)(2,1)S(1)}, bf16[2,8192]{1,0:T(2,128)(2,1)S(1)}, u32[]{:S(2)}, u32[]{:S(2)}) collective-permute-start(bf16[2,8192]{1,0:T(2,128)(2,1)S(1)} %get-tuple-element.61), channel_id=1, source_target_pairs={{0,8},{1,9},{2,10},{3,11},{4,12},{5,13},{6,14},{7,15},{8,0},{9,1},... | collective-permute-start | bytes 98312 | tf_op jit(solution)/shard_map/ppermute | solution.py:25
  27.2 4.8 %collective-permute-start.13 = (bf16[2,8192]{1,0:T(2,128)(2,1)S(1)}, bf16[2,8192]{1,0:T(2,128)(2,1)S(1)}, u32[]{:S(2)}, u32[]{:S(2)}) collective-permute-start(bf16[2,8192]{1,0:T(2,128)(2,1)S(1)} %get-tuple-element.62), channel_id=1, source_target_pairs={{0,4},{1,5},{2,6},{3,7},{4,0},{5,1},{6,2},{7,3},{8,12},{9,13},{10,... | collective-permute-start | bytes 98312 | tf_op jit(solution)/shard_map/ppermute | solution.py:25

commit v8 on v7

--- a/solution.py
+++ b/solution.py
@@ -13,21 +13,29 @@
 
 def stages_of(devices):
     bits = [1 << k for k in range(1, devices.bit_length() - 1)]
-    stages = [[b] for b in bits[:1]]
-    rest = bits[1:]
+    stages = [[b] for b in bits[-1:]]
+    rest = bits[:-1]
     for k in range(0, len(rest), 2):
         low = rest[k]
         stages.append([low, rest[k + 1], low + rest[k + 1]] if k + 1 < len(rest) else [low])
     return stages
 
 
+def order_of(devices):
+    held = [0]
+    for stage in stages_of(devices):
+        held += [mask ^ h for mask in stage for h in held]
+    return held
+
+
 def exchange(array, mask, devices):
     return lax.ppermute(array, "pool", [(d, d ^ mask) for d in range(devices)])
 
 
 def by_y(rows, array):
-    blocks = [array[r : r + rows] for r in range(0, array.shape[0], rows)]
-    return jnp.concatenate(blocks[::2] + blocks[1::2], axis=0)
+    held = order_of(2 * array.shape[0] // rows)
+    places = sorted(range(len(held)), key=lambda k: (held[k] & 2, held[k]))
+    return jnp.concatenate([array[k * rows : (k + 1) * rows] for k in places], axis=0)
 
 
 def mask_kernel(rows, extent, ident_ref, count_ref, slot_ref, out_ref):
@@ -171,7 +179,7 @@
         name="mask",
     )(request_adapter.reshape(1, -1), adapter_block_count[None], adapter_store_slot[None])
     weight, down, up = base_projection_weight, adapter_down_weight, adapter_up_weight
-    cut = model // 4
+    cut = model * 5 // 8
     near, head, up = load((tokens, 0, rows), (weight, 0, cut), (up, 0, extent))
     for k, stage in enumerate(stages_of(devices)):
         got = [exchange(near if k else tokens, m, devices) for m in stage]
@@ -180,8 +188,8 @@
         if k == 1:
             weight, down, up, near = lax.optimization_barrier((weight, down, up, near))
             (tail,) = load((weight, cut, model))
-            near, tail, mask, *got = lax.optimization_barrier((near, tail, mask, *got[::-1]))
-            got = got[::-1]
+            near, tail, mask, *got = lax.optimization_barrier((near, tail, mask, *[got[i] for i in (2, 0, 1)]))
+            got = [got[i] for i in [1, 2, 0]]
         near = jnp.concatenate([near] + got, axis=0)
     far = exchange(near, 1, devices)
 

time: 32.8 us -> 32.3 us (0.985)
  waiting for transfers between devices: 6.63 us -> 6.09 us
    ppermute x14, waiting for transfers between devices: 6.63 us -> 6.09 us  [exchange(): return lax.ppermute(array, 'pool', [(d, d ^ mask) for d in range(devices)])]
  transfers between devices with their start and end apart: 14 -> 14, of which waited for: 5 -> 6; matrix products, arithmetic and copies ran while one was open for 1% -> 1% of each run, Pallas kernels for 27% -> 27%
where the time goes in v8:
time: 32.3 us; the launch traced here: 32.1 us
  starting transfers between devices  16.2 us (50%)
  Pallas kernels  9.54 us (30%)
  waiting for transfers between devices  6.09 us (19%)
    ppermute x14, starting transfers between devices, exchange(): return lax.ppermute(array, 'pool', [(d, d ^ mask) for d in range(devices)])  16.2 us
    ppermute x14, waiting for transfers between devices, exchange(): return lax.ppermute(array, 'pool', [(d, d ^ mask) for d in range(devices)])  6.09 us
    pallas_call x2, Pallas kernels, load(): pl.pallas_call(functools.partial(load_kernel, [start for _, start, _ in p...  5.25 us
    pallas_call x1, Pallas kernels, body(): pl.pallas_call(functools.partial(base_kernel, rows), out_shape=[jax.Shape...  1.54 us
    pallas_call x1, Pallas kernels, body(): pl.pallas_call(functools.partial(shrink_kernel, rows), out_shape=jax.Shap...  1.19 us
    pallas_call x1, Pallas kernels, body(): pl.pallas_call(sum_kernel, out_shape=jax.ShapeDtypeStruct((rows, model),...  0.66 us
    pallas_call x1, Pallas kernels, body(): pl.pallas_call(delta_kernel, out_shape=[jax.ShapeDtypeStruct((half // 2,...  0.65 us
  transfers between devices with their start and end apart: 14, of which 6 were waited for; matrix products, arithmetic and copies ran while one was open for 1% of the time, Pallas kernels for 27%

profile of v8, /device:TPU:0, one launch (start us, length us, event | category | flops | bytes accessed | tf_op | source)
XLA Modules:
  0.0 32.1 jit_solution(10846638829310898024)
XLA Ops:
  0.0 0.5 %collective-permute-start.5 = (bf16[128,8192]{1,0:T(8,128)(2,1)}, bf16[128,8192]{1,0:T(8,128)(2,1)S(1)}, u32[]{:S(2)}, u32[]{:S(2)}) collective-permute-start(bf16[128,8192]{1,0:T(8,128)(2,1)} %down_ref), channel_id=1, source_target_pairs={{0,1},{1,0},{2,3},{3,2},{4,5},{5,4},{6,7},{7,6},{8,9},{9,8},{10,11... | collective-permute-start | bytes 6291464 | tf_op jit(solution)/shard_map/ppermute | solution.py:32
  0.5 0.1 collective-permute-start.6
  0.6 4.0 %collective-permute-start = (bf16[2,8192]{1,0:T(2,128)(2,1)}, bf16[2,8192]{1,0:T(2,128)(2,1)S(1)}, u32[]{:S(2)}, u32[]{:S(2)}) collective-permute-start(bf16[2,8192]{1,0:T(2,128)(2,1)} %refs_0_.1), channel_id=1, source_target_pairs={{0,8},{1,9},{2,10},{3,11},{4,12},{5,13},{6,14},{7,15},{8,0},{9,1},... | collective-permute-start | bytes 98312 | tf_op jit(solution)/shard_map/ppermute | solution.py:32
  4.6 3.2 %load.2 = (bf16[2,8192]{1,0:T(2,128)(2,1)S(1)}, bf16[5120,512]{1,0:T(8,128)(2,1)S(1)}, bf16[128,8192]{1,0:T(8,128)(2,1)S(1)}) custom-call(bf16[2,8192]{1,0:T(2,128)(2,1)} %refs_0_.1, bf16[8192,512]{1,0:T(8,128)(2,1)} %refs_0_.2, bf16[128,8192]{1,0:T(8,128)(2,1)} %refs_2_.1), custom_call_target="tpu_custom_call" | custom-call | bytes 14745600 | tf_op jit(solution)/shard_map/load/pallas_call | solution.py:113
  7.8 0.0 collective-permute-done
  7.8 0.1 pad_maximum_fusion.1
  7.9 2.6 %collective-permute-start.1 = (bf16[4,8192]{1,0:T(4,128)(2,1)S(1)}, bf16[4,8192]{1,0:T(4,128)(2,1)S(1)}, u32[]{:S(2)}, u32[]{:S(2)}) collective-permute-start(bf16[4,8192]{1,0:T(4,128)(2,1)S(1)} %pad_maximum_fusion.1), channel_id=1, source_target_pairs={{0,6},{1,7},{2,4},{3,5},{4,2},{5,3},{6,0},{7,1},{8,14},{9,15},{10,... | collective-permute-start | bytes 196616 | tf_op jit(solution)/shard_map/ppermute | solution.py:32
  10.5 0.5 %collective-permute-start.2 = (bf16[4,8192]{1,0:T(4,128)(2,1)S(1)}, bf16[4,8192]{1,0:T(4,128)(2,1)S(1)}, u32[]{:S(2)}, u32[]{:S(2)}) collective-permute-start(bf16[4,8192]{1,0:T(4,128)(2,1)S(1)} %pad_maximum_fusion.1), channel_id=1, source_target_pairs={{0,2},{1,3},{2,0},{3,1},{4,6},{5,7},{6,4},{7,5},{8,10},{9,11},{10,... | collective-permute-start | bytes 196616 | tf_op jit(solution)/shard_map/ppermute | solution.py:32
  11.0 0.4 %collective-permute-start.3 = (bf16[4,8192]{1,0:T(4,128)(2,1)S(1)}, bf16[4,8192]{1,0:T(4,128)(2,1)S(1)}, u32[]{:S(2)}, u32[]{:S(2)}) collective-permute-start(bf16[4,8192]{1,0:T(4,128)(2,1)S(1)} %pad_maximum_fusion.1), channel_id=1, source_target_pairs={{0,4},{1,5},{2,6},{3,7},{4,0},{5,1},{6,2},{7,3},{8,12},{9,13},{10,... | collective-permute-start | bytes 196616 | tf_op jit(solution)/shard_map/ppermute | solution.py:32
  11.5 0.2 mask.1.mask_ref
  11.7 2.1 %load.3.weight2_ref = bf16[3072,512]{1,0:T(8,128)(2,1)S(1)} custom-call(bf16[8192,512]{1,0:T(8,128)(2,1)} %refs_0_.2), custom_call_target="tpu_custom_call" | custom-call | bytes 6291456 | tf_op jit(solution)/shard_map/load/pallas_call | solution.py:113
  13.7 1.1 %collective-permute-done.2 = bf16[4,8192]{1,0:T(4,128)(2,1)S(1)} collective-permute-done((bf16[4,8192]{1,0:T(4,128)(2,1)S(1)}, bf16[4,8192]{1,0:T(4,128)(2,1)S(1)}, u32[]{:S(2)}, u32[]{:S(2)}) %collective-permute-start.2) | collective-permute-done | bytes 65568 | tf_op jit(solution)/shard_map/ppermute | solution.py:32
  14.8 0.5 %collective-permute-done.3 = bf16[4,8192]{1,0:T(4,128)(2,1)S(1)} collective-permute-done((bf16[4,8192]{1,0:T(4,128)(2,1)S(1)}, bf16[4,8192]{1,0:T(4,128)(2,1)S(1)}, u32[]{:S(2)}, u32[]{:S(2)}) %collective-permute-start.3) | collective-permute-done | bytes 65568 | tf_op jit(solution)/shard_map/ppermute | solution.py:32
  15.3 0.2 pad_maximum_fusion.near_ref
  15.5 0.1 collective-permute-start.4
  15.6 1.2 %shrink.1.shrink_ref = bf16[16,256]{1,0:T(8,128)(2,1)S(1)} custom-call(f32[16,256]{1,0:T(8,128)S(1)} %mask.1.mask_ref, bf16[16,8192]{1,0:T(8,128)(2,1)S(1)} %pad_maximum_fusion.near_ref, bf16[128,8192]{1,0:T(8,128)(2,1)S(1)} %copy-done, bf16[128,8192]{1,0:T(8,128)(2,1)S(1)} %collective-permute-done.5.down2_ref), custom_call_target="tpu_custom_call" | custom-call | tf_op jit(solution)/shard_map/shrink/pallas_call | solution.py:196
  16.7 0.0 collective-permute-done.6.up2_ref
  16.8 0.6 %delta.1 = (bf16[8,8192]{1,0:T(8,128)(2,1)S(1)}, bf16[8,8192]{1,0:T(8,128)(2,1)S(1)}) custom-call(bf16[16,256]{1,0:T(8,128)(2,1)S(1)} %shrink.1.shrink_ref, bf16[128,8192]{1,0:T(8,128)(2,1)S(1)} %get-tuple-element.48.up_ref, bf16[128,8192]{1,0:T(8,128)(2,1)S(1)} %collective-permute-done.6.up2_ref), custom_call_target="tpu_custom_call" | custom-call | tf_op jit(solution)/shard_map/delta/pallas_call | solution.py:204
  17.4 1.5 %collective-permute-start.7 = (bf16[8,8192]{1,0:T(8,128)(2,1)S(1)}, bf16[8,8192]{1,0:T(8,128)(2,1)S(1)}, u32[]{:S(2)}, u32[]{:S(2)}) collective-permute-start(bf16[8,8192]{1,0:T(8,128)(2,1)S(1)} %get-tuple-element.51), channel_id=1, source_target_pairs={{0,2},{1,3},{2,0},{3,1},{4,6},{5,7},{6,4},{7,5},{8,10},{9,11},{10,... | collective-permute-start | bytes 393224 | tf_op jit(solution)/shard_map/ppermute | solution.py:32
  19.0 1.5 %base.1 = (f32[8,512]{1,0:T(8,128)S(1)}, f32[8,512]{1,0:T(8,128)S(1)}, f32[8,512]{1,0:T(8,128)S(1)}, f32[8,512]{1,0:T(8,128)S(1)}) custom-call(bf16[16,8192]{1,0:T(8,128)(2,1)S(1)} %pad_maximum_fusion.near_ref, bf16[16,8192]{1,0:T(8,128)(2,1)S(1)} %collective-permute-done.4.far_ref, bf16[5120,512]{1,0:T(8,128)(2,1)S(1)} %get-tuple-element.53.weight_ref, ...), custom_call_target="tpu_custom_call" | custom-call | tf_op jit(solution)/shard_map/base/pallas_call | solution.py:214
  20.5 0.3 collective-permute-start.10
  20.8 0.5 %collective-permute-start.8 = (f32[8,512]{1,0:T(8,128)S(1)}, f32[8,512]{1,0:T(8,128)S(1)}, u32[]{:S(2)}, u32[]{:S(2)}) collective-permute-start(f32[8,512]{1,0:T(8,128)S(1)} %get-tuple-element.56), channel_id=1, source_target_pairs={{0,2},{1,3},{2,0},{3,1},{4,6},{5,7},{6,4},{7,5},{8,10},{9,11},{10,... | collective-permute-start | bytes 49160 | tf_op jit(solution)/shard_map/ppermute | solution.py:32
  21.3 1.2 %collective-permute-start.9 = (f32[8,512]{1,0:T(8,128)S(1)}, f32[8,512]{1,0:T(8,128)S(1)}, u32[]{:S(2)}, u32[]{:S(2)}) collective-permute-start(f32[8,512]{1,0:T(8,128)S(1)} %get-tuple-element.57), channel_id=1, source_target_pairs={{0,3},{1,2},{2,1},{3,0},{4,7},{5,6},{6,5},{7,4},{8,11},{9,10},{10,... | collective-permute-start | bytes 49160 | tf_op jit(solution)/shard_map/ppermute | solution.py:32
  22.4 2.2 %collective-permute-done.8.refs_1_ = f32[8,512]{1,0:T(8,128)S(1)} collective-permute-done((f32[8,512]{1,0:T(8,128)S(1)}, f32[8,512]{1,0:T(8,128)S(1)}, u32[]{:S(2)}, u32[]{:S(2)}) %collective-permute-start.8) | collective-permute-done | bytes 16416 | tf_op jit(solution)/shard_map/ppermute | solution.py:32
  24.6 0.1 add.1
  24.7 1.8 %collective-permute-start.11 = (bf16[2,8192]{1,0:T(2,128)(2,1)S(1)}, bf16[2,8192]{1,0:T(2,128)(2,1)S(1)}, u32[]{:S(2)}, u32[]{:S(2)}) collective-permute-start(bf16[2,8192]{1,0:T(2,128)(2,1)S(1)} %get-tuple-element.60), channel_id=1, source_target_pairs={{0,12},{1,13},{2,14},{3,15},{4,8},{5,9},{6,10},{7,11},{8,4},{9,5},... | collective-permute-start | bytes 98312 | tf_op jit(solution)/shard_map/ppermute | solution.py:32
  26.5 0.4 %collective-permute-start.12 = (bf16[2,8192]{1,0:T(2,128)(2,1)S(1)}, bf16[2,8192]{1,0:T(2,128)(2,1)S(1)}, u32[]{:S(2)}, u32[]{:S(2)}) collective-permute-start(bf16[2,8192]{1,0:T(2,128)(2,1)S(1)} %get-tuple-element.61), channel_id=1, source_target_pairs={{0,8},{1,9},{2,10},{3,11},{4,12},{5,13},{6,14},{7,15},{8,0},{9,1},... | collective-permute-start | bytes 98312 | tf_op jit(solution)/shard_map/ppermute | solution.py:32
  26.9 2.3 %collective-permute-start.13 = (bf16[2,8192]{1,0:T(2,128)(2,1)S(1)}, bf16[2,8192]{1,0:T(2,128)(2,1)S(1)}, u32[]{:S(2)}, u32[]{:S(2)}) collective-permute-start(bf16[2,8192]{1,0:T(2,128)(2,1)S(1)} %get-tuple-element.62), channel_id=1, source_target_pairs={{0,4},{1,5},{2,6},{3,7},{4,0},{5,1},{6,2},{7,3},{8,12},{9,13},{10,... | collective-permute-start | bytes 98312 | tf_op jit(solution)/shard_map/ppermute | solution.py:32
  29.2 1.7 %collective-permute-done.11.refs_1_ = bf16[2,8192]{1,0:T(2,128)(2,1)S(1)} collective-permute-done((bf16[2,8192]{1,0:T(2,128)(2,1)S(1)}, bf16[2,8192]{1,0:T(2,128)(2,1)S(1)}, u32[]{:S(2)}, u32[]{:S(2)}) %collective-permute-start.11) | collective-permute-done | bytes 32800 | tf_op jit(solution)/shard_map/ppermute | solution.py:32
  30.8 0.5 %collective-permute-done.12.refs_2_ = bf16[2,8192]{1,0:T(2,128)(2,1)S(1)} collective-permute-done((bf16[2,8192]{1,0:T(2,128)(2,1)S(1)}, bf16[2,8192]{1,0:T(2,128)(2,1)S(1)}, u32[]{:S(2)}, u32[]{:S(2)}) %collective-permute-start.12) | collective-permute-done | bytes 32800 | tf_op jit(solution)/shard_map/ppermute | solution.py:32
  31.3 0.1 collective-permute-done.13.refs_3_
  31.5 0.7 %sum.1 = bf16[2,8192]{1,0:T(2,128)(2,1)} custom-call(bf16[2,8192]{1,0:T(2,128)(2,1)S(1)} %get-tuple-element.59.refs_0_, bf16[2,8192]{1,0:T(2,128)(2,1)S(1)} %collective-permute-done.11.refs_1_, bf16[2,8192]{1,0:T(2,128)(2,1)S(1)} %collective-permute-done.12.refs_2_, bf16[2,8192]{1,0:T(2,128)(2,1)S(1)} %collective-permute-done.13.refs_3_), custom_call_target="tpu_custom_call" | custom-call | tf_op jit(solution)/shard_map/sum/pallas_call | solution.py:232
  (14 shorter events, 0.0 us)
Async XLA Ops:
  0.0 11.5 %copy-start.1 = (s32[32,1]{0,1:T(1,128)S(1)}, s32[32,1]{0,1:T(1,128)}, u32[]{:S(2)}) copy-start(s32[32,1]{0,1:T(1,128)} %param.11) | copy-start | bytes 388
  0.0 11.5 %copy-start.2 = (s32[16]{0:T(128)S(1)}, s32[16]{0:T(128)}, u32[]{:S(2)}) copy-start(s32[16]{0:T(128)} %param.12) | copy-start | bytes 196
  0.0 11.5 %copy-start.3 = (s32[16]{0:T(128)S(1)}, s32[16]{0:T(128)}, u32[]{:S(2)}) copy-start(s32[16]{0:T(128)} %param.13) | copy-start | bytes 196
  0.0 15.5 %collective-permute-start.5 = (bf16[128,8192]{1,0:T(8,128)(2,1)}, bf16[128,8192]{1,0:T(8,128)(2,1)S(1)}, u32[]{:S(2)}, u32[]{:S(2)}) collective-permute-start(bf16[128,8192]{1,0:T(8,128)(2,1)} %down_ref), channel_id=1, source_target_pairs={{0,1},{1,0},{2,3},{3,2},{4,5},{5,4},{6,7},{7,6},{8,9},{9,8},{10,11... | collective-permute-start | bytes 6291464 | tf_op jit(solution)/shard_map/ppermute | solution.py:32
  0.5 16.2 %collective-permute-start.6 = (bf16[128,8192]{1,0:T(8,128)(2,1)}, bf16[128,8192]{1,0:T(8,128)(2,1)S(1)}, u32[]{:S(2)}, u32[]{:S(2)}) collective-permute-start(bf16[128,8192]{1,0:T(8,128)(2,1)} %refs_2_.1), channel_id=1, source_target_pairs={{0,1},{1,0},{2,3},{3,2},{4,5},{5,4},{6,7},{7,6},{8,9},{9,8},{10,11... | collective-permute-start | bytes 6291464 | tf_op jit(solution)/shard_map/ppermute | solution.py:32
  0.6 7.2 %collective-permute-start = (bf16[2,8192]{1,0:T(2,128)(2,1)}, bf16[2,8192]{1,0:T(2,128)(2,1)S(1)}, u32[]{:S(2)}, u32[]{:S(2)}) collective-permute-start(bf16[2,8192]{1,0:T(2,128)(2,1)} %refs_0_.1), channel_id=1, source_target_pairs={{0,8},{1,9},{2,10},{3,11},{4,12},{5,13},{6,14},{7,15},{8,0},{9,1},... | collective-permute-start | bytes 98312 | tf_op jit(solution)/shard_map/ppermute | solution.py:32
  7.9 5.8 %collective-permute-start.1 = (bf16[4,8192]{1,0:T(4,128)(2,1)S(1)}, bf16[4,8192]{1,0:T(4,128)(2,1)S(1)}, u32[]{:S(2)}, u32[]{:S(2)}) collective-permute-start(bf16[4,8192]{1,0:T(4,128)(2,1)S(1)} %pad_maximum_fusion.1), channel_id=1, source_target_pairs={{0,6},{1,7},{2,4},{3,5},{4,2},{5,3},{6,0},{7,1},{8,14},{9,15},{10,... | collective-permute-start | bytes 196616 | tf_op jit(solution)/shard_map/ppermute | solution.py:32
  10.5 4.3 %collective-permute-start.2 = (bf16[4,8192]{1,0:T(4,128)(2,1)S(1)}, bf16[4,8192]{1,0:T(4,128)(2,1)S(1)}, u32[]{:S(2)}, u32[]{:S(2)}) collective-permute-start(bf16[4,8192]{1,0:T(4,128)(2,1)S(1)} %pad_maximum_fusion.1), channel_id=1, source_target_pairs={{0,2},{1,3},{2,0},{3,1},{4,6},{5,7},{6,4},{7,5},{8,10},{9,11},{10,... | collective-permute-start | bytes 196616 | tf_op jit(solution)/shard_map/ppermute | solution.py:32
  11.0 4.3 %collective-permute-start.3 = (bf16[4,8192]{1,0:T(4,128)(2,1)S(1)}, bf16[4,8192]{1,0:T(4,128)(2,1)S(1)}, u32[]{:S(2)}, u32[]{:S(2)}) collective-permute-start(bf16[4,8192]{1,0:T(4,128)(2,1)S(1)} %pad_maximum_fusion.1), channel_id=1, source_target_pairs={{0,4},{1,5},{2,6},{3,7},{4,0},{5,1},{6,2},{7,3},{8,12},{9,13},{10,... | collective-permute-start | bytes 196616 | tf_op jit(solution)/shard_map/ppermute | solution.py:32
  11.7 3.9 %copy-start = (bf16[128,8192]{1,0:T(8,128)(2,1)S(1)}, bf16[128,8192]{1,0:T(8,128)(2,1)}, u32[]{:S(2)}) copy-start(bf16[128,8192]{1,0:T(8,128)(2,1)} %down_ref) | copy-start | bytes 6291460
  15.5 3.5 %collective-permute-start.4 = (bf16[16,8192]{1,0:T(8,128)(2,1)S(1)}, bf16[16,8192]{1,0:T(8,128)(2,1)S(1)}, u32[]{:S(2)}, u32[]{:S(2)}) collective-permute-start(bf16[16,8192]{1,0:T(8,128)(2,1)S(1)} %pad_maximum_fusion.near_ref), channel_id=1, source_target_pairs={{0,1},{1,0},{2,3},{3,2},{4,5},{5,4},{6,7},{7,6},{8,9},{9,8},{10,11... | collective-permute-start | bytes 786440 | tf_op jit(solution)/shard_map/ppermute | solution.py:32
  17.4 7.2 %collective-permute-start.7 = (bf16[8,8192]{1,0:T(8,128)(2,1)S(1)}, bf16[8,8192]{1,0:T(8,128)(2,1)S(1)}, u32[]{:S(2)}, u32[]{:S(2)}) collective-permute-start(bf16[8,8192]{1,0:T(8,128)(2,1)S(1)} %get-tuple-element.51), channel_id=1, source_target_pairs={{0,2},{1,3},{2,0},{3,1},{4,6},{5,7},{6,4},{7,5},{8,10},{9,11},{10,... | collective-permute-start | bytes 393224 | tf_op jit(solution)/shard_map/ppermute | solution.py:32
  20.5 1.9 %collective-permute-start.10 = (f32[8,512]{1,0:T(8,128)S(1)}, f32[8,512]{1,0:T(8,128)S(1)}, u32[]{:S(2)}, u32[]{:S(2)}) collective-permute-start(f32[8,512]{1,0:T(8,128)S(1)} %get-tuple-element.58), channel_id=1, source_target_pairs={{0,1},{1,0},{2,3},{3,2},{4,5},{5,4},{6,7},{7,6},{8,9},{9,8},{10,11... | collective-permute-start | bytes 49160 | tf_op jit(solution)/shard_map/ppermute | solution.py:32
  20.8 3.8 %collective-permute-start.8 = (f32[8,512]{1,0:T(8,128)S(1)}, f32[8,512]{1,0:T(8,128)S(1)}, u32[]{:S(2)}, u32[]{:S(2)}) collective-permute-start(f32[8,512]{1,0:T(8,128)S(1)} %get-tuple-element.56), channel_id=1, source_target_pairs={{0,2},{1,3},{2,0},{3,1},{4,6},{5,7},{6,4},{7,5},{8,10},{9,11},{10,... | collective-permute-start | bytes 49160 | tf_op jit(solution)/shard_map/ppermute | solution.py:32
  21.3 3.3 %collective-permute-start.9 = (f32[8,512]{1,0:T(8,128)S(1)}, f32[8,512]{1,0:T(8,128)S(1)}, u32[]{:S(2)}, u32[]{:S(2)}) collective-permute-start(f32[8,512]{1,0:T(8,128)S(1)} %get-tuple-element.57), channel_id=1, source_target_pairs={{0,3},{1,2},{2,1},{3,0},{4,7},{5,6},{6,5},{7,4},{8,11},{9,10},{10,... | collective-permute-start | bytes 49160 | tf_op jit(solution)/shard_map/ppermute | solution.py:32
  24.7 6.1 %collective-permute-start.11 = (bf16[2,8192]{1,0:T(2,128)(2,1)S(1)}, bf16[2,8192]{1,0:T(2,128)(2,1)S(1)}, u32[]{:S(2)}, u32[]{:S(2)}) collective-permute-start(bf16[2,8192]{1,0:T(2,128)(2,1)S(1)} %get-tuple-element.60), channel_id=1, source_target_pairs={{0,12},{1,13},{2,14},{3,15},{4,8},{5,9},{6,10},{7,11},{8,4},{9,5},... | collective-permute-start | bytes 98312 | tf_op jit(solution)/shard_map/ppermute | solution.py:32
  26.5 4.9 %collective-permute-start.12 = (bf16[2,8192]{1,0:T(2,128)(2,1)S(1)}, bf16[2,8192]{1,0:T(2,128)(2,1)S(1)}, u32[]{:S(2)}, u32[]{:S(2)}) collective-permute-start(bf16[2,8192]{1,0:T(2,128)(2,1)S(1)} %get-tuple-element.61), channel_id=1, source_target_pairs={{0,8},{1,9},{2,10},{3,11},{4,12},{5,13},{6,14},{7,15},{8,0},{9,1},... | collective-permute-start | bytes 98312 | tf_op jit(solution)/shard_map/ppermute | solution.py:32
  26.9 4.6 %collective-permute-start.13 = (bf16[2,8192]{1,0:T(2,128)(2,1)S(1)}, bf16[2,8192]{1,0:T(2,128)(2,1)S(1)}, u32[]{:S(2)}, u32[]{:S(2)}) collective-permute-start(bf16[2,8192]{1,0:T(2,128)(2,1)S(1)} %get-tuple-element.62), channel_id=1, source_target_pairs={{0,4},{1,5},{2,6},{3,7},{4,0},{5,1},{6,2},{7,3},{8,12},{9,13},{10,... | collective-permute-start | bytes 98312 | tf_op jit(solution)/shard_map/ppermute | solution.py:32

commit v9 on v8

--- a/solution.py
+++ b/solution.py
@@ -179,7 +179,7 @@
         name="mask",
     )(request_adapter.reshape(1, -1), adapter_block_count[None], adapter_store_slot[None])
     weight, down, up = base_projection_weight, adapter_down_weight, adapter_up_weight
-    cut = model * 5 // 8
+    cut = model * 11 // 16
     near, head, up = load((tokens, 0, rows), (weight, 0, cut), (up, 0, extent))
     for k, stage in enumerate(stages_of(devices)):
         got = [exchange(near if k else tokens, m, devices) for m in stage]

time: 32.3 us -> 32.4 us (level)
  no operation moved by 1% of the time
where the time goes in v9:
time: 32.4 us; the launch traced here: 32.2 us
  starting transfers between devices  16.2 us (50%)
  Pallas kernels  9.52 us (29%)
  waiting for transfers between devices  6.19 us (19%)
    ppermute x14, starting transfers between devices, exchange(): return lax.ppermute(array, 'pool', [(d, d ^ mask) for d in range(devices)])  16.2 us
    ppermute x14, waiting for transfers between devices, exchange(): return lax.ppermute(array, 'pool', [(d, d ^ mask) for d in range(devices)])  6.19 us
    pallas_call x2, Pallas kernels, load(): pl.pallas_call(functools.partial(load_kernel, [start for _, start, _ in p...  5.23 us
    pallas_call x1, Pallas kernels, body(): pl.pallas_call(functools.partial(base_kernel, rows), out_shape=[jax.Shape...  1.54 us
    pallas_call x1, Pallas kernels, body(): pl.pallas_call(functools.partial(shrink_kernel, rows), out_shape=jax.Shap...  1.19 us
    pallas_call x1, Pallas kernels, body(): pl.pallas_call(sum_kernel, out_shape=jax.ShapeDtypeStruct((rows, model),...  0.66 us
    pallas_call x1, Pallas kernels, body(): pl.pallas_call(delta_kernel, out_shape=[jax.ShapeDtypeStruct((half // 2,...  0.65 us
  transfers between devices with their start and end apart: 14, of which 6 were waited for; matrix products, arithmetic and copies ran while one was open for 1% of the time, Pallas kernels for 27%

profile of v9, /device:TPU:0, one launch (start us, length us, event | category | flops | bytes accessed | tf_op | source)
XLA Modules:
  0.0 32.2 jit_solution(6304258422923518014)
XLA Ops:
  0.0 0.5 %collective-permute-start.5 = (bf16[128,8192]{1,0:T(8,128)(2,1)}, bf16[128,8192]{1,0:T(8,128)(2,1)S(1)}, u32[]{:S(2)}, u32[]{:S(2)}) collective-permute-start(bf16[128,8192]{1,0:T(8,128)(2,1)} %down_ref), channel_id=1, source_target_pairs={{0,1},{1,0},{2,3},{3,2},{4,5},{5,4},{6,7},{7,6},{8,9},{9,8},{10,11... | collective-permute-start | bytes 6291464 | tf_op jit(solution)/shard_map/ppermute | solution.py:32
  0.5 0.1 collective-permute-start.6
  0.6 4.0 %collective-permute-start = (bf16[2,8192]{1,0:T(2,128)(2,1)}, bf16[2,8192]{1,0:T(2,128)(2,1)S(1)}, u32[]{:S(2)}, u32[]{:S(2)}) collective-permute-start(bf16[2,8192]{1,0:T(2,128)(2,1)} %refs_0_.1), channel_id=1, source_target_pairs={{0,8},{1,9},{2,10},{3,11},{4,12},{5,13},{6,14},{7,15},{8,0},{9,1},... | collective-permute-start | bytes 98312 | tf_op jit(solution)/shard_map/ppermute | solution.py:32
  4.6 3.3 %load.2 = (bf16[2,8192]{1,0:T(2,128)(2,1)S(1)}, bf16[5632,512]{1,0:T(8,128)(2,1)S(1)}, bf16[128,8192]{1,0:T(8,128)(2,1)S(1)}) custom-call(bf16[2,8192]{1,0:T(2,128)(2,1)} %refs_0_.1, bf16[8192,512]{1,0:T(8,128)(2,1)} %refs_0_.2, bf16[128,8192]{1,0:T(8,128)(2,1)} %refs_2_.1), custom_call_target="tpu_custom_call" | custom-call | bytes 15794176 | tf_op jit(solution)/shard_map/load/pallas_call | solution.py:113
  8.0 0.1 pad_maximum_fusion.1
  8.0 2.6 %collective-permute-start.1 = (bf16[4,8192]{1,0:T(4,128)(2,1)S(1)}, bf16[4,8192]{1,0:T(4,128)(2,1)S(1)}, u32[]{:S(2)}, u32[]{:S(2)}) collective-permute-start(bf16[4,8192]{1,0:T(4,128)(2,1)S(1)} %pad_maximum_fusion.1), channel_id=1, source_target_pairs={{0,6},{1,7},{2,4},{3,5},{4,2},{5,3},{6,0},{7,1},{8,14},{9,15},{10,... | collective-permute-start | bytes 196616 | tf_op jit(solution)/shard_map/ppermute | solution.py:32
  10.6 0.5 %collective-permute-start.2 = (bf16[4,8192]{1,0:T(4,128)(2,1)S(1)}, bf16[4,8192]{1,0:T(4,128)(2,1)S(1)}, u32[]{:S(2)}, u32[]{:S(2)}) collective-permute-start(bf16[4,8192]{1,0:T(4,128)(2,1)S(1)} %pad_maximum_fusion.1), channel_id=1, source_target_pairs={{0,2},{1,3},{2,0},{3,1},{4,6},{5,7},{6,4},{7,5},{8,10},{9,11},{10,... | collective-permute-start | bytes 196616 | tf_op jit(solution)/shard_map/ppermute | solution.py:32
  11.2 0.4 %collective-permute-start.3 = (bf16[4,8192]{1,0:T(4,128)(2,1)S(1)}, bf16[4,8192]{1,0:T(4,128)(2,1)S(1)}, u32[]{:S(2)}, u32[]{:S(2)}) collective-permute-start(bf16[4,8192]{1,0:T(4,128)(2,1)S(1)} %pad_maximum_fusion.1), channel_id=1, source_target_pairs={{0,4},{1,5},{2,6},{3,7},{4,0},{5,1},{6,2},{7,3},{8,12},{9,13},{10,... | collective-permute-start | bytes 196616 | tf_op jit(solution)/shard_map/ppermute | solution.py:32
  11.6 0.2 mask.1.mask_ref
  11.8 1.9 %load.3.weight2_ref = bf16[2560,512]{1,0:T(8,128)(2,1)S(1)} custom-call(bf16[8192,512]{1,0:T(8,128)(2,1)} %refs_0_.2), custom_call_target="tpu_custom_call" | custom-call | bytes 5242880 | tf_op jit(solution)/shard_map/load/pallas_call | solution.py:113
  13.7 1.2 %collective-permute-done.2 = bf16[4,8192]{1,0:T(4,128)(2,1)S(1)} collective-permute-done((bf16[4,8192]{1,0:T(4,128)(2,1)S(1)}, bf16[4,8192]{1,0:T(4,128)(2,1)S(1)}, u32[]{:S(2)}, u32[]{:S(2)}) %collective-permute-start.2) | collective-permute-done | bytes 65568 | tf_op jit(solution)/shard_map/ppermute | solution.py:32
  14.9 0.5 %collective-permute-done.3 = bf16[4,8192]{1,0:T(4,128)(2,1)S(1)} collective-permute-done((bf16[4,8192]{1,0:T(4,128)(2,1)S(1)}, bf16[4,8192]{1,0:T(4,128)(2,1)S(1)}, u32[]{:S(2)}, u32[]{:S(2)}) %collective-permute-start.3) | collective-permute-done | bytes 65568 | tf_op jit(solution)/shard_map/ppermute | solution.py:32
  15.4 0.2 pad_maximum_fusion.near_ref
  15.6 0.1 collective-permute-start.4
  15.7 0.0 collective-permute-done.5.down2_ref
  15.7 1.2 %shrink.1.shrink_ref = bf16[16,256]{1,0:T(8,128)(2,1)S(1)} custom-call(f32[16,256]{1,0:T(8,128)S(1)} %mask.1.mask_ref, bf16[16,8192]{1,0:T(8,128)(2,1)S(1)} %pad_maximum_fusion.near_ref, bf16[128,8192]{1,0:T(8,128)(2,1)S(1)} %copy-done, bf16[128,8192]{1,0:T(8,128)(2,1)S(1)} %collective-permute-done.5.down2_ref), custom_call_target="tpu_custom_call" | custom-call | tf_op jit(solution)/shard_map/shrink/pallas_call | solution.py:196
  16.9 0.0 collective-permute-done.6.up2_ref
  16.9 0.6 %delta.1 = (bf16[8,8192]{1,0:T(8,128)(2,1)S(1)}, bf16[8,8192]{1,0:T(8,128)(2,1)S(1)}) custom-call(bf16[16,256]{1,0:T(8,128)(2,1)S(1)} %shrink.1.shrink_ref, bf16[128,8192]{1,0:T(8,128)(2,1)S(1)} %get-tuple-element.48.up_ref, bf16[128,8192]{1,0:T(8,128)(2,1)S(1)} %collective-permute-done.6.up2_ref), custom_call_target="tpu_custom_call" | custom-call | tf_op jit(solution)/shard_map/delta/pallas_call | solution.py:204
  17.5 1.5 %collective-permute-start.7 = (bf16[8,8192]{1,0:T(8,128)(2,1)S(1)}, bf16[8,8192]{1,0:T(8,128)(2,1)S(1)}, u32[]{:S(2)}, u32[]{:S(2)}) collective-permute-start(bf16[8,8192]{1,0:T(8,128)(2,1)S(1)} %get-tuple-element.51), channel_id=1, source_target_pairs={{0,2},{1,3},{2,0},{3,1},{4,6},{5,7},{6,4},{7,5},{8,10},{9,11},{10,... | collective-permute-start | bytes 393224 | tf_op jit(solution)/shard_map/ppermute | solution.py:32
  19.1 1.5 %base.1 = (f32[8,512]{1,0:T(8,128)S(1)}, f32[8,512]{1,0:T(8,128)S(1)}, f32[8,512]{1,0:T(8,128)S(1)}, f32[8,512]{1,0:T(8,128)S(1)}) custom-call(bf16[16,8192]{1,0:T(8,128)(2,1)S(1)} %pad_maximum_fusion.near_ref, bf16[16,8192]{1,0:T(8,128)(2,1)S(1)} %collective-permute-done.4.far_ref, bf16[5632,512]{1,0:T(8,128)(2,1)S(1)} %get-tuple-element.53.weight_ref, ...), custom_call_target="tpu_custom_call" | custom-call | tf_op jit(solution)/shard_map/base/pallas_call | solution.py:214
  20.6 0.3 collective-permute-start.10
  20.9 0.5 %collective-permute-start.8 = (f32[8,512]{1,0:T(8,128)S(1)}, f32[8,512]{1,0:T(8,128)S(1)}, u32[]{:S(2)}, u32[]{:S(2)}) collective-permute-start(f32[8,512]{1,0:T(8,128)S(1)} %get-tuple-element.56), channel_id=1, source_target_pairs={{0,2},{1,3},{2,0},{3,1},{4,6},{5,7},{6,4},{7,5},{8,10},{9,11},{10,... | collective-permute-start | bytes 49160 | tf_op jit(solution)/shard_map/ppermute | solution.py:32
  21.4 1.2 %collective-permute-start.9 = (f32[8,512]{1,0:T(8,128)S(1)}, f32[8,512]{1,0:T(8,128)S(1)}, u32[]{:S(2)}, u32[]{:S(2)}) collective-permute-start(f32[8,512]{1,0:T(8,128)S(1)} %get-tuple-element.57), channel_id=1, source_target_pairs={{0,3},{1,2},{2,1},{3,0},{4,7},{5,6},{6,5},{7,4},{8,11},{9,10},{10,... | collective-permute-start | bytes 49160 | tf_op jit(solution)/shard_map/ppermute | solution.py:32
  22.6 2.2 %collective-permute-done.8.refs_1_ = f32[8,512]{1,0:T(8,128)S(1)} collective-permute-done((f32[8,512]{1,0:T(8,128)S(1)}, f32[8,512]{1,0:T(8,128)S(1)}, u32[]{:S(2)}, u32[]{:S(2)}) %collective-permute-start.8) | collective-permute-done | bytes 16416 | tf_op jit(solution)/shard_map/ppermute | solution.py:32
  24.7 0.1 add.1
  24.8 1.6 %collective-permute-start.11 = (bf16[2,8192]{1,0:T(2,128)(2,1)S(1)}, bf16[2,8192]{1,0:T(2,128)(2,1)S(1)}, u32[]{:S(2)}, u32[]{:S(2)}) collective-permute-start(bf16[2,8192]{1,0:T(2,128)(2,1)S(1)} %get-tuple-element.60), channel_id=1, source_target_pairs={{0,12},{1,13},{2,14},{3,15},{4,8},{5,9},{6,10},{7,11},{8,4},{9,5},... | collective-permute-start | bytes 98312 | tf_op jit(solution)/shard_map/ppermute | solution.py:32
  26.5 0.4 %collective-permute-start.12 = (bf16[2,8192]{1,0:T(2,128)(2,1)S(1)}, bf16[2,8192]{1,0:T(2,128)(2,1)S(1)}, u32[]{:S(2)}, u32[]{:S(2)}) collective-permute-start(bf16[2,8192]{1,0:T(2,128)(2,1)S(1)} %get-tuple-element.61), channel_id=1, source_target_pairs={{0,8},{1,9},{2,10},{3,11},{4,12},{5,13},{6,14},{7,15},{8,0},{9,1},... | collective-permute-start | bytes 98312 | tf_op jit(solution)/shard_map/ppermute | solution.py:32
  26.9 2.4 %collective-permute-start.13 = (bf16[2,8192]{1,0:T(2,128)(2,1)S(1)}, bf16[2,8192]{1,0:T(2,128)(2,1)S(1)}, u32[]{:S(2)}, u32[]{:S(2)}) collective-permute-start(bf16[2,8192]{1,0:T(2,128)(2,1)S(1)} %get-tuple-element.62), channel_id=1, source_target_pairs={{0,4},{1,5},{2,6},{3,7},{4,0},{5,1},{6,2},{7,3},{8,12},{9,13},{10,... | collective-permute-start | bytes 98312 | tf_op jit(solution)/shard_map/ppermute | solution.py:32
  29.3 1.6 %collective-permute-done.11.refs_1_ = bf16[2,8192]{1,0:T(2,128)(2,1)S(1)} collective-permute-done((bf16[2,8192]{1,0:T(2,128)(2,1)S(1)}, bf16[2,8192]{1,0:T(2,128)(2,1)S(1)}, u32[]{:S(2)}, u32[]{:S(2)}) %collective-permute-start.11) | collective-permute-done | bytes 32800 | tf_op jit(solution)/shard_map/ppermute | solution.py:32
  30.8 0.5 %collective-permute-done.12.refs_2_ = bf16[2,8192]{1,0:T(2,128)(2,1)S(1)} collective-permute-done((bf16[2,8192]{1,0:T(2,128)(2,1)S(1)}, bf16[2,8192]{1,0:T(2,128)(2,1)S(1)}, u32[]{:S(2)}, u32[]{:S(2)}) %collective-permute-start.12) | collective-permute-done | bytes 32800 | tf_op jit(solution)/shard_map/ppermute | solution.py:32
  31.3 0.2 collective-permute-done.13.refs_3_
  31.6 0.7 %sum.1 = bf16[2,8192]{1,0:T(2,128)(2,1)} custom-call(bf16[2,8192]{1,0:T(2,128)(2,1)S(1)} %get-tuple-element.59.refs_0_, bf16[2,8192]{1,0:T(2,128)(2,1)S(1)} %collective-permute-done.11.refs_1_, bf16[2,8192]{1,0:T(2,128)(2,1)S(1)} %collective-permute-done.12.refs_2_, bf16[2,8192]{1,0:T(2,128)(2,1)S(1)} %collective-permute-done.13.refs_3_), custom_call_target="tpu_custom_call" | custom-call | tf_op jit(solution)/shard_map/sum/pallas_call | solution.py:232
  (14 shorter events, 0.0 us)
Async XLA Ops:
  0.0 11.6 %copy-start.1 = (s32[32,1]{0,1:T(1,128)S(1)}, s32[32,1]{0,1:T(1,128)}, u32[]{:S(2)}) copy-start(s32[32,1]{0,1:T(1,128)} %param.11) | copy-start | bytes 388
  0.0 11.6 %copy-start.2 = (s32[16]{0:T(128)S(1)}, s32[16]{0:T(128)}, u32[]{:S(2)}) copy-start(s32[16]{0:T(128)} %param.12) | copy-start | bytes 196
  0.0 11.6 %copy-start.3 = (s32[16]{0:T(128)S(1)}, s32[16]{0:T(128)}, u32[]{:S(2)}) copy-start(s32[16]{0:T(128)} %param.13) | copy-start | bytes 196
  0.0 15.7 %collective-permute-start.5 = (bf16[128,8192]{1,0:T(8,128)(2,1)}, bf16[128,8192]{1,0:T(8,128)(2,1)S(1)}, u32[]{:S(2)}, u32[]{:S(2)}) collective-permute-start(bf16[128,8192]{1,0:T(8,128)(2,1)} %down_ref), channel_id=1, source_target_pairs={{0,1},{1,0},{2,3},{3,2},{4,5},{5,4},{6,7},{7,6},{8,9},{9,8},{10,11... | collective-permute-start | bytes 6291464 | tf_op jit(solution)/shard_map/ppermute | solution.py:32
  0.5 16.4 %collective-permute-start.6 = (bf16[128,8192]{1,0:T(8,128)(2,1)}, bf16[128,8192]{1,0:T(8,128)(2,1)S(1)}, u32[]{:S(2)}, u32[]{:S(2)}) collective-permute-start(bf16[128,8192]{1,0:T(8,128)(2,1)} %refs_2_.1), channel_id=1, source_target_pairs={{0,1},{1,0},{2,3},{3,2},{4,5},{5,4},{6,7},{7,6},{8,9},{9,8},{10,11... | collective-permute-start | bytes 6291464 | tf_op jit(solution)/shard_map/ppermute | solution.py:32
  0.6 7.4 %collective-permute-start = (bf16[2,8192]{1,0:T(2,128)(2,1)}, bf16[2,8192]{1,0:T(2,128)(2,1)S(1)}, u32[]{:S(2)}, u32[]{:S(2)}) collective-permute-start(bf16[2,8192]{1,0:T(2,128)(2,1)} %refs_0_.1), channel_id=1, source_target_pairs={{0,8},{1,9},{2,10},{3,11},{4,12},{5,13},{6,14},{7,15},{8,0},{9,1},... | collective-permute-start | bytes 98312 | tf_op jit(solution)/shard_map/ppermute | solution.py:32
  8.0 5.7 %collective-permute-start.1 = (bf16[4,8192]{1,0:T(4,128)(2,1)S(1)}, bf16[4,8192]{1,0:T(4,128)(2,1)S(1)}, u32[]{:S(2)}, u32[]{:S(2)}) collective-permute-start(bf16[4,8192]{1,0:T(4,128)(2,1)S(1)} %pad_maximum_fusion.1), channel_id=1, source_target_pairs={{0,6},{1,7},{2,4},{3,5},{4,2},{5,3},{6,0},{7,1},{8,14},{9,15},{10,... | collective-permute-start | bytes 196616 | tf_op jit(solution)/shard_map/ppermute | solution.py:32
  10.6 4.3 %collective-permute-start.2 = (bf16[4,8192]{1,0:T(4,128)(2,1)S(1)}, bf16[4,8192]{1,0:T(4,128)(2,1)S(1)}, u32[]{:S(2)}, u32[]{:S(2)}) collective-permute-start(bf16[4,8192]{1,0:T(4,128)(2,1)S(1)} %pad_maximum_fusion.1), channel_id=1, source_target_pairs={{0,2},{1,3},{2,0},{3,1},{4,6},{5,7},{6,4},{7,5},{8,10},{9,11},{10,... | collective-permute-start | bytes 196616 | tf_op jit(solution)/shard_map/ppermute | solution.py:32
  11.2 4.3 %collective-permute-start.3 = (bf16[4,8192]{1,0:T(4,128)(2,1)S(1)}, bf16[4,8192]{1,0:T(4,128)(2,1)S(1)}, u32[]{:S(2)}, u32[]{:S(2)}) collective-permute-start(bf16[4,8192]{1,0:T(4,128)(2,1)S(1)} %pad_maximum_fusion.1), channel_id=1, source_target_pairs={{0,4},{1,5},{2,6},{3,7},{4,0},{5,1},{6,2},{7,3},{8,12},{9,13},{10,... | collective-permute-start | bytes 196616 | tf_op jit(solution)/shard_map/ppermute | solution.py:32
  11.8 3.9 %copy-start = (bf16[128,8192]{1,0:T(8,128)(2,1)S(1)}, bf16[128,8192]{1,0:T(8,128)(2,1)}, u32[]{:S(2)}) copy-start(bf16[128,8192]{1,0:T(8,128)(2,1)} %down_ref) | copy-start | bytes 6291460
  15.6 3.5 %collective-permute-start.4 = (bf16[16,8192]{1,0:T(8,128)(2,1)S(1)}, bf16[16,8192]{1,0:T(8,128)(2,1)S(1)}, u32[]{:S(2)}, u32[]{:S(2)}) collective-permute-start(bf16[16,8192]{1,0:T(8,128)(2,1)S(1)} %pad_maximum_fusion.near_ref), channel_id=1, source_target_pairs={{0,1},{1,0},{2,3},{3,2},{4,5},{5,4},{6,7},{7,6},{8,9},{9,8},{10,11... | collective-permute-start | bytes 786440 | tf_op jit(solution)/shard_map/ppermute | solution.py:32
  17.5 7.2 %collective-permute-start.7 = (bf16[8,8192]{1,0:T(8,128)(2,1)S(1)}, bf16[8,8192]{1,0:T(8,128)(2,1)S(1)}, u32[]{:S(2)}, u32[]{:S(2)}) collective-permute-start(bf16[8,8192]{1,0:T(8,128)(2,1)S(1)} %get-tuple-element.51), channel_id=1, source_target_pairs={{0,2},{1,3},{2,0},{3,1},{4,6},{5,7},{6,4},{7,5},{8,10},{9,11},{10,... | collective-permute-start | bytes 393224 | tf_op jit(solution)/shard_map/ppermute | solution.py:32
  20.6 1.9 %collective-permute-start.10 = (f32[8,512]{1,0:T(8,128)S(1)}, f32[8,512]{1,0:T(8,128)S(1)}, u32[]{:S(2)}, u32[]{:S(2)}) collective-permute-start(f32[8,512]{1,0:T(8,128)S(1)} %get-tuple-element.58), channel_id=1, source_target_pairs={{0,1},{1,0},{2,3},{3,2},{4,5},{5,4},{6,7},{7,6},{8,9},{9,8},{10,11... | collective-permute-start | bytes 49160 | tf_op jit(solution)/shard_map/ppermute | solution.py:32
  20.9 3.8 %collective-permute-start.8 = (f32[8,512]{1,0:T(8,128)S(1)}, f32[8,512]{1,0:T(8,128)S(1)}, u32[]{:S(2)}, u32[]{:S(2)}) collective-permute-start(f32[8,512]{1,0:T(8,128)S(1)} %get-tuple-element.56), channel_id=1, source_target_pairs={{0,2},{1,3},{2,0},{3,1},{4,6},{5,7},{6,4},{7,5},{8,10},{9,11},{10,... | collective-permute-start | bytes 49160 | tf_op jit(solution)/shard_map/ppermute | solution.py:32
  21.4 3.3 %collective-permute-start.9 = (f32[8,512]{1,0:T(8,128)S(1)}, f32[8,512]{1,0:T(8,128)S(1)}, u32[]{:S(2)}, u32[]{:S(2)}) collective-permute-start(f32[8,512]{1,0:T(8,128)S(1)} %get-tuple-element.57), channel_id=1, source_target_pairs={{0,3},{1,2},{2,1},{3,0},{4,7},{5,6},{6,5},{7,4},{8,11},{9,10},{10,... | collective-permute-start | bytes 49160 | tf_op jit(solution)/shard_map/ppermute | solution.py:32
  24.8 6.0 %collective-permute-start.11 = (bf16[2,8192]{1,0:T(2,128)(2,1)S(1)}, bf16[2,8192]{1,0:T(2,128)(2,1)S(1)}, u32[]{:S(2)}, u32[]{:S(2)}) collective-permute-start(bf16[2,8192]{1,0:T(2,128)(2,1)S(1)} %get-tuple-element.60), channel_id=1, source_target_pairs={{0,12},{1,13},{2,14},{3,15},{4,8},{5,9},{6,10},{7,11},{8,4},{9,5},... | collective-permute-start | bytes 98312 | tf_op jit(solution)/shard_map/ppermute | solution.py:32
  26.5 4.9 %collective-permute-start.12 = (bf16[2,8192]{1,0:T(2,128)(2,1)S(1)}, bf16[2,8192]{1,0:T(2,128)(2,1)S(1)}, u32[]{:S(2)}, u32[]{:S(2)}) collective-permute-start(bf16[2,8192]{1,0:T(2,128)(2,1)S(1)} %get-tuple-element.61), channel_id=1, source_target_pairs={{0,8},{1,9},{2,10},{3,11},{4,12},{5,13},{6,14},{7,15},{8,0},{9,1},... | collective-permute-start | bytes 98312 | tf_op jit(solution)/shard_map/ppermute | solution.py:32
  26.9 4.7 %collective-permute-start.13 = (bf16[2,8192]{1,0:T(2,128)(2,1)S(1)}, bf16[2,8192]{1,0:T(2,128)(2,1)S(1)}, u32[]{:S(2)}, u32[]{:S(2)}) collective-permute-start(bf16[2,8192]{1,0:T(2,128)(2,1)S(1)} %get-tuple-element.62), channel_id=1, source_target_pairs={{0,4},{1,5},{2,6},{3,7},{4,0},{5,1},{6,2},{7,3},{8,12},{9,13},{10,... | collective-permute-start | bytes 98312 | tf_op jit(solution)/shard_map/ppermute | solution.py:32
